TPU v7x, 512 devices: a whole 4x4x16 slice. The times are simulated.
512 devices in a mesh: replica: 32 (over z, core), shard: 16 (over y, x).
Axes of the slice: x: 4, y: 4, z: 16, core: 2. Of those that a mesh axis runs over, the one named last changes fastest.
Arguments:
- context_one: bfloat16 [8192, 5120], P('replica', 'shard'), may hold values from -8 to 8
- cotangent_one: bfloat16 [8192, 5120], P('replica', 'shard'), may hold values from -32 to 32
- context_two: bfloat16 [8192, 5120], P('replica', 'shard'), may hold values from -8 to 8
- cotangent_two: bfloat16 [8192, 5120], P('replica', 'shard'), may hold values from -32 to 32
Outputs:
- combined_one: float32 [5120, 5120], P('shard', 'replica')
- combined_two: float32 [5120, 5120], P('shard', 'replica')
All inputs are finite; a program needn't handle non-finite values.
Results may differ from a plain program's by a relative error of at most 0.0047.
Values may be sent and summed in bfloat16 or wider, within the bound.
No kernel may reach another device: no remote copies, remote signals or barrier semaphores. Data moves between devices by JAX's collectives and lax.ppermute only.
A program may use at most 64 MiB of HBM per device.

v0:
```python
import jax
import jax.numpy as jnp
from jax import lax
from jax.sharding import PartitionSpec as P

EPSILON = 1e-06


def from_partner(value, axis, stride):
    return lax.ppermute(value, axis, [(i, i ^ 1 << stride) for i in range(lax.axis_size(axis))])


def layer_gradient(context, cotangent):
    tokens = context.shape[0]
    gathered = lax.dot_general(
        context,
        lax.all_gather(cotangent, "shard", axis=1, tiled=True),
        (((0,), (0,)), ((), ())),
        preferred_element_type=jnp.float32,
    )
    return (gathered / float(tokens)).astype(jnp.bfloat16)


def group_total(partial_value, section):
    totals = lax.psum(partial_value, "shard")
    for bit_index in range(section + 1):
        totals = totals + from_partner(totals, "replica", bit_index)
    return totals


def run_sections(carried):
    levels = lax.axis_size("replica").bit_length() - 1
    rep_index = lax.axis_index("replica")
    layer_count = carried.shape[0]
    for section in range(levels):
        my_bit = rep_index >> section & 1
        position = 2 + (levels - 1 - section)
        own_half = lax.dynamic_index_in_dim(carried, my_bit, position, keepdims=False)
        sent_half = lax.dynamic_index_in_dim(carried, 1 - my_bit, position, keepdims=False)
        got_half = from_partner(sent_half, "replica", section)
        own_f = own_half.astype(jnp.float32)
        got_f = got_half.astype(jnp.float32)
        reduce_axes = tuple(range(1, own_f.ndim))
        inner_sum = jnp.sum(own_f * got_f, axis=reduce_axes)
        own_sq = jnp.sum(own_f * own_f, axis=reduce_axes)
        other_sq = jnp.sum(got_f * got_f, axis=reduce_axes)
        lower_sq = jnp.where(my_bit == 0, own_sq, other_sq)
        upper_sq = jnp.where(my_bit == 0, other_sq, own_sq)
        partial_value = jnp.concatenate([inner_sum, lower_sq, upper_sq])
        totals = group_total(partial_value, section)
        inner_total = totals[:layer_count]
        lower_total = totals[layer_count : 2 * layer_count]
        upper_total = totals[2 * layer_count :]
        coeff_lower = 1.0 - inner_total / (2.0 * (lower_total + EPSILON))
        coeff_upper = 1.0 - inner_total / (2.0 * (upper_total + EPSILON))
        own_coeff = jnp.where(my_bit == 0, coeff_lower, coeff_upper)
        other_coeff = jnp.where(my_bit == 0, coeff_upper, coeff_lower)
        bshape = (layer_count,) + (1,) * (own_f.ndim - 1)
        combined = own_coeff.reshape(bshape) * own_f + other_coeff.reshape(bshape) * got_f
        if section == levels - 1:
            carried = combined
        else:
            carried = combined.astype(jnp.bfloat16)
    return carried


def shards(context_one, cotangent_one, context_two, cotangent_two):
    levels = lax.axis_size("replica").bit_length() - 1
    gradients = [
        layer_gradient(context_one, cotangent_one),
        layer_gradient(context_two, cotangent_two),
    ]
    row_count, col_count = gradients[0].shape
    reshaped = [
        grad_block.reshape((1, row_count) + (2,) * levels + (col_count >> levels,))
        for grad_block in gradients
    ]
    first_layer = run_sections(reshaped[0])[0]
    second_layer = run_sections(reshaped[1])[0]
    return (first_layer, second_layer)


def solution(mesh):
    return jax.shard_map(
        shards,
        mesh=mesh,
        in_specs=(
            P("replica", "shard"),
            P("replica", "shard"),
            P("replica", "shard"),
            P("replica", "shard"),
        ),
        out_specs=(P("shard", "replica"), P("shard", "replica")),
        check_vma=False,
    )
```

profile of v0, /device:TPU:1, one launch (start us, length us, event | category | flops | bytes accessed | tf_op | source)
XLA Modules:
  0.0 700.0 jit_solution(9751954637996621559)
XLA Ops:
  8.7 68.9 %all-gather.3.cloned.1.call-done = bf16[256,5120]{0,1:T(8,128)(2,1)} async-done(((bf16[256,320]{0,1:T(8,128)(2,1)}), bf16[256,5120]{0,1:T(8,128)(2,1)}) %all-gather.3.cloned.1.call-update) | async-done | bytes 2621456 | tf_op jit(solution)/shard_map/all_gather | solution.py:17
  80.4 3.6 copy.10
  84.0 3.1 dynamic-slice_bitcast_fusion.1
  87.1 3.0 collective-permute-start
  90.1 51.6 %all-gather.5.cloned.1.call-done = bf16[256,5120]{0,1:T(8,128)(2,1)} async-done(((bf16[256,320]{0,1:T(8,128)(2,1)}), bf16[256,5120]{0,1:T(8,128)(2,1)}) %all-gather.5.cloned.1.call-update) | async-done | bytes 2621456 | tf_op jit(solution)/shard_map/all_gather | solution.py:17
  141.7 2.9 fusion.1
  144.6 3.7 copy.11
  148.2 3.0 dynamic-slice_bitcast_fusion
  151.2 2.9 collective-permute-start.20
  154.2 4.1 fusion.8
  167.0 30.9 %all-reduce.4 = (f32[3]{0:T(128)S(1)}, f32[3]{0:T(128)S(1)}) all-reduce(f32[3]{0:T(128)S(1)} %get-tuple-element.72, f32[3]{0:T(128)S(1)} %get-tuple-element.73), channel_id=1, replica_groups=mesh['replica'=32,'shard'=16] {'shard'}, use_global_device_ids=true, to_apply=%region_3.4 | all-reduce | flops 6 | bytes 48 | tf_op jit(solution)/shard_map/psum | solution.py:25
  197.9 9.2 %collective-permute-start.1 = (f32[3]{0:T(128)S(1)}, f32[3]{0:T(128)S(1)}, u32[]{:S(2)}, u32[]{:S(2)}) collective-permute-start(f32[3]{0:T(128)S(1)} %get-tuple-element.40), channel_id=1, source_target_pairs={{0,16},{16,0},{32,48},{48,32},{64,80},{80,64},{96,112},{112,96},{1... | collective-permute-start | bytes 44 | tf_op jit(solution)/shard_map/ppermute | solution.py:10
  215.3 3.0 fusion.4
  219.4 3.2 collective-permute-start.2
  227.9 16.5 %collective-permute-done.2 = bf16[1,320,2,2,2,160]{1,5,4,3,2,0:T(8,128)(2,1)S(1)} collective-permute-done((bf16[1,320,2,2,2,160]{1,5,4,3,2,0:T(8,128)(2,1)}, bf16[1,320,2,2,2,160]{1,5,4,3,2,0:T(8,128)(2,1)S(1)}, u32[]{:S(2)}, u32[]{:S(2)}) %collective-permute-start.2) | collective-permute-done | bytes 819232 | tf_op jit(solution)/shard_map/ppermute | solution.py:10
  248.3 17.2 %collective-permute-done.22 = bf16[1,320,2,2,2,160]{1,5,4,3,2,0:T(8,128)(2,1)} collective-permute-done((bf16[1,320,2,2,2,160]{1,5,4,3,2,0:T(8,128)(2,1)}, bf16[1,320,2,2,2,160]{1,5,4,3,2,0:T(8,128)(2,1)}, u32[]{:S(2)}, u32[]{:S(2)}) %collective-permute-start.22) | collective-permute-done | bytes 819232 | tf_op jit(solution)/shard_map/ppermute | solution.py:10
  271.8 28.5 %all-reduce.3 = (f32[3]{0:T(128)S(1)}, f32[3]{0:T(128)S(1)}) all-reduce(f32[3]{0:T(128)S(1)} %pad_maximum_fusion.1, f32[3]{0:T(128)S(1)} %pad_maximum_fusion.6), channel_id=1, replica_groups=mesh['replica'=32,'shard'=16] {'shard'}, use_global_device_ids=true, to_apply=%region_7.8 | all-reduce | flops 6 | bytes 48 | tf_op jit(solution)/shard_map/psum | solution.py:25
  300.3 10.3 %collective-permute-start.3 = (f32[3]{0:T(128)S(1)}, f32[3]{0:T(128)S(1)}, u32[]{:S(2)}, u32[]{:S(2)}) collective-permute-start(f32[3]{0:T(128)S(1)} %get-tuple-element.38), channel_id=1, source_target_pairs={{0,16},{16,0},{32,48},{48,32},{64,80},{80,64},{96,112},{112,96},{1... | collective-permute-start | bytes 44 | tf_op jit(solution)/shard_map/ppermute | solution.py:10
  312.6 3.2 collective-permute-start.4
  326.7 4.3 collective-permute-start.5
  335.5 27.3 %collective-permute-done.5 = bf16[1,320,2,2,160]{1,4,3,2,0:T(8,128)(2,1)S(1)} collective-permute-done((bf16[1,320,2,2,160]{1,4,3,2,0:T(8,128)(2,1)}, bf16[1,320,2,2,160]{1,4,3,2,0:T(8,128)(2,1)S(1)}, u32[]{:S(2)}, u32[]{:S(2)}) %collective-permute-start.5) | collective-permute-done | bytes 409632 | tf_op jit(solution)/shard_map/ppermute | solution.py:10
  366.4 7.0 %collective-permute-done.25 = bf16[1,320,2,2,160]{1,4,3,2,0:T(8,128)(2,1)S(1)} collective-permute-done((bf16[1,320,2,2,160]{1,4,3,2,0:T(8,128)(2,1)}, bf16[1,320,2,2,160]{1,4,3,2,0:T(8,128)(2,1)S(1)}, u32[]{:S(2)}, u32[]{:S(2)}) %collective-permute-start.25) | collective-permute-done | bytes 409632 | tf_op jit(solution)/shard_map/ppermute | solution.py:10
  378.5 30.2 %all-reduce.2 = (f32[3]{0:T(128)S(1)}, f32[3]{0:T(128)S(1)}) all-reduce(f32[3]{0:T(128)S(1)} %pad_maximum_fusion.2, f32[3]{0:T(128)S(1)} %pad_maximum_fusion.7), channel_id=1, replica_groups=mesh['replica'=32,'shard'=16] {'shard'}, use_global_device_ids=true, to_apply=%region_11.12 | all-reduce | flops 6 | bytes 48 | tf_op jit(solution)/shard_map/psum | solution.py:25
  408.7 10.7 %collective-permute-start.6 = (f32[3]{0:T(128)S(1)}, f32[3]{0:T(128)S(1)}, u32[]{:S(2)}, u32[]{:S(2)}) collective-permute-start(f32[3]{0:T(128)S(1)} %get-tuple-element.36), channel_id=1, source_target_pairs={{0,16},{16,0},{32,48},{48,32},{64,80},{80,64},{96,112},{112,96},{1... | collective-permute-start | bytes 44 | tf_op jit(solution)/shard_map/ppermute | solution.py:10
  423.7 2.9 collective-permute-start.27
  426.7 3.9 collective-permute-start.8
  439.5 7.4 %collective-permute-start.9 = (bf16[1,320,2,160]{1,3,2,0:T(8,128)(2,1)S(1)}, bf16[1,320,2,160]{1,3,2,0:T(8,128)(2,1)S(1)}, u32[]{:S(2)}, u32[]{:S(2)}) collective-permute-start(bf16[1,320,2,160]{1,3,2,0:T(8,128)(2,1)S(1)} %dynamic-slice_bitcast_fusion.7), channel_id=1, source_target_pairs={{0,128},{16,144},{32,160},{48,176},{64,192},{80,208},{96,224},{112... | collective-permute-start | bytes 614408 | tf_op jit(solution)/shard_map/ppermute | solution.py:10
  450.1 33.9 %collective-permute-done.9 = bf16[1,320,2,160]{1,3,2,0:T(8,128)(2,1)S(1)} collective-permute-done((bf16[1,320,2,160]{1,3,2,0:T(8,128)(2,1)S(1)}, bf16[1,320,2,160]{1,3,2,0:T(8,128)(2,1)S(1)}, u32[]{:S(2)}, u32[]{:S(2)}) %collective-permute-start.9) | collective-permute-done | bytes 204832 | tf_op jit(solution)/shard_map/ppermute | solution.py:10
  494.0 28.5 %all-reduce.1 = (f32[3]{0:T(128)S(1)}, f32[3]{0:T(128)S(1)}) all-reduce(f32[3]{0:T(128)S(1)} %pad_maximum_fusion.3, f32[3]{0:T(128)S(1)} %pad_maximum_fusion.8), channel_id=1, replica_groups=mesh['replica'=32,'shard'=16] {'shard'}, use_global_device_ids=true, to_apply=%region_15.16 | all-reduce | flops 6 | bytes 48 | tf_op jit(solution)/shard_map/psum | solution.py:25
  522.5 10.3 %collective-permute-start.10 = (f32[3]{0:T(128)S(1)}, f32[3]{0:T(128)S(1)}, u32[]{:S(2)}, u32[]{:S(2)}) collective-permute-start(f32[3]{0:T(128)S(1)} %get-tuple-element.34), channel_id=1, source_target_pairs={{0,16},{16,0},{32,48},{48,32},{64,80},{80,64},{96,112},{112,96},{1... | collective-permute-start | bytes 44 | tf_op jit(solution)/shard_map/ppermute | solution.py:10
  536.7 3.4 collective-permute-start.31
  540.1 2.9 collective-permute-start.12
  543.0 3.3 collective-permute-start.32
  546.3 7.0 %collective-permute-start.13 = (f32[3]{0:T(128)S(1)}, f32[3]{0:T(128)S(1)}, u32[]{:S(2)}, u32[]{:S(2)}) collective-permute-start(f32[3]{0:T(128)S(1)} %add.275), channel_id=1, source_target_pairs={{0,128},{16,144},{32,160},{48,176},{64,192},{80,208},{96,224},{112... | collective-permute-start | bytes 44 | tf_op jit(solution)/shard_map/ppermute | solution.py:10
  553.3 2.8 collective-permute-start.33
  564.8 9.3 %collective-permute-start.14 = (bf16[1,320,160]{1,2,0:T(8,128)(2,1)S(1)}, bf16[1,320,160]{1,2,0:T(8,128)(2,1)S(1)}, u32[]{:S(2)}, u32[]{:S(2)}) collective-permute-start(bf16[1,320,160]{1,2,0:T(8,128)(2,1)S(1)} %dynamic-slice_bitcast_fusion.9), channel_id=1, source_target_pairs={{0,256},{16,272},{32,288},{48,304},{64,320},{80,336},{96,352},{112... | collective-permute-start | bytes 307208 | tf_op jit(solution)/shard_map/ppermute | solution.py:10
  574.3 4.7 collective-permute-start.34
  579.0 3.6 collective-permute-done.14
  585.7 11.1 %collective-permute-done.34 = bf16[1,320,160]{1,2,0:T(8,128)(2,1)S(1)} collective-permute-done((bf16[1,320,160]{1,2,0:T(8,128)(2,1)S(1)}, bf16[1,320,160]{1,2,0:T(8,128)(2,1)S(1)}, u32[]{:S(2)}, u32[]{:S(2)}) %collective-permute-start.34) | collective-permute-done | bytes 102432 | tf_op jit(solution)/shard_map/ppermute | solution.py:10
  601.5 30.4 %all-reduce = (f32[3]{0:T(128)S(1)}, f32[3]{0:T(128)S(1)}) all-reduce(f32[3]{0:T(128)S(1)} %pad_maximum_fusion.4, f32[3]{0:T(128)S(1)} %pad_maximum_fusion.9), channel_id=1, replica_groups=mesh['replica'=32,'shard'=16] {'shard'}, use_global_device_ids=true, to_apply=%region_19.20 | all-reduce | flops 6 | bytes 48 | tf_op jit(solution)/shard_map/psum | solution.py:25
  631.8 10.2 %collective-permute-start.15 = (f32[3]{0:T(128)S(1)}, f32[3]{0:T(128)S(1)}, u32[]{:S(2)}, u32[]{:S(2)}) collective-permute-start(f32[3]{0:T(128)S(1)} %get-tuple-element.32), channel_id=1, source_target_pairs={{0,16},{16,0},{32,48},{48,32},{64,80},{80,64},{96,112},{112,96},{1... | collective-permute-start | bytes 44 | tf_op jit(solution)/shard_map/ppermute | solution.py:10
  646.3 3.0 collective-permute-start.36
  649.3 5.4 collective-permute-start.17
  657.1 5.7 collective-permute-start.18
  662.8 3.5 collective-permute-start.38
  666.3 9.1 %collective-permute-start.19 = (f32[3]{0:T(128)S(1)}, f32[3]{0:T(128)S(1)}, u32[]{:S(2)}, u32[]{:S(2)}) collective-permute-start(f32[3]{0:T(128)S(1)} %add.285), channel_id=1, source_target_pairs={{0,256},{16,272},{32,288},{48,304},{64,320},{80,336},{96,352},{112... | collective-permute-start | bytes 44 | tf_op jit(solution)/shard_map/ppermute | solution.py:10
  675.5 6.2 collective-permute-start.39
  684.7 3.7 collective-permute-done.39
  (146 shorter events, 74.5 us)
Async XLA Ops:
  7.2 70.4 %copy-start = (bf16[256,320]{0,1:T(8,128)(2,1)S(1)}, bf16[256,320]{0,1:T(8,128)(2,1)}, u32[]{:S(2)}) copy-start(bf16[256,320]{0,1:T(8,128)(2,1)} %param.4) | copy-start | bytes 491524
  7.2 70.4 %all-gather.3.cloned.1.call-start = ((), (), s32[]{:S(2)}) async-start(), calls=%async_computation | async-start | bytes 2785280 | tf_op jit(solution)/shard_map/all_gather | solution.py:17
  7.9 133.7 %all-gather.5.cloned.1.call-start = ((), (), s32[]{:S(2)}) async-start(), calls=%async_computation.1 | async-start | bytes 2785280 | tf_op jit(solution)/shard_map/all_gather | solution.py:17
  87.1 67.1 %collective-permute-start = (bf16[1,320,2,2,2,2,160]{1,6,5,4,3,2,0:T(8,128)(2,1)}, bf16[1,320,2,2,2,2,160]{1,6,5,4,3,2,0:T(8,128)(2,1)}, u32[]{:S(2)}, u32[]{:S(2)}) collective-permute-start(bf16[1,320,2,2,2,2,160]{1,6,5,4,3,2,0:T(8,128)(2,1)} %dynamic-slice_bitcast_fusion.1), channel_id=1, source_target_pairs={{0,16},{16,0},{32,48},{48,32},{64,80},{80,64},{96,112},{112,96},{1... | collective-permute-start | bytes 4915208 | tf_op jit(solution)/shard_map/ppermute | solution.py:10
  151.2 9.6 %collective-permute-start.20 = (bf16[1,320,2,2,2,2,160]{1,6,5,4,3,2,0:T(8,128)(2,1)}, bf16[1,320,2,2,2,2,160]{1,6,5,4,3,2,0:T(8,128)(2,1)S(1)}, u32[]{:S(2)}, u32[]{:S(2)}) collective-permute-start(bf16[1,320,2,2,2,2,160]{1,6,5,4,3,2,0:T(8,128)(2,1)} %dynamic-slice_bitcast_fusion), channel_id=1, source_target_pairs={{0,16},{16,0},{32,48},{48,32},{64,80},{80,64},{96,112},{112,96},{1... | collective-permute-start | bytes 4915208 | tf_op jit(solution)/shard_map/ppermute | solution.py:10
  160.9 54.4 %copy-start.6 = (bf16[1,320,2,2,2,2,160]{1,6,5,4,3,2,0:T(8,128)(2,1)}, bf16[1,320,2,2,2,2,160]{1,6,5,4,3,2,0:T(8,128)(2,1)S(1)}, u32[]{:S(2)}) copy-start(bf16[1,320,2,2,2,2,160]{1,6,5,4,3,2,0:T(8,128)(2,1)S(1)} %collective-permute-done.20) | copy-start | bytes 4915204
  197.9 11.1 %collective-permute-start.1 = (f32[3]{0:T(128)S(1)}, f32[3]{0:T(128)S(1)}, u32[]{:S(2)}, u32[]{:S(2)}) collective-permute-start(f32[3]{0:T(128)S(1)} %get-tuple-element.40), channel_id=1, source_target_pairs={{0,16},{16,0},{32,48},{48,32},{64,80},{80,64},{96,112},{112,96},{1... | collective-permute-start | bytes 44 | tf_op jit(solution)/shard_map/ppermute | solution.py:10
  207.1 5.2 collective-permute-start.21
  219.4 24.9 %collective-permute-start.2 = (bf16[1,320,2,2,2,160]{1,5,4,3,2,0:T(8,128)(2,1)}, bf16[1,320,2,2,2,160]{1,5,4,3,2,0:T(8,128)(2,1)S(1)}, u32[]{:S(2)}, u32[]{:S(2)}) collective-permute-start(bf16[1,320,2,2,2,160]{1,5,4,3,2,0:T(8,128)(2,1)} %dynamic-slice_bitcast_fusion.3), channel_id=1, source_target_pairs={{0,32},{16,48},{32,0},{48,16},{64,96},{80,112},{96,64},{112,80},{1... | collective-permute-start | bytes 2457608 | tf_op jit(solution)/shard_map/ppermute | solution.py:10
  225.7 39.8 %collective-permute-start.22 = (bf16[1,320,2,2,2,160]{1,5,4,3,2,0:T(8,128)(2,1)}, bf16[1,320,2,2,2,160]{1,5,4,3,2,0:T(8,128)(2,1)}, u32[]{:S(2)}, u32[]{:S(2)}) collective-permute-start(bf16[1,320,2,2,2,160]{1,5,4,3,2,0:T(8,128)(2,1)} %dynamic-slice_bitcast_fusion.2), channel_id=1, source_target_pairs={{0,32},{16,48},{32,0},{48,16},{64,96},{80,112},{96,64},{112,80},{1... | collective-permute-start | bytes 2457608 | tf_op jit(solution)/shard_map/ppermute | solution.py:10
  227.8 37.7 %copy-start.4 = (bf16[1,320,2,2,2,2,160]{1,6,5,4,3,2,0:T(8,128)(2,1)S(1)}, bf16[1,320,2,2,2,2,160]{1,6,5,4,3,2,0:T(8,128)(2,1)}, u32[]{:S(2)}) copy-start(bf16[1,320,2,2,2,2,160]{1,6,5,4,3,2,0:T(8,128)(2,1)} %copy-done.3) | copy-start | bytes 4915204
  244.3 79.9 %copy-start.8 = (bf16[1,320,2,2,2,160]{1,5,4,3,2,0:T(8,128)(2,1)}, bf16[1,320,2,2,2,160]{1,5,4,3,2,0:T(8,128)(2,1)S(1)}, u32[]{:S(2)}) copy-start(bf16[1,320,2,2,2,160]{1,5,4,3,2,0:T(8,128)(2,1)S(1)} %collective-permute-done.2) | copy-start | bytes 2457604
  300.3 30.7 %copy-start.5 = (bf16[1,320,2,2,2,2,160]{1,6,5,4,3,2,0:T(8,128)(2,1)S(1)}, bf16[1,320,2,2,2,2,160]{1,6,5,4,3,2,0:T(8,128)(2,1)}, u32[]{:S(2)}) copy-start(bf16[1,320,2,2,2,2,160]{1,6,5,4,3,2,0:T(8,128)(2,1)} %copy-done.3) | copy-start | bytes 4915204
  300.3 12.3 %collective-permute-start.3 = (f32[3]{0:T(128)S(1)}, f32[3]{0:T(128)S(1)}, u32[]{:S(2)}, u32[]{:S(2)}) collective-permute-start(f32[3]{0:T(128)S(1)} %get-tuple-element.38), channel_id=1, source_target_pairs={{0,16},{16,0},{32,48},{48,32},{64,80},{80,64},{96,112},{112,96},{1... | collective-permute-start | bytes 44 | tf_op jit(solution)/shard_map/ppermute | solution.py:10
  310.7 5.1 collective-permute-start.23
  312.6 5.3 collective-permute-start.4
  315.8 5.3 collective-permute-start.24
  326.7 36.1 %collective-permute-start.5 = (bf16[1,320,2,2,160]{1,4,3,2,0:T(8,128)(2,1)}, bf16[1,320,2,2,160]{1,4,3,2,0:T(8,128)(2,1)S(1)}, u32[]{:S(2)}, u32[]{:S(2)}) collective-permute-start(bf16[1,320,2,2,160]{1,4,3,2,0:T(8,128)(2,1)} %dynamic-slice_bitcast_fusion.5), channel_id=1, source_target_pairs={{0,64},{16,80},{32,96},{48,112},{64,0},{80,16},{96,32},{112,48},{1... | collective-permute-start | bytes 1228808 | tf_op jit(solution)/shard_map/ppermute | solution.py:10
  333.5 39.9 %collective-permute-start.25 = (bf16[1,320,2,2,160]{1,4,3,2,0:T(8,128)(2,1)}, bf16[1,320,2,2,160]{1,4,3,2,0:T(8,128)(2,1)S(1)}, u32[]{:S(2)}, u32[]{:S(2)}) collective-permute-start(bf16[1,320,2,2,160]{1,4,3,2,0:T(8,128)(2,1)} %dynamic-slice_bitcast_fusion.4), channel_id=1, source_target_pairs={{0,64},{16,80},{32,96},{48,112},{64,0},{80,16},{96,32},{112,48},{1... | collective-permute-start | bytes 1228808 | tf_op jit(solution)/shard_map/ppermute | solution.py:10
  373.4 65.9 %copy-start.9 = (bf16[1,320,2,2,160]{1,4,3,2,0:T(8,128)(2,1)}, bf16[1,320,2,2,160]{1,4,3,2,0:T(8,128)(2,1)S(1)}, u32[]{:S(2)}) copy-start(bf16[1,320,2,2,160]{1,4,3,2,0:T(8,128)(2,1)S(1)} %collective-permute-done.25) | copy-start | bytes 1228804
  408.7 12.6 %collective-permute-start.6 = (f32[3]{0:T(128)S(1)}, f32[3]{0:T(128)S(1)}, u32[]{:S(2)}, u32[]{:S(2)}) collective-permute-start(f32[3]{0:T(128)S(1)} %get-tuple-element.36), channel_id=1, source_target_pairs={{0,16},{16,0},{32,48},{48,32},{64,80},{80,64},{96,112},{112,96},{1... | collective-permute-start | bytes 44 | tf_op jit(solution)/shard_map/ppermute | solution.py:10
  419.4 4.3 collective-permute-start.26
  421.4 5.3 collective-permute-start.7
  423.7 6.9 collective-permute-start.27
  426.7 6.2 collective-permute-start.8
  430.6 5.5 collective-permute-start.28
  439.5 44.4 %collective-permute-start.9 = (bf16[1,320,2,160]{1,3,2,0:T(8,128)(2,1)S(1)}, bf16[1,320,2,160]{1,3,2,0:T(8,128)(2,1)S(1)}, u32[]{:S(2)}, u32[]{:S(2)}) collective-permute-start(bf16[1,320,2,160]{1,3,2,0:T(8,128)(2,1)S(1)} %dynamic-slice_bitcast_fusion.7), channel_id=1, source_target_pairs={{0,128},{16,144},{32,160},{48,176},{64,192},{80,208},{96,224},{112... | collective-permute-start | bytes 614408 | tf_op jit(solution)/shard_map/ppermute | solution.py:10
  448.2 41.1 %collective-permute-start.29 = (bf16[1,320,2,160]{1,3,2,0:T(8,128)(2,1)S(1)}, bf16[1,320,2,160]{1,3,2,0:T(8,128)(2,1)S(1)}, u32[]{:S(2)}, u32[]{:S(2)}) collective-permute-start(bf16[1,320,2,160]{1,3,2,0:T(8,128)(2,1)S(1)} %dynamic-slice_bitcast_fusion.6), channel_id=1, source_target_pairs={{0,128},{16,144},{32,160},{48,176},{64,192},{80,208},{96,224},{112... | collective-permute-start | bytes 614408 | tf_op jit(solution)/shard_map/ppermute | solution.py:10
  522.5 12.2 %collective-permute-start.10 = (f32[3]{0:T(128)S(1)}, f32[3]{0:T(128)S(1)}, u32[]{:S(2)}, u32[]{:S(2)}) collective-permute-start(f32[3]{0:T(128)S(1)} %get-tuple-element.34), channel_id=1, source_target_pairs={{0,16},{16,0},{32,48},{48,32},{64,80},{80,64},{96,112},{112,96},{1... | collective-permute-start | bytes 44 | tf_op jit(solution)/shard_map/ppermute | solution.py:10
  532.8 3.9 collective-permute-start.30
  534.7 5.3 collective-permute-start.11
  536.7 6.3 collective-permute-start.31
  540.1 6.2 collective-permute-start.12
  543.0 10.4 %collective-permute-start.32 = (f32[3]{0:T(128)S(1)}, f32[3]{0:T(128)S(1)}, u32[]{:S(2)}, u32[]{:S(2)}) collective-permute-start(f32[3]{0:T(128)S(1)} %add.306), channel_id=1, source_target_pairs={{0,64},{16,80},{32,96},{48,112},{64,0},{80,16},{96,32},{112,48},{1... | collective-permute-start | bytes 44 | tf_op jit(solution)/shard_map/ppermute | solution.py:10
  546.3 9.9 %collective-permute-start.13 = (f32[3]{0:T(128)S(1)}, f32[3]{0:T(128)S(1)}, u32[]{:S(2)}, u32[]{:S(2)}) collective-permute-start(f32[3]{0:T(128)S(1)} %add.275), channel_id=1, source_target_pairs={{0,128},{16,144},{32,160},{48,176},{64,192},{80,208},{96,224},{112... | collective-permute-start | bytes 44 | tf_op jit(solution)/shard_map/ppermute | solution.py:10
  553.3 8.2 %collective-permute-start.33 = (f32[3]{0:T(128)S(1)}, f32[3]{0:T(128)S(1)}, u32[]{:S(2)}, u32[]{:S(2)}) collective-permute-start(f32[3]{0:T(128)S(1)} %add.307), channel_id=1, source_target_pairs={{0,128},{16,144},{32,160},{48,176},{64,192},{80,208},{96,224},{112... | collective-permute-start | bytes 44 | tf_op jit(solution)/shard_map/ppermute | solution.py:10
  564.8 17.8 %collective-permute-start.14 = (bf16[1,320,160]{1,2,0:T(8,128)(2,1)S(1)}, bf16[1,320,160]{1,2,0:T(8,128)(2,1)S(1)}, u32[]{:S(2)}, u32[]{:S(2)}) collective-permute-start(bf16[1,320,160]{1,2,0:T(8,128)(2,1)S(1)} %dynamic-slice_bitcast_fusion.9), channel_id=1, source_target_pairs={{0,256},{16,272},{32,288},{48,304},{64,320},{80,336},{96,352},{112... | collective-permute-start | bytes 307208 | tf_op jit(solution)/shard_map/ppermute | solution.py:10
  574.3 22.6 %collective-permute-start.34 = (bf16[1,320,160]{1,2,0:T(8,128)(2,1)S(1)}, bf16[1,320,160]{1,2,0:T(8,128)(2,1)S(1)}, u32[]{:S(2)}, u32[]{:S(2)}) collective-permute-start(bf16[1,320,160]{1,2,0:T(8,128)(2,1)S(1)} %dynamic-slice_bitcast_fusion.8), channel_id=1, source_target_pairs={{0,256},{16,272},{32,288},{48,304},{64,320},{80,336},{96,352},{112... | collective-permute-start | bytes 307208 | tf_op jit(solution)/shard_map/ppermute | solution.py:10
  631.8 12.2 %collective-permute-start.15 = (f32[3]{0:T(128)S(1)}, f32[3]{0:T(128)S(1)}, u32[]{:S(2)}, u32[]{:S(2)}) collective-permute-start(f32[3]{0:T(128)S(1)} %get-tuple-element.32), channel_id=1, source_target_pairs={{0,16},{16,0},{32,48},{48,32},{64,80},{80,64},{96,112},{112,96},{1... | collective-permute-start | bytes 44 | tf_op jit(solution)/shard_map/ppermute | solution.py:10
  642.1 4.3 collective-permute-start.35
  644.0 5.3 collective-permute-start.16
  646.3 8.4 %collective-permute-start.36 = (f32[3]{0:T(128)S(1)}, f32[3]{0:T(128)S(1)}, u32[]{:S(2)}, u32[]{:S(2)}) collective-permute-start(f32[3]{0:T(128)S(1)} %add.312), channel_id=1, source_target_pairs={{0,32},{16,48},{32,0},{48,16},{64,96},{80,112},{96,64},{112,80},{1... | collective-permute-start | bytes 44 | tf_op jit(solution)/shard_map/ppermute | solution.py:10
  649.3 7.7 %collective-permute-start.17 = (f32[3]{0:T(128)S(1)}, f32[3]{0:T(128)S(1)}, u32[]{:S(2)}, u32[]{:S(2)}) collective-permute-start(f32[3]{0:T(128)S(1)} %add.283), channel_id=1, source_target_pairs={{0,64},{16,80},{32,96},{48,112},{64,0},{80,16},{96,32},{112,48},{1... | collective-permute-start | bytes 44 | tf_op jit(solution)/shard_map/ppermute | solution.py:10
  654.7 8.0 %collective-permute-start.37 = (f32[3]{0:T(128)S(1)}, f32[3]{0:T(128)S(1)}, u32[]{:S(2)}, u32[]{:S(2)}) collective-permute-start(f32[3]{0:T(128)S(1)} %add.313), channel_id=1, source_target_pairs={{0,64},{16,80},{32,96},{48,112},{64,0},{80,16},{96,32},{112,48},{1... | collective-permute-start | bytes 44 | tf_op jit(solution)/shard_map/ppermute | solution.py:10
  657.1 9.2 %collective-permute-start.18 = (f32[3]{0:T(128)S(1)}, f32[3]{0:T(128)S(1)}, u32[]{:S(2)}, u32[]{:S(2)}) collective-permute-start(f32[3]{0:T(128)S(1)} %add.284), channel_id=1, source_target_pairs={{0,128},{16,144},{32,160},{48,176},{64,192},{80,208},{96,224},{112... | collective-permute-start | bytes 44 | tf_op jit(solution)/shard_map/ppermute | solution.py:10
  662.8 12.7 %collective-permute-start.38 = (f32[3]{0:T(128)S(1)}, f32[3]{0:T(128)S(1)}, u32[]{:S(2)}, u32[]{:S(2)}) collective-permute-start(f32[3]{0:T(128)S(1)} %add.314), channel_id=1, source_target_pairs={{0,128},{16,144},{32,160},{48,176},{64,192},{80,208},{96,224},{112... | collective-permute-start | bytes 44 | tf_op jit(solution)/shard_map/ppermute | solution.py:10
  666.3 15.4 %collective-permute-start.19 = (f32[3]{0:T(128)S(1)}, f32[3]{0:T(128)S(1)}, u32[]{:S(2)}, u32[]{:S(2)}) collective-permute-start(f32[3]{0:T(128)S(1)} %add.285), channel_id=1, source_target_pairs={{0,256},{16,272},{32,288},{48,304},{64,320},{80,336},{96,352},{112... | collective-permute-start | bytes 44 | tf_op jit(solution)/shard_map/ppermute | solution.py:10
  675.5 13.0 %collective-permute-start.39 = (f32[3]{0:T(128)S(1)}, f32[3]{0:T(128)S(1)}, u32[]{:S(2)}, u32[]{:S(2)}) collective-permute-start(f32[3]{0:T(128)S(1)} %add.315), channel_id=1, source_target_pairs={{0,256},{16,272},{32,288},{48,304},{64,320},{80,336},{96,352},{112... | collective-permute-start | bytes 44 | tf_op jit(solution)/shard_map/ppermute | solution.py:10
  (4 other events, 22.5 us)
Sparse Core Ops, SparseCore 0:
  11.0 66.5 all-gather.2
  80.6 61.0 all-gather.4
where the time goes:
time: 703 us; the launch traced here: 700 us
  waiting for transfers between devices  247 us (35%)
  starting transfers between devices  177 us (25%)
  blocking collectives  148 us (21%)
  between operations  65 us (9%)
  other arithmetic  32.6 us (5%)
  local copies, waits for them, and re-layouts  25 us (4%)
    ppermute x40, starting transfers between devices, from_partner(): lax.ppermute(value, axis, [(i, i ^ 1 << stride) for i in range(lax.axis_s...  177 us
    psum x5, blocking collectives, group_total(): totals = lax.psum(partial_value, 'shard')  148 us
    ppermute x40, waiting for transfers between devices, from_partner(): lax.ppermute(value, axis, [(i, i ^ 1 << stride) for i in range(lax.axis_s...  125 us
    all_gather x2, waiting for transfers between devices, layer_gradient(): lax.all_gather(cotangent, 'shard', axis=1, tiled=True)  120 us
    reduce_sum x10, other arithmetic, run_sections(): inner_sum = jnp.sum(own_f * got_f, axis=reduce_axes)  15.4 us
  transfers between devices with their start and end apart: 42, of which 12 were waited for; matrix products, arithmetic and copies ran while one was open for 5% of the time, Pallas kernels for 0%

commit v1 on v0

v1 whole, which is shorter than its diff:
```python
import functools

import jax
import jax.numpy as jnp
import numpy as np
from jax import lax
from jax.experimental import pallas as pl
from jax.experimental.pallas import tpu as pltpu
from jax.sharding import PartitionSpec as P

EPSILON = 1e-06
SIDE = 4
MAIN = 128
SHIFTS = (0, 1, -1, 2)


def x_moves(d):
    return [
        (y * SIDE + x, y * SIDE + (x + d) % SIDE) for y in range(SIDE) for x in range(SIDE)
    ]


def y_moves(d):
    return [
        (y * SIDE + x, ((y + d) % SIDE) * SIDE + x) for y in range(SIDE) for x in range(SIDE)
    ]


def gather_pieces(piece):
    half = piece.shape[0] // 2
    along_x, along_y = piece[:half], piece[half:]
    got_x = [lax.ppermute(along_x, "shard", x_moves(d)) for d in SHIFTS[1:]]
    got_y = [lax.ppermute(along_y, "shard", y_moves(d)) for d in SHIFTS[1:]]
    line_x = jnp.stack([along_x] + got_x)
    line_y = jnp.stack([along_y] + got_y)
    line_x, line_y = lax.optimization_barrier((line_x, line_y))
    all_x = [line_x] + [lax.ppermute(line_x, "shard", y_moves(d)) for d in SHIFTS[1:]]
    all_y = [line_y] + [lax.ppermute(line_y, "shard", x_moves(d)) for d in SHIFTS[1:]]
    return all_x, all_y


def piece_offsets(tokens_piece):
    me = lax.axis_index("shard")
    y, x = me // SIDE, me % SIDE
    d = jnp.array(SHIFTS, jnp.int32)
    first, second = d[None, :], d[:, None]
    off_x = ((y - second) % SIDE) * SIDE + (x - first) % SIDE
    off_y = ((y - first) % SIDE) * SIDE + (x - second) % SIDE
    return (jnp.stack([off_x, off_y]) * tokens_piece).astype(jnp.int32).reshape(-1)


def gradient_kernel(reps, rows, rem, inv_tokens, off_ref, ctx_ref, *refs):
    pieces = refs[:8]
    grad_ref, gram_ref, cot_ref, store_ref, acc_ref = refs[8:]
    step = pl.program_id(0)
    steps = pl.num_programs(0)
    tok = pieces[0].shape[2]

    def place(which):
        for second in range(4):
            for first in range(4):
                off = pl.multiple_of(off_ref[which * 16 + second * 4 + first], tok)
                cot_ref[pl.ds(off, tok), :] = pieces[which * 4 + second][first, 0]

    @pl.when(step < steps // 2)
    def _():
        place(0)

    @pl.when(step >= steps // 2)
    def _():
        place(1)

    lane = lax.broadcasted_iota(jnp.int32, (rows, MAIN), 1)
    edge = cot_ref[:, 4 * MAIN :]
    for core in range(2):
        both = []
        for layer in range(2):
            j = 2 * core + layer
            rhs = jnp.concatenate([cot_ref[:, j * MAIN : (j + 1) * MAIN], edge], axis=1)
            lhs = ctx_ref[core, layer * rows : (layer + 1) * rows, :]
            g = jnp.dot(lhs, rhs, preferred_element_type=jnp.float32) * inv_tokens
            main = g[:, :MAIN].astype(jnp.bfloat16)
            grad_ref[layer, core] = main
            store_ref[layer, step * 2 + core] = main.astype(jnp.float32)
            both.append(g[:, MAIN:])
        edges = jnp.where(lane < (2 * core + 1) * rem, both[0], both[1])
        if core:
            edges = pltpu.roll(edges, MAIN - 2 * rem, 1)
        edges = jnp.where(lane < 2 * rem, edges, 0.0).astype(jnp.bfloat16)
        grad_ref[2, core] = edges
        store_ref[2, step * 2 + core] = edges.astype(jnp.float32)

    @pl.when(step == steps - 1)
    def _():
        size = reps * 8
        group = 4
        acc_ref[...] = jnp.zeros_like(acc_ref)
        lane_e = lax.broadcasted_iota(jnp.int32, (size, MAIN), 1)

        def body(i, carry):
            lefts, rights = ([], []), ([], [])
            for u in range(group):
                at = pl.multiple_of((i * group + u) * 8, 8)
                e = store_ref[2, :, pl.ds(at, 8), :].reshape(size, MAIN)
                eb = e.astype(jnp.bfloat16)
                for layer in range(2):
                    m = store_ref[layer, :, pl.ds(at, 8), :].reshape(size, MAIN)
                    m = m.astype(jnp.bfloat16)
                    keep = (lane_e >= layer * rem) & (lane_e < (layer + 1) * rem)
                    ek = jnp.where(keep, e, 0.0).astype(jnp.bfloat16)
                    lefts[layer].extend([m, ek])
                    rights[layer].extend([m, eb])
            for layer in range(2):
                acc_ref[layer] += lax.dot_general(
                    jnp.concatenate(lefts[layer], axis=1),
                    jnp.concatenate(rights[layer], axis=1),
                    (((1,), (1,)), ((), ())),
                    preferred_element_type=jnp.float32,
                )
            return carry

        lax.fori_loop(0, rows // (8 * group), body, 0)
        ri = lax.broadcasted_iota(jnp.int32, (size, size), 0)
        ci = lax.broadcasted_iota(jnp.int32, (size, size), 1)
        si = lax.broadcasted_iota(jnp.int32, (size, 128), 0)
        sj = lax.broadcasted_iota(jnp.int32, (size, 128), 1)
        total = jnp.zeros((16, 128), jnp.float32)
        for layer in range(2):
            z = jnp.where(ri % 8 == ci % 8, acc_ref[layer], 0.0)
            z = jnp.sum(z.reshape(reps, 8, size), axis=1)
            for h in range(2):
                pick = jnp.where(sj == (2 * layer + h) * 32 + si // 8, 1.0, 0.0)
                total += jnp.dot(
                    z[h * 16 : (h + 1) * 16],
                    pick.astype(jnp.float32),
                    precision=lax.Precision.HIGHEST,
                    preferred_element_type=jnp.float32,
                )
        gram_ref[...] = jnp.broadcast_to(total[None], gram_ref.shape)


def gradients(ctx, pieces_x, pieces_y, offsets, shards, tokens):
    reps, rows2, _ = ctx.shape
    rows = rows2 // 2
    rem = (pieces_x[0].shape[-1] - 4 * MAIN) // 4
    steps = reps // 2
    half = steps // 2
    _, _, tok, width = pieces_x[0].shape
    block = (4, 1, tok, width)
    in_specs = [pl.BlockSpec((2, rows2, tokens), lambda i, o: (i, 0, 0))]
    in_specs += [
        pl.BlockSpec(block, lambda i, o: (0, jnp.minimum(i, half - 1), 0, 0))
    ] * 4
    in_specs += [
        pl.BlockSpec(block, lambda i, o: (0, jnp.maximum(i - half, 0), 0, 0))
    ] * 4
    return pl.pallas_call(
        functools.partial(gradient_kernel, reps, rows, rem, 1.0 / tokens),
        grid_spec=pltpu.PrefetchScalarGridSpec(
            num_scalar_prefetch=1,
            grid=(steps,),
            in_specs=in_specs,
            out_specs=[
                pl.BlockSpec((3, 2, rows, MAIN), lambda i, o: (0, i, 0, 0)),
                pl.BlockSpec((shards, 16, 128), lambda i, o: (0, 0, 0)),
            ],
            scratch_shapes=[
                pltpu.VMEM((tokens, width), jnp.bfloat16),
                pltpu.VMEM((3, reps, rows, MAIN), jnp.float32),
                pltpu.VMEM((2, reps * 8, reps * 8), jnp.float32),
            ],
        ),
        out_shape=[
            jax.ShapeDtypeStruct((3, reps, rows, MAIN), jnp.bfloat16),
            jax.ShapeDtypeStruct((shards, 16, 128), jnp.float32),
        ],
        compiler_params=pltpu.CompilerParams(vmem_limit_bytes=48 * 1024 * 1024),
    )(offsets, ctx, *pieces_x, *pieces_y)


def tree_weights(gram):
    n = gram.shape[0]
    ri = lax.broadcasted_iota(jnp.int32, (n, n), 0)
    ci = lax.broadcasted_iota(jnp.int32, (n, n), 1)
    weight = jnp.ones((n, 1), jnp.float32)
    for k in range(n.bit_length() - 1):
        same = (ri >> k) == (ci >> k)
        other = (ri >> k) == ((ci >> k) ^ 1)
        twin = ri == (ci ^ (1 << k))
        own = jnp.where(same, gram, 0.0)
        cross = jnp.where(other, gram, 0.0)
        coeffs = []
        for axis in (1, 0):
            norm = jnp.sum(own, axis=1 - axis, keepdims=True)
            norm = jnp.sum(jnp.where(same, norm, 0.0), axis=axis, keepdims=True)
            inner = jnp.sum(cross, axis=1 - axis, keepdims=True)
            inner = jnp.sum(jnp.where(same, inner, 0.0), axis=axis, keepdims=True)
            coeffs.append((jnp.maximum(norm, 0.0), inner))
        (norm_r, inner_r), (norm_c, inner_c) = coeffs
        twin_r = jnp.sum(jnp.where(twin, norm_c, 0.0), axis=1, keepdims=True)
        twin_c = jnp.sum(jnp.where(twin, norm_r, 0.0), axis=0, keepdims=True)
        cap_r = jnp.sqrt(norm_r) * jnp.sqrt(twin_r)
        cap_c = jnp.sqrt(norm_c) * jnp.sqrt(twin_c)
        inner_r = jnp.clip(inner_r, -cap_r, cap_r)
        inner_c = jnp.clip(inner_c, -cap_c, cap_c)
        coeff_r = 1.0 - inner_r / (2.0 * (norm_r + EPSILON))
        coeff_c = 1.0 - inner_c / (2.0 * (norm_c + EPSILON))
        weight = weight * coeff_r
        gram = gram * coeff_r * coeff_c
    return weight


def combine_kernel(rem, gram_ref, grad_ref, one_ref, two_ref, weight_ref):
    reps = grad_ref.shape[1]
    rows = grad_ref.shape[2]

    @pl.when(pl.program_id(0) == 0)
    def _():
        total = jnp.sum(gram_ref[...], axis=0)
        lane = lax.broadcasted_iota(jnp.int32, (reps, MAIN), 1)
        weights = []
        for layer in range(2):
            parts = [total[:, (2 * layer + h) * 32 : (2 * layer + h + 1) * 32] for h in range(2)]
            weights.append(
                jnp.broadcast_to(tree_weights(jnp.concatenate(parts, axis=0)), (reps, MAIN))
            )
        weight_ref[0] = weights[0]
        weight_ref[1] = weights[1]
        weight_ref[2] = jnp.where(lane < rem, weights[0], weights[1])

    sums = []
    for part in range(3):
        acc = jnp.zeros((rows, MAIN), jnp.float32)
        for r in range(reps):
            acc += weight_ref[part, r : r + 1, :] * grad_ref[part, r].astype(jnp.float32)
        sums.append(acc)
    for layer, ref in enumerate((one_ref, two_ref)):
        ref[:, :MAIN] = sums[layer]
        ref[:, MAIN:] = sums[2][:, layer * rem : (layer + 1) * rem]


def combine(gram_parts, grads, rem):
    _, reps, rows, _ = grads.shape
    block = 64
    cols = MAIN + rem
    return pl.pallas_call(
        functools.partial(combine_kernel, rem),
        grid=(rows // block,),
        in_specs=[
            pl.BlockSpec(gram_parts.shape, lambda i: (0, 0, 0)),
            pl.BlockSpec((3, reps, block, MAIN), lambda i: (0, 0, i, 0)),
        ],
        out_specs=[pl.BlockSpec((block, cols), lambda i: (i, 0))] * 2,
        out_shape=[jax.ShapeDtypeStruct((rows, cols), jnp.float32)] * 2,
        scratch_shapes=[pltpu.VMEM((3, reps, MAIN), jnp.float32)],
        compiler_params=pltpu.CompilerParams(vmem_limit_bytes=32 * 1024 * 1024),
    )(gram_parts, grads)


def core_columns(one, two, core, cols):
    a, b = one[:, core * cols : (core + 1) * cols], two[:, core * cols : (core + 1) * cols]
    return jnp.concatenate([a[:, :MAIN], b[:, :MAIN], a[:, MAIN:], b[:, MAIN:]], axis=1)


def shards(context_one, cotangent_one, context_two, cotangent_two):
    tokens, feats = context_one.shape
    reps = lax.axis_size("replica")
    n_shards = lax.axis_size("shard")
    cols = feats // 2
    core = lax.axis_index("replica") % 2
    same_core = [list(range(c, reps, 2)) for c in range(2)]

    ctx = jnp.concatenate([context_one.T, context_two.T], axis=0)
    ctx = lax.all_gather(ctx, "replica")

    low = core_columns(cotangent_one, cotangent_two, 0, cols)
    high = core_columns(cotangent_one, cotangent_two, 1, cols)
    keep = jnp.where(core == 0, low, high)
    give = jnp.where(core == 0, high, low)
    got = lax.ppermute(give, "replica", [(i, i ^ 1) for i in range(reps)])
    first = jnp.where(core == 0, keep, got)
    second = jnp.where(core == 0, got, keep)
    cot = jnp.concatenate(
        [first[:, : 2 * MAIN], second[:, : 2 * MAIN], first[:, 2 * MAIN :], second[:, 2 * MAIN :]],
        axis=1,
    )
    cot = cot.reshape(n_shards, tokens // n_shards, cot.shape[1])
    cot = lax.all_to_all(cot, "shard", 0, 0)
    cot = lax.all_to_all(cot, "replica", 0, 0, axis_index_groups=same_core)
    pieces_x, pieces_y = gather_pieces(cot)

    offsets = piece_offsets(tokens // n_shards)
    grads, gram = gradients(ctx, pieces_x, pieces_y, offsets, n_shards, tokens)
    gram = jnp.sum(lax.all_to_all(gram, "shard", 0, 0), axis=0)
    gram = lax.all_to_all(jnp.broadcast_to(gram[None], (reps,) + gram.shape), "replica", 0, 0)
    one, two = combine(gram, grads, cols - MAIN)
    return one, two


def solution(mesh):
    spec = P("replica", "shard")
    return jax.shard_map(
        shards,
        mesh=mesh,
        in_specs=(spec, spec, spec, spec),
        out_specs=(P("shard", "replica"), P("shard", "replica")),
        check_vma=False,
    )
```

time: 703 us -> 216 us (0.31)
  waiting for transfers between devices: 247 us -> 25.1 us
  starting transfers between devices: 177 us -> 44.9 us
  blocking collectives: 148 us -> 95.4 us
  between operations: 65 us -> 14.3 us
  other arithmetic: 32.6 us -> 2.86 us
  Pallas kernels: 0 us -> 25.1 us
  local copies, waits for them, and re-layouts: 25 us -> 7.02 us
    psum x5 -> x0, blocking collectives: 148 us -> none  [group_total(): totals = lax.psum(partial_value, 'shard')]
    ppermute x40 -> x13, starting transfers between devices: 177 us -> 44.9 us  [the longest x3 10.2 us: gather_pieces(): lax.ppermute(line_x, 'shard', y_moves(d))]
    all_gather x2 -> x1, waiting for transfers between devices: 120 us -> 0.01 us  [shards(): ctx = lax.all_gather(ctx, 'replica')]
    ppermute x40 -> x13, waiting for transfers between devices: 125 us -> 25.1 us  [the longest x3 11 us: gather_pieces(): lax.ppermute(line_y, 'shard', x_moves(d))]
    all_to_all x0 -> x4, blocking collectives: none -> 95.4 us  [the longest x1 35.8 us: shards(): lax.all_to_all(jnp.broadcast_to(gram[None], (reps,) + gram.shape), 'repli...]
    pallas_call x0 -> x2, Pallas kernels: none -> 25.1 us  [the longest x1 21.5 us: gradients(): pl.pallas_call(functools.partial(gradient_kernel, reps, rows, rem, 1.0 /...]
    reduce_sum x10 -> x1, other arithmetic: 15.4 us -> 0.02 us  [shards(): gram = jnp.sum(lax.all_to_all(gram, 'shard', 0, 0), axis=0)]
    squeeze x10 -> x0, local copies, waits for them, and re-layouts: 10.1 us -> none  [run_sections(): lax.dynamic_index_in_dim(carried, 1 - my_bit, position, keepdims=False)]
  transfers between devices with their start and end apart: 42 -> 14, of which waited for: 12 -> 6; matrix products, arithmetic and copies ran while one was open for 5% -> 1% of each run, Pallas kernels for 0% -> 0%
where the time goes in v1:
time: 216 us; the launch traced here: 215 us
  blocking collectives  95.4 us (44%)
  starting transfers between devices  44.9 us (21%)
  waiting for transfers between devices  25.1 us (12%)
  Pallas kernels  25.1 us (12%)
  between operations  14.3 us (7%)
  local copies, waits for them, and re-layouts  7.02 us (3%)
  other arithmetic  2.86 us (1%)
    all_to_all x1, blocking collectives, shards(): lax.all_to_all(jnp.broadcast_to(gram[None], (reps,) + gram.shape), 'repli...  35.8 us
    all_to_all x1, blocking collectives, shards(): cot = lax.all_to_all(cot, 'replica', 0, 0, axis_index_groups=same_core)  34.4 us
    pallas_call x1, Pallas kernels, gradients(): pl.pallas_call(functools.partial(gradient_kernel, reps, rows, rem, 1.0 /...  21.5 us
    all_to_all x1, blocking collectives, shards(): gram = jnp.sum(lax.all_to_all(gram, 'shard', 0, 0), axis=0)  13.7 us
    all_to_all x1, blocking collectives, shards(): cot = lax.all_to_all(cot, 'shard', 0, 0)  11.6 us
    ppermute x3, waiting for transfers between devices, gather_pieces(): lax.ppermute(line_y, 'shard', x_moves(d))  11 us
    ppermute x3, starting transfers between devices, gather_pieces(): lax.ppermute(line_x, 'shard', y_moves(d))  10.2 us
    ppermute x3, starting transfers between devices, gather_pieces(): lax.ppermute(line_y, 'shard', x_moves(d))  9.94 us
  transfers between devices with their start and end apart: 14, of which 6 were waited for; matrix products, arithmetic and copies ran while one was open for 1% of the time, Pallas kernels for 0%

profile of v1, /device:TPU:1, one launch (start us, length us, event | category | flops | bytes accessed | tf_op | source)
XLA Modules:
  0.0 214.7 jit_solution(11704299985958345314)
XLA Ops:
  7.2 0.0 all-gather.3.cloned.1.call-start
  7.2 1.7 pad_maximum_fusion.2
  8.9 0.0 all-gather.3.cloned.1.call-update
  9.0 0.8 fusion.5
  9.8 1.0 fusion.3
  10.8 8.8 %collective-permute-start = (bf16[256,320]{0,1:T(8,128)(2,1)S(1)}, bf16[256,320]{0,1:T(8,128)(2,1)S(1)}, u32[]{:S(2)}, u32[]{:S(2)}) collective-permute-start(bf16[256,320]{0,1:T(8,128)(2,1)S(1)} %broadcast_select_fusion.2), channel_id=1, source_target_pairs={{0,16},{16,0},{32,48},{48,32},{64,80},{80,64},{96,112},{112,96},{1... | collective-permute-start | bytes 491528 | tf_op jit(solution)/shard_map/ppermute | solution.py:280
  19.6 1.0 collective-permute-done
  20.6 0.1 broadcast_select_fusion.1
  20.7 0.2 copy.7
  21.0 11.6 %all_to_all.20 = bf16[16,16,640]{2,1,0:T(8,128)(2,1)S(1)} all-to-all(bf16[16,16,640]{2,1,0:T(8,128)(2,1)S(1)} %bitcast.15), channel_id=1, replica_groups=mesh['replica'=32,'shard'=16] {'shard'}, dimensions={0} | all-to-all | bytes 655360 | tf_op jit(solution)/shard_map/all_to_all | solution.py:288
  32.5 34.4 %all_to_all.21 = bf16[16,16,640]{2,1,0:T(8,128)(2,1)S(1)} all-to-all(bf16[16,16,640]{2,1,0:T(8,128)(2,1)S(1)} %all_to_all.20), channel_id=1, replica_groups={{0,32,64,96,128,160,192,224,256,288,320,352,384,416,448,480},{16,48,80,..., dimensions={0} | all-to-all | bytes 655360 | tf_op jit(solution)/shard_map/all_to_all | solution.py:289
  66.9 0.1 slice_bitcast_fusion
  66.9 1.9 collective-permute-start.5
  68.9 3.4 %collective-permute-start.4 = (bf16[8,16,640]{2,1,0:T(8,128)(2,1)S(1)}, bf16[8,16,640]{2,1,0:T(8,128)(2,1)S(1)}, u32[]{:S(2)}, u32[]{:S(2)}) collective-permute-start(bf16[8,16,640]{2,1,0:T(8,128)(2,1)S(1)} %get-tuple-element.16), channel_id=1, source_target_pairs={{0,4},{1,5},{2,6},{3,7},{4,8},{5,9},{6,10},{7,11},{8,12},{9,13},{1... | collective-permute-start | bytes 491528 | tf_op jit(solution)/shard_map/ppermute | solution.py:33
  72.2 1.9 collective-permute-start.6
  74.2 2.8 %collective-permute-start.2 = (bf16[8,16,640]{2,1,0:T(8,128)(2,1)S(1)}, bf16[8,16,640]{2,1,0:T(8,128)(2,1)S(1)}, u32[]{:S(2)}, u32[]{:S(2)}) collective-permute-start(bf16[8,16,640]{2,1,0:T(8,128)(2,1)S(1)} %get-tuple-element.17), channel_id=1, source_target_pairs={{0,3},{1,0},{2,1},{3,2},{4,7},{5,4},{6,5},{7,6},{8,11},{9,8},{10,9... | collective-permute-start | bytes 491528 | tf_op jit(solution)/shard_map/ppermute | solution.py:32
  76.9 2.5 %collective-permute-start.1 = (bf16[8,16,640]{2,1,0:T(8,128)(2,1)S(1)}, bf16[8,16,640]{2,1,0:T(8,128)(2,1)S(1)}, u32[]{:S(2)}, u32[]{:S(2)}) collective-permute-start(bf16[8,16,640]{2,1,0:T(8,128)(2,1)S(1)} %get-tuple-element.17), channel_id=1, source_target_pairs={{0,1},{1,2},{2,3},{3,0},{4,5},{5,6},{6,7},{7,4},{8,9},{9,10},{10,1... | collective-permute-start | bytes 491528 | tf_op jit(solution)/shard_map/ppermute | solution.py:32
  79.5 0.0 collective-permute-done.5
  79.5 3.5 %collective-permute-start.3 = (bf16[8,16,640]{2,1,0:T(8,128)(2,1)S(1)}, bf16[8,16,640]{2,1,0:T(8,128)(2,1)S(1)}, u32[]{:S(2)}, u32[]{:S(2)}) collective-permute-start(bf16[8,16,640]{2,1,0:T(8,128)(2,1)S(1)} %get-tuple-element.17), channel_id=1, source_target_pairs={{0,2},{1,3},{2,0},{3,1},{4,6},{5,7},{6,4},{7,5},{8,10},{9,11},{10,... | collective-permute-start | bytes 491528 | tf_op jit(solution)/shard_map/ppermute | solution.py:32
  82.9 0.0 collective-permute-done.4
  82.9 0.0 collective-permute-done.6
  83.0 0.1 pad_maximum_fusion.1.refs_4_
  83.1 0.0 collective-permute-done.2
  83.1 1.5 collective-permute-done.1
  84.6 2.4 %collective-permute-done.3 = bf16[8,16,640]{2,1,0:T(8,128)(2,1)S(1)} collective-permute-done((bf16[8,16,640]{2,1,0:T(8,128)(2,1)S(1)}, bf16[8,16,640]{2,1,0:T(8,128)(2,1)S(1)}, u32[]{:S(2)}, u32[]{:S(2)}) %collective-permute-start.3) | collective-permute-done | bytes 163872 | tf_op jit(solution)/shard_map/ppermute | solution.py:32
  87.0 0.1 pad_maximum_fusion.refs_0_
  87.1 4.9 %collective-permute-start.9 = (bf16[4,8,16,640]{3,2,1,0:T(8,128)(2,1)S(1)}, bf16[4,8,16,640]{3,2,1,0:T(8,128)(2,1)S(1)}, u32[]{:S(2)}, u32[]{:S(2)}) collective-permute-start(bf16[4,8,16,640]{3,2,1,0:T(8,128)(2,1)S(1)} %pad_maximum_fusion.refs_0_), channel_id=1, source_target_pairs={{0,8},{1,9},{2,10},{3,11},{4,12},{5,13},{6,14},{7,15},{8,0},{9,1},... | collective-permute-start | bytes 1966088 | tf_op jit(solution)/shard_map/ppermute | solution.py:37
  92.1 3.1 %collective-permute-start.8 = (bf16[4,8,16,640]{3,2,1,0:T(8,128)(2,1)S(1)}, bf16[4,8,16,640]{3,2,1,0:T(8,128)(2,1)S(1)}, u32[]{:S(2)}, u32[]{:S(2)}) collective-permute-start(bf16[4,8,16,640]{3,2,1,0:T(8,128)(2,1)S(1)} %pad_maximum_fusion.refs_0_), channel_id=1, source_target_pairs={{0,12},{1,13},{2,14},{3,15},{4,0},{5,1},{6,2},{7,3},{8,4},{9,5},{1... | collective-permute-start | bytes 1966088 | tf_op jit(solution)/shard_map/ppermute | solution.py:37
  95.2 2.2 %collective-permute-start.7 = (bf16[4,8,16,640]{3,2,1,0:T(8,128)(2,1)S(1)}, bf16[4,8,16,640]{3,2,1,0:T(8,128)(2,1)S(1)}, u32[]{:S(2)}, u32[]{:S(2)}) collective-permute-start(bf16[4,8,16,640]{3,2,1,0:T(8,128)(2,1)S(1)} %pad_maximum_fusion.refs_0_), channel_id=1, source_target_pairs={{0,4},{1,5},{2,6},{3,7},{4,8},{5,9},{6,10},{7,11},{8,12},{9,13},{1... | collective-permute-start | bytes 1966088 | tf_op jit(solution)/shard_map/ppermute | solution.py:37
  97.4 3.0 %collective-permute-start.12 = (bf16[4,8,16,640]{3,2,1,0:T(8,128)(2,1)S(1)}, bf16[4,8,16,640]{3,2,1,0:T(8,128)(2,1)}, u32[]{:S(2)}, u32[]{:S(2)}) collective-permute-start(bf16[4,8,16,640]{3,2,1,0:T(8,128)(2,1)S(1)} %pad_maximum_fusion.1.refs_4_), channel_id=1, source_target_pairs={{0,2},{1,3},{2,0},{3,1},{4,6},{5,7},{6,4},{7,5},{8,10},{9,11},{10,... | collective-permute-start | bytes 1966088 | tf_op jit(solution)/shard_map/ppermute | solution.py:38
  100.4 5.0 %collective-permute-start.11 = (bf16[4,8,16,640]{3,2,1,0:T(8,128)(2,1)S(1)}, bf16[4,8,16,640]{3,2,1,0:T(8,128)(2,1)}, u32[]{:S(2)}, u32[]{:S(2)}) collective-permute-start(bf16[4,8,16,640]{3,2,1,0:T(8,128)(2,1)S(1)} %pad_maximum_fusion.1.refs_4_), channel_id=1, source_target_pairs={{0,3},{1,0},{2,1},{3,2},{4,7},{5,4},{6,5},{7,6},{8,11},{9,8},{10,9... | collective-permute-start | bytes 1966088 | tf_op jit(solution)/shard_map/ppermute | solution.py:38
  105.4 0.0 collective-permute-done.9.refs_3_
  105.4 1.9 collective-permute-start.10
  107.3 0.7 fusion.1
  108.0 0.1 broadcast_add_fusion.1
  108.1 0.1 mul.19.off_ref
  108.2 8.9 %collective-permute-done.8.refs_2_ = bf16[4,8,16,640]{3,2,1,0:T(8,128)(2,1)S(1)} collective-permute-done((bf16[4,8,16,640]{3,2,1,0:T(8,128)(2,1)S(1)}, bf16[4,8,16,640]{3,2,1,0:T(8,128)(2,1)S(1)}, u32[]{:S(2)}, u32[]{:S(2)}) %collective-permute-start.8) | collective-permute-done | bytes 655392 | tf_op jit(solution)/shard_map/ppermute | solution.py:37
  117.1 0.2 collective-permute-done.7.refs_1_
  117.2 0.0 collective-permute-done.12.refs_7_
  117.2 11.0 %collective-permute-done.11.refs_6_ = bf16[4,8,16,640]{3,2,1,0:T(8,128)(2,1)} collective-permute-done((bf16[4,8,16,640]{3,2,1,0:T(8,128)(2,1)S(1)}, bf16[4,8,16,640]{3,2,1,0:T(8,128)(2,1)}, u32[]{:S(2)}, u32[]{:S(2)}) %collective-permute-start.11) | collective-permute-done | bytes 655392 | tf_op jit(solution)/shard_map/ppermute | solution.py:38
  128.3 0.0 collective-permute-done.10.refs_5_
  128.3 21.5 %shard_map.68 = (bf16[3,32,320,128]{3,2,1,0:T(8,128)(2,1)}, f32[16,16,128]{2,1,0:T(8,128)S(1)}) custom-call(s32[32]{0:T(128)S(1)} %mul.19.off_ref, bf16[32,640,256]{2,1,0:T(8,128)(2,1)} %bitcast.14, bf16[4,8,16,640]{3,2,1,0:T(8,128)(2,1)S(1)} %pad_maximum_fusion.refs_0_, bf16[4,8,16,640]{3,2,1,0:T(8,128)(2,1)S(1)} %collective-permute-done.7.refs_1_, ...), custom_call_target="tpu_custom_call" | custom-call | tf_op jit(solution)/shard_map/pallas_call | solution.py:157
  149.8 13.7 %all_to_all.22 = f32[16,16,128]{2,1,0:T(8,128)S(1)} all-to-all(f32[16,16,128]{2,1,0:T(8,128)S(1)} %get-tuple-element.8), channel_id=1, replica_groups=mesh['replica'=32,'shard'=16] {'shard'}, dimensions={0} | all-to-all | bytes 262144 | tf_op jit(solution)/shard_map/all_to_all | solution.py:294
  163.6 35.8 %all_to_all.23.gram_ref = f32[32,16,128]{2,1,0:T(8,128)S(1)} all-to-all(f32[32,16,128]{2,1,0:T(8,128)S(1)} %broadcast_in_dim.2), channel_id=1, replica_groups=mesh['replica'=32,'shard'=16] {'replica'}, dimensions={0} | all-to-all | bytes 524288 | tf_op jit(solution)/shard_map/all_to_all | solution.py:295
  199.3 3.2 %copy-done = bf16[3,32,320,128]{3,2,1,0:T(8,128)(2,1)S(1)} copy-done((bf16[3,32,320,128]{3,2,1,0:T(8,128)(2,1)S(1)}, bf16[3,32,320,128]{3,2,1,0:T(8,128)(2,1)}, u32[]{:S(2)}) %copy-start) | copy-done | bytes 7864344
  202.6 3.6 %shard_map.69 = (f32[320,160]{1,0:T(8,128)S(1)}, f32[320,160]{1,0:T(8,128)S(1)}) custom-call(f32[32,16,128]{2,1,0:T(8,128)S(1)} %all_to_all.23.gram_ref, bf16[3,32,320,128]{3,2,1,0:T(8,128)(2,1)S(1)} %copy-done), custom_call_target="tpu_custom_call" | custom-call | tf_op jit(solution)/shard_map/pallas_call | solution.py:246
  206.2 0.8 copy.8
  207.0 0.8 copy.9
  (11 shorter events, 0.1 us)
Async XLA Ops:
  7.2 121.1 %all-gather.3.cloned.1.call-start = ((), (), s32[]{:S(2)}) async-start(), calls=%async_computation.4 | async-start | bytes 10813440 | tf_op jit(solution)/shard_map/all_gather | solution.py:274
  10.8 9.8 %collective-permute-start = (bf16[256,320]{0,1:T(8,128)(2,1)S(1)}, bf16[256,320]{0,1:T(8,128)(2,1)S(1)}, u32[]{:S(2)}, u32[]{:S(2)}) collective-permute-start(bf16[256,320]{0,1:T(8,128)(2,1)S(1)} %broadcast_select_fusion.2), channel_id=1, source_target_pairs={{0,16},{16,0},{32,48},{48,32},{64,80},{80,64},{96,112},{112,96},{1... | collective-permute-start | bytes 491528 | tf_op jit(solution)/shard_map/ppermute | solution.py:280
  66.9 12.5 %collective-permute-start.5 = (bf16[8,16,640]{2,1,0:T(8,128)(2,1)S(1)}, bf16[8,16,640]{2,1,0:T(8,128)(2,1)S(1)}, u32[]{:S(2)}, u32[]{:S(2)}) collective-permute-start(bf16[8,16,640]{2,1,0:T(8,128)(2,1)S(1)} %get-tuple-element.16), channel_id=1, source_target_pairs={{0,12},{1,13},{2,14},{3,15},{4,0},{5,1},{6,2},{7,3},{8,4},{9,5},{1... | collective-permute-start | bytes 491528 | tf_op jit(solution)/shard_map/ppermute | solution.py:33
  68.9 14.1 %collective-permute-start.4 = (bf16[8,16,640]{2,1,0:T(8,128)(2,1)S(1)}, bf16[8,16,640]{2,1,0:T(8,128)(2,1)S(1)}, u32[]{:S(2)}, u32[]{:S(2)}) collective-permute-start(bf16[8,16,640]{2,1,0:T(8,128)(2,1)S(1)} %get-tuple-element.16), channel_id=1, source_target_pairs={{0,4},{1,5},{2,6},{3,7},{4,8},{5,9},{6,10},{7,11},{8,12},{9,13},{1... | collective-permute-start | bytes 491528 | tf_op jit(solution)/shard_map/ppermute | solution.py:33
  72.2 10.7 %collective-permute-start.6 = (bf16[8,16,640]{2,1,0:T(8,128)(2,1)S(1)}, bf16[8,16,640]{2,1,0:T(8,128)(2,1)S(1)}, u32[]{:S(2)}, u32[]{:S(2)}) collective-permute-start(bf16[8,16,640]{2,1,0:T(8,128)(2,1)S(1)} %get-tuple-element.16), channel_id=1, source_target_pairs={{0,8},{1,9},{2,10},{3,11},{4,12},{5,13},{6,14},{7,15},{8,0},{9,1},... | collective-permute-start | bytes 491528 | tf_op jit(solution)/shard_map/ppermute | solution.py:33
  74.2 8.9 %collective-permute-start.2 = (bf16[8,16,640]{2,1,0:T(8,128)(2,1)S(1)}, bf16[8,16,640]{2,1,0:T(8,128)(2,1)S(1)}, u32[]{:S(2)}, u32[]{:S(2)}) collective-permute-start(bf16[8,16,640]{2,1,0:T(8,128)(2,1)S(1)} %get-tuple-element.17), channel_id=1, source_target_pairs={{0,3},{1,0},{2,1},{3,2},{4,7},{5,4},{6,5},{7,6},{8,11},{9,8},{10,9... | collective-permute-start | bytes 491528 | tf_op jit(solution)/shard_map/ppermute | solution.py:32
  76.9 7.7 %collective-permute-start.1 = (bf16[8,16,640]{2,1,0:T(8,128)(2,1)S(1)}, bf16[8,16,640]{2,1,0:T(8,128)(2,1)S(1)}, u32[]{:S(2)}, u32[]{:S(2)}) collective-permute-start(bf16[8,16,640]{2,1,0:T(8,128)(2,1)S(1)} %get-tuple-element.17), channel_id=1, source_target_pairs={{0,1},{1,2},{2,3},{3,0},{4,5},{5,6},{6,7},{7,4},{8,9},{9,10},{10,1... | collective-permute-start | bytes 491528 | tf_op jit(solution)/shard_map/ppermute | solution.py:32
  79.5 7.6 %collective-permute-start.3 = (bf16[8,16,640]{2,1,0:T(8,128)(2,1)S(1)}, bf16[8,16,640]{2,1,0:T(8,128)(2,1)S(1)}, u32[]{:S(2)}, u32[]{:S(2)}) collective-permute-start(bf16[8,16,640]{2,1,0:T(8,128)(2,1)S(1)} %get-tuple-element.17), channel_id=1, source_target_pairs={{0,2},{1,3},{2,0},{3,1},{4,6},{5,7},{6,4},{7,5},{8,10},{9,11},{10,... | collective-permute-start | bytes 491528 | tf_op jit(solution)/shard_map/ppermute | solution.py:32
  87.1 18.3 %collective-permute-start.9 = (bf16[4,8,16,640]{3,2,1,0:T(8,128)(2,1)S(1)}, bf16[4,8,16,640]{3,2,1,0:T(8,128)(2,1)S(1)}, u32[]{:S(2)}, u32[]{:S(2)}) collective-permute-start(bf16[4,8,16,640]{3,2,1,0:T(8,128)(2,1)S(1)} %pad_maximum_fusion.refs_0_), channel_id=1, source_target_pairs={{0,8},{1,9},{2,10},{3,11},{4,12},{5,13},{6,14},{7,15},{8,0},{9,1},... | collective-permute-start | bytes 1966088 | tf_op jit(solution)/shard_map/ppermute | solution.py:37
  92.1 25.0 %collective-permute-start.8 = (bf16[4,8,16,640]{3,2,1,0:T(8,128)(2,1)S(1)}, bf16[4,8,16,640]{3,2,1,0:T(8,128)(2,1)S(1)}, u32[]{:S(2)}, u32[]{:S(2)}) collective-permute-start(bf16[4,8,16,640]{3,2,1,0:T(8,128)(2,1)S(1)} %pad_maximum_fusion.refs_0_), channel_id=1, source_target_pairs={{0,12},{1,13},{2,14},{3,15},{4,0},{5,1},{6,2},{7,3},{8,4},{9,5},{1... | collective-permute-start | bytes 1966088 | tf_op jit(solution)/shard_map/ppermute | solution.py:37
  95.2 22.1 %collective-permute-start.7 = (bf16[4,8,16,640]{3,2,1,0:T(8,128)(2,1)S(1)}, bf16[4,8,16,640]{3,2,1,0:T(8,128)(2,1)S(1)}, u32[]{:S(2)}, u32[]{:S(2)}) collective-permute-start(bf16[4,8,16,640]{3,2,1,0:T(8,128)(2,1)S(1)} %pad_maximum_fusion.refs_0_), channel_id=1, source_target_pairs={{0,4},{1,5},{2,6},{3,7},{4,8},{5,9},{6,10},{7,11},{8,12},{9,13},{1... | collective-permute-start | bytes 1966088 | tf_op jit(solution)/shard_map/ppermute | solution.py:37
  97.4 19.9 %collective-permute-start.12 = (bf16[4,8,16,640]{3,2,1,0:T(8,128)(2,1)S(1)}, bf16[4,8,16,640]{3,2,1,0:T(8,128)(2,1)}, u32[]{:S(2)}, u32[]{:S(2)}) collective-permute-start(bf16[4,8,16,640]{3,2,1,0:T(8,128)(2,1)S(1)} %pad_maximum_fusion.1.refs_4_), channel_id=1, source_target_pairs={{0,2},{1,3},{2,0},{3,1},{4,6},{5,7},{6,4},{7,5},{8,10},{9,11},{10,... | collective-permute-start | bytes 1966088 | tf_op jit(solution)/shard_map/ppermute | solution.py:38
  100.4 27.9 %collective-permute-start.11 = (bf16[4,8,16,640]{3,2,1,0:T(8,128)(2,1)S(1)}, bf16[4,8,16,640]{3,2,1,0:T(8,128)(2,1)}, u32[]{:S(2)}, u32[]{:S(2)}) collective-permute-start(bf16[4,8,16,640]{3,2,1,0:T(8,128)(2,1)S(1)} %pad_maximum_fusion.1.refs_4_), channel_id=1, source_target_pairs={{0,3},{1,0},{2,1},{3,2},{4,7},{5,4},{6,5},{7,6},{8,11},{9,8},{10,9... | collective-permute-start | bytes 1966088 | tf_op jit(solution)/shard_map/ppermute | solution.py:38
  105.4 22.9 %collective-permute-start.10 = (bf16[4,8,16,640]{3,2,1,0:T(8,128)(2,1)S(1)}, bf16[4,8,16,640]{3,2,1,0:T(8,128)(2,1)}, u32[]{:S(2)}, u32[]{:S(2)}) collective-permute-start(bf16[4,8,16,640]{3,2,1,0:T(8,128)(2,1)S(1)} %pad_maximum_fusion.1.refs_4_), channel_id=1, source_target_pairs={{0,1},{1,2},{2,3},{3,0},{4,5},{5,6},{6,7},{7,4},{8,9},{9,10},{10,1... | collective-permute-start | bytes 1966088 | tf_op jit(solution)/shard_map/ppermute | solution.py:38
  199.3 3.2 %copy-start = (bf16[3,32,320,128]{3,2,1,0:T(8,128)(2,1)S(1)}, bf16[3,32,320,128]{3,2,1,0:T(8,128)(2,1)}, u32[]{:S(2)}) copy-start(bf16[3,32,320,128]{3,2,1,0:T(8,128)(2,1)} %get-tuple-element.9.grad_ref) | copy-start | bytes 23592964
Sparse Core Ops, SparseCore 0:
  10.1 101.3 all-gather.2

commit v2 on v0

v2 whole, which is shorter than its diff:
```python
import functools

import jax
import jax.numpy as jnp
import numpy as np
from jax import lax
from jax.experimental import pallas as pl
from jax.experimental.pallas import tpu as pltpu
from jax.sharding import PartitionSpec as P

EPSILON = 1e-06
SIDE = 4
MAIN = 128
SHIFTS = (0, 1, -1, 2)


def plane_moves(reps, stage, d):
    moves = []
    for r in range(reps):
        for y in range(SIDE):
            for x in range(SIDE):
                if (r + stage) % 2:
                    to = y * SIDE + (x + d) % SIDE
                else:
                    to = ((y + d) % SIDE) * SIDE + x
                moves.append((r * SIDE * SIDE + y * SIDE + x, r * SIDE * SIDE + to))
    return moves


def gather_pieces(piece, reps):
    def move(value, stage, d):
        return lax.ppermute(value, ("replica", "shard"), plane_moves(reps, stage, d))

    after, before, far = [move(piece, 0, d) for d in SHIFTS[1:]]
    low, high = jnp.stack([piece, after]), jnp.stack([before, far])
    low_after = move(low, 1, 1)
    high_before = move(high, 1, -1)
    low_before = move(low, 1, -1)
    high_after = move(high, 1, 1)
    low_far = move(low_after, 1, 1)
    high_far = move(high_before, 1, -1)
    return [low, high, low_after, high_after, low_before, high_before, low_far, high_far]


def piece_offsets(tokens_piece):
    me = lax.axis_index("shard")
    core = lax.axis_index("replica") % 2
    y, x = me // SIDE, me % SIDE
    d = jnp.array(SHIFTS, jnp.int32)
    first, second = d[None, :], d[:, None]
    off_0 = ((y - second) % SIDE) * SIDE + (x - first) % SIDE
    off_1 = ((y - first) % SIDE) * SIDE + (x - second) % SIDE
    off = jnp.where(core == 1, off_0, off_1)
    return (off * tokens_piece).astype(jnp.int32).reshape(-1)


def gradient_kernel(off_ref, ctx_hbm, *refs):
    pieces = refs[:8]
    grad_hbm, gram_ref, ctx_ref, cot_ref, grad_ref, acc_ref, ctx_sems, cot_sems, grad_sems = refs[8:]
    chips, _, _, rows, tokens = ctx_hbm.shape
    _, _, tok, width = pieces[0].shape
    reps = 2 * chips
    rem = (width - 4 * MAIN) // 4
    fold = MAIN // rem
    low = rows // fold
    groups = cot_sems.shape[0]
    span = chips // groups

    def ctx_copy(chip):
        return pltpu.make_async_copy(ctx_hbm.at[chip], ctx_ref.at[chip], ctx_sems.at[chip])

    def cot_copy(group, second, first):
        off = pl.multiple_of(off_ref[second * 4 + first], tok)
        part = pl.ds(group * span, span)
        return pltpu.make_async_copy(
            pieces[second * 2 + first // 2].at[first % 2, part],
            cot_ref.at[part, pl.ds(off, tok), :],
            cot_sems.at[group, second, first],
        )

    def grad_copy(chip):
        part = pl.ds(chip * 2, 2)
        return pltpu.make_async_copy(
            grad_ref.at[:, part], grad_hbm.at[:, part], grad_sems.at[chip]
        )

    for group in range(groups):
        for second in range(4):
            for first in range(4):
                cot_copy(group, second, first).start()
        for chip in range(group * span, (group + 1) * span):
            ctx_copy(chip).start()

    quarter = lax.broadcasted_iota(jnp.int32, (low, MAIN), 1) // rem

    def one_chip(chip, carry):
        ctx_copy(chip).wait()
        edge = cot_ref[chip, :, 4 * MAIN :]
        for core in range(2):
            for layer in range(2):
                j = 2 * core + layer
                rhs = jnp.concatenate([cot_ref[chip, :, j * MAIN : (j + 1) * MAIN], edge], axis=1)
                g = jnp.dot(ctx_ref[chip, core, layer], rhs, preferred_element_type=jnp.float32)
                packed = None
                for q in range(fold):
                    part = g[q * low : (q + 1) * low, MAIN:]
                    if (q - j) % fold:
                        part = pltpu.roll(part, ((q - j) % fold) * rem, 1)
                    packed = part if packed is None else jnp.where(quarter == q, part, packed)
                for at, size, value in ((0, rows, g[:, :MAIN]), (rows, low, packed)):
                    grad_ref[layer, chip * 2 + core, at : at + size] = value.astype(jnp.bfloat16)
        grad_copy(chip).start()
        return carry

    for group in range(groups):
        for second in range(4):
            for first in range(4):
                cot_copy(group, second, first).wait()
        lax.fori_loop(group * span, (group + 1) * span, one_chip, 0)

    size = reps * 8
    deep = 5
    acc_ref[...] = jnp.zeros_like(acc_ref)

    def body(i, carry):
        for layer in range(2):
            parts = []
            for u in range(deep):
                at = pl.multiple_of((i * deep + u) * 16, 16)
                part = grad_ref[layer, :, pl.ds(at, 16), :].astype(jnp.float32)
                part = part.reshape(reps, 2, 8, MAIN)
                for h in range(2):
                    parts.append(part[:, h].reshape(size, MAIN).astype(jnp.bfloat16))
            part = jnp.concatenate(parts, axis=1)
            acc_ref[layer] += lax.dot_general(
                part, part, (((1,), (1,)), ((), ())), preferred_element_type=jnp.float32
            )
        return carry

    lax.fori_loop(0, (rows + low) // (16 * deep), body, 0)
    ri = lax.broadcasted_iota(jnp.int32, (size, size), 0)
    ci = lax.broadcasted_iota(jnp.int32, (size, size), 1)
    si = lax.broadcasted_iota(jnp.int32, (size, MAIN), 0)
    sj = lax.broadcasted_iota(jnp.int32, (size, MAIN), 1)
    rows_of = []
    for layer in range(2):
        z = jnp.where(ri % 8 == ci % 8, acc_ref[layer], 0.0)
        rows_of.append(jnp.sum(z.reshape(reps, 8, size), axis=1))
    pick = jnp.where(sj % 32 == si // 8, 1.0, 0.0)
    z = jnp.dot(
        jnp.concatenate(rows_of, axis=0),
        pick,
        precision=lax.Precision.HIGHEST,
        preferred_element_type=jnp.float32,
    )
    place = lax.broadcasted_iota(jnp.int32, (16, MAIN), 1) // 32
    total = z[:16]
    for k in range(1, 4):
        total = jnp.where(place == k, z[16 * k : 16 * (k + 1)], total)
    gram_ref[...] = total
    for chip in range(chips):
        grad_copy(chip).wait()


def gradients(ctx, pieces, offsets, tokens):
    reps, rows2, _ = ctx.shape
    rows = rows2 // 2
    rem = (pieces[0].shape[-1] - 4 * MAIN) // 4
    _, chips, tok, width = pieces[0].shape
    held = rows + rows * rem // MAIN
    groups = 4
    ctx = ctx.reshape(chips, 2, 2, rows, tokens)
    return pl.pallas_call(
        gradient_kernel,
        in_specs=[pl.BlockSpec(memory_space=pltpu.SMEM)] + [pl.BlockSpec(memory_space=pltpu.HBM)] * 9,
        out_specs=[pl.BlockSpec(memory_space=pltpu.HBM), pl.BlockSpec(memory_space=pltpu.VMEM)],
        scratch_shapes=[
            pltpu.VMEM((chips, 2, 2, rows, tokens), jnp.bfloat16),
            pltpu.VMEM((chips, tokens, width), jnp.bfloat16),
            pltpu.VMEM((2, reps, held, MAIN), jnp.bfloat16),
            pltpu.VMEM((2, reps * 8, reps * 8), jnp.float32),
            pltpu.SemaphoreType.DMA((chips,)),
            pltpu.SemaphoreType.DMA((groups, 4, 4)),
            pltpu.SemaphoreType.DMA((chips,)),
        ],
        out_shape=[
            jax.ShapeDtypeStruct((2, reps, held, MAIN), jnp.bfloat16),
            jax.ShapeDtypeStruct((16, MAIN), jnp.float32),
        ],
        compiler_params=pltpu.CompilerParams(vmem_limit_bytes=48 * 1024 * 1024),
    )(offsets, ctx, *pieces)


def tree_weights(gram):
    n = gram.shape[0]
    ri = lax.broadcasted_iota(jnp.int32, (n, n), 0)
    ci = lax.broadcasted_iota(jnp.int32, (n, n), 1)
    weight = jnp.ones((n, 1), jnp.float32)
    for k in range(n.bit_length() - 1):
        same = (ri >> k) == (ci >> k)
        other = (ri >> k) == ((ci >> k) ^ 1)
        twin = ri == (ci ^ (1 << k))
        own = jnp.where(same, gram, 0.0)
        cross = jnp.where(other, gram, 0.0)
        coeffs = []
        for axis in (1, 0):
            norm = jnp.sum(own, axis=1 - axis, keepdims=True)
            norm = jnp.sum(jnp.where(same, norm, 0.0), axis=axis, keepdims=True)
            inner = jnp.sum(cross, axis=1 - axis, keepdims=True)
            inner = jnp.sum(jnp.where(same, inner, 0.0), axis=axis, keepdims=True)
            coeffs.append((jnp.maximum(norm, 0.0), inner))
        (norm_r, inner_r), (norm_c, inner_c) = coeffs
        twin_r = jnp.sum(jnp.where(twin, norm_c, 0.0), axis=1, keepdims=True)
        twin_c = jnp.sum(jnp.where(twin, norm_r, 0.0), axis=0, keepdims=True)
        cap_r = jnp.sqrt(norm_r) * jnp.sqrt(twin_r)
        cap_c = jnp.sqrt(norm_c) * jnp.sqrt(twin_c)
        inner_r = jnp.clip(inner_r, -cap_r, cap_r)
        inner_c = jnp.clip(inner_c, -cap_c, cap_c)
        coeff_r = 1.0 - inner_r / (2.0 * (norm_r + EPSILON))
        coeff_c = 1.0 - inner_c / (2.0 * (norm_c + EPSILON))
        weight = weight * coeff_r
        gram = gram * coeff_r * coeff_c
    return weight


def combine_kernel(scale, gram_ref, grad_hbm, one_hbm, two_hbm, *scratch):
    grad_ref, one_ref, two_ref, weight_ref, grad_sems, out_sems = scratch
    _, reps, held, _ = grad_ref.shape
    cols, rows = one_ref.shape
    rem = cols - MAIN
    low = held - rows
    starts = range(0, held, low)

    def grad_copy(layer, k):
        part = pl.ds(k * low, low)
        return pltpu.make_async_copy(
            grad_hbm.at[layer, :, part], grad_ref.at[layer, :, part], grad_sems.at[layer, k]
        )

    for layer in range(2):
        for k in range(len(starts)):
            grad_copy(layer, k).start()
    total = jnp.sum(gram_ref[...], axis=0) * (scale * scale)
    for layer in range(2):
        parts = [total[:, (2 * layer + h) * 32 : (2 * layer + h + 1) * 32] for h in range(2)]
        weights = tree_weights(jnp.concatenate(parts, axis=0))
        weight_ref[layer] = jnp.broadcast_to(weights * scale, (reps, MAIN))
    outs = []
    for layer, (out_ref, out_hbm) in enumerate(((one_ref, one_hbm), (two_ref, two_hbm))):
        sums = []
        for k, at in enumerate(starts):
            grad_copy(layer, k).wait()
            acc = jnp.zeros((low, MAIN), jnp.float32)
            for r in range(reps):
                value = grad_ref[layer, r, at : at + low].astype(jnp.float32)
                acc += weight_ref[layer, r : r + 1, :] * value
            sums.append(acc)
        out_ref[:MAIN] = jnp.concatenate(sums[:-1], axis=0).T
        edge = sums[-1].T
        for q in range(MAIN // rem):
            out_ref[MAIN:, q * low : (q + 1) * low] = edge[q * rem : (q + 1) * rem]
        outs.append(pltpu.make_async_copy(out_ref, out_hbm, out_sems.at[layer]))
        outs[-1].start()
    for out in outs:
        out.wait()


def combine(gram_parts, grads, rows, cols, scale):
    out = pltpu.HBM((cols, rows), jnp.float32)
    grads = pltpu.with_memory_space_constraint(grads, pltpu.HBM)
    held = grads.shape[2]
    return pl.pallas_call(
        functools.partial(combine_kernel, scale),
        in_specs=[pl.BlockSpec(memory_space=pltpu.VMEM), pl.BlockSpec(memory_space=pltpu.HBM)],
        out_specs=[pl.BlockSpec(memory_space=pltpu.HBM)] * 2,
        out_shape=[out] * 2,
        scratch_shapes=[
            pltpu.VMEM(grads.shape, grads.dtype),
            pltpu.VMEM((cols, rows), jnp.float32),
            pltpu.VMEM((cols, rows), jnp.float32),
            pltpu.VMEM((2, grads.shape[1], MAIN), jnp.float32),
            pltpu.SemaphoreType.DMA((2, held // (held - rows))),
            pltpu.SemaphoreType.DMA((2,)),
        ],
        compiler_params=pltpu.CompilerParams(vmem_limit_bytes=32 * 1024 * 1024),
    )(gram_parts, grads)


def split_kernel(core_ref, a_ref, b_ref, one_ref, two_ref, ctx_ref, keep_ref, give_ref):
    rows = a_ref.shape[0]
    cols = rows // 2
    rem = cols - MAIN
    ctx_ref[:rows] = a_ref[...]
    ctx_ref[rows:] = b_ref[...]

    def fill(out_ref, core):
        for layer, ref in enumerate((one_ref, two_ref)):
            at = core * cols
            out_ref[layer * MAIN : (layer + 1) * MAIN] = ref[at : at + MAIN]
            to = 2 * MAIN + layer * rem
            out_ref[to : to + rem] = ref[at + MAIN : at + cols]

    for core in range(2):

        @pl.when(core_ref[0] == core)
        def _():
            fill(give_ref, 1 - core)
            fill(keep_ref, core)


def split_columns(core, contexts, cotangents):
    shape, dtype = contexts[0].shape, contexts[0].dtype
    return pl.pallas_call(
        split_kernel,
        in_specs=[pl.BlockSpec(memory_space=pltpu.SMEM)]
        + [pl.BlockSpec(memory_space=pltpu.VMEM)] * 4,
        out_specs=[pl.BlockSpec(memory_space=pltpu.VMEM)] * 3,
        out_shape=[
            jax.ShapeDtypeStruct((2 * shape[0], shape[1]), dtype),
            jax.ShapeDtypeStruct(shape, dtype),
            jax.ShapeDtypeStruct(shape, dtype),
        ],
    )(core, *contexts, *cotangents)


def join_kernel(core_ref, keep_ref, got_ref, out_ref):
    main = 2 * MAIN

    def fill(first, second):
        parts = [first[:main], second[:main], first[main:], second[main:]]
        out_ref[...] = jnp.concatenate(parts, axis=0).T

    for core, (first, second) in enumerate(((keep_ref, got_ref), (got_ref, keep_ref))):

        @pl.when(core_ref[0] == core)
        def _():
            fill(first, second)


def join_columns(core, keep, got):
    cols, tokens = keep.shape
    return pl.pallas_call(
        join_kernel,
        in_specs=[pl.BlockSpec(memory_space=pltpu.SMEM)]
        + [pl.BlockSpec(memory_space=pltpu.VMEM)] * 2,
        out_specs=pl.BlockSpec(memory_space=pltpu.VMEM),
        out_shape=jax.ShapeDtypeStruct((tokens, 2 * cols), keep.dtype),
    )(core, keep, got)


def shards(context_one, cotangent_one, context_two, cotangent_two):
    tokens, feats = context_one.shape
    reps = lax.axis_size("replica")
    n_shards = lax.axis_size("shard")
    cols = feats // 2
    core = (lax.axis_index("replica") % 2).reshape(1).astype(jnp.int32)
    same_core = [list(range(c, reps, 2)) for c in range(2)]

    ctx, keep, give = split_columns(
        core, (context_one.T, context_two.T), (cotangent_one.T, cotangent_two.T)
    )
    ctx = lax.all_gather(ctx, "replica")
    got = lax.ppermute(give, "replica", [(i, i ^ 1) for i in range(reps)])
    cot = join_columns(core, keep, got)
    cot = cot.reshape(n_shards, tokens // n_shards, cot.shape[1])
    cot = lax.all_to_all(cot, "shard", 0, 0)
    cot = lax.all_to_all(cot, "replica", 0, 0, axis_index_groups=same_core)
    pieces = gather_pieces(cot, reps)

    offsets = piece_offsets(tokens // n_shards)
    grads, gram = gradients(ctx, pieces, offsets, tokens)
    gram = gram + lax.ppermute(gram, "replica", [(i, i ^ 1) for i in range(reps)])
    gram = jnp.broadcast_to(gram[None], (n_shards,) + gram.shape)
    gram = jnp.sum(lax.all_to_all(gram, "shard", 0, 0), axis=0)
    gram = jnp.broadcast_to(gram[None], (reps // 2,) + gram.shape)
    gram = lax.all_to_all(gram, "replica", 0, 0, axis_index_groups=same_core)
    one, two = combine(gram, grads, feats, cols, 1.0 / tokens)
    return one.T, two.T


def solution(mesh):
    spec = P("replica", "shard")
    return jax.shard_map(
        shards,
        mesh=mesh,
        in_specs=(spec, spec, spec, spec),
        out_specs=(P("shard", "replica"), P("shard", "replica")),
        check_vma=False,
    )
```

time: 703 us -> 174 us (0.25)
  waiting for transfers between devices: 247 us -> 18.9 us
  starting transfers between devices: 177 us -> 43.1 us
  blocking collectives: 148 us -> 72.7 us
  between operations: 65 us -> 14.2 us
  other arithmetic: 32.6 us -> 0.91 us
  local copies, waits for them, and re-layouts: 25 us -> 0.77 us
  Pallas kernels: 0 us -> 21.1 us
    psum x5 -> x0, blocking collectives: 148 us -> none  [group_total(): totals = lax.psum(partial_value, 'shard')]
    ppermute x40 -> x11, starting transfers between devices: 177 us -> 43.1 us  [the longest x9 26.2 us: move(): lax.ppermute(value, ('replica', 'shard'), plane_moves(reps, stage, d))]
    all_gather x2 -> x1, waiting for transfers between devices: 120 us -> 1.26 us  [shards(): ctx = lax.all_gather(ctx, 'replica')]
    ppermute x40 -> x11, waiting for transfers between devices: 125 us -> 17.6 us  [the longest x9 15.6 us: move(): lax.ppermute(value, ('replica', 'shard'), plane_moves(reps, stage, d))]
    all_to_all x0 -> x4, blocking collectives: none -> 72.7 us  [the longest x1 33.2 us: shards(): cot = lax.all_to_all(cot, 'replica', 0, 0, axis_index_groups=same_core)]
    pallas_call x0 -> x4, Pallas kernels: none -> 21.1 us  [the longest x1 13.2 us: gradients(): pl.pallas_call(gradient_kernel, in_specs=[pl.BlockSpec(memory_space=pltpu...]
    reduce_sum x10 -> x1, other arithmetic: 15.4 us -> 0.02 us  [shards(): gram = jnp.sum(lax.all_to_all(gram, 'shard', 0, 0), axis=0)]
    squeeze x10 -> x0, local copies, waits for them, and re-layouts: 10.1 us -> none  [run_sections(): lax.dynamic_index_in_dim(carried, 1 - my_bit, position, keepdims=False)]
  transfers between devices with their start and end apart: 42 -> 12, of which waited for: 12 -> 10; matrix products, arithmetic and copies ran while one was open for 5% -> 1% of each run, Pallas kernels for 0% -> 1%
where the time goes in v2:
time: 174 us; the launch traced here: 172 us
  blocking collectives  72.7 us (42%)
  starting transfers between devices  43.1 us (25%)
  Pallas kernels  21.1 us (12%)
  waiting for transfers between devices  18.9 us (11%)
  between operations  14.2 us (8%)
    all_to_all x1, blocking collectives, shards(): cot = lax.all_to_all(cot, 'replica', 0, 0, axis_index_groups=same_core)  33.2 us
    ppermute x9, starting transfers between devices, move(): lax.ppermute(value, ('replica', 'shard'), plane_moves(reps, stage, d))  26.2 us
    all_to_all x1, blocking collectives, shards(): gram = lax.all_to_all(gram, 'replica', 0, 0, axis_index_groups=same_core)  16.6 us
    ppermute x9, waiting for transfers between devices, move(): lax.ppermute(value, ('replica', 'shard'), plane_moves(reps, stage, d))  15.6 us
    pallas_call x1, Pallas kernels, gradients(): pl.pallas_call(gradient_kernel, in_specs=[pl.BlockSpec(memory_space=pltpu...  13.2 us
    all_to_all x1, blocking collectives, shards(): cot = lax.all_to_all(cot, 'shard', 0, 0)  12.5 us
    all_to_all x1, blocking collectives, shards(): gram = jnp.sum(lax.all_to_all(gram, 'shard', 0, 0), axis=0)  10.5 us
    ppermute x1, starting transfers between devices, shards(): got = lax.ppermute(give, 'replica', [(i, i ^ 1) for i in range(reps)])  8.79 us
  transfers between devices with their start and end apart: 12, of which 10 were waited for; matrix products, arithmetic and copies ran while one was open for 1% of the time, Pallas kernels for 1%

profile of v2, /device:TPU:1, one launch (start us, length us, event | category | flops | bytes accessed | tf_op | source)
XLA Modules:
  0.0 171.7 jit_solution(14569655983185377075)
XLA Ops:
  7.2 0.0 all-gather.3.cloned.1.call-start
  7.2 2.0 %shard_map.68 = (bf16[640,256]{1,0:T(8,128)(2,1)}, bf16[320,256]{1,0:T(8,128)(2,1)}, bf16[320,256]{1,0:T(8,128)(2,1)}) custom-call(s32[1]{0:T(128)} %bitcast.core_ref, bf16[320,256]{1,0:T(8,128)(2,1)} %bitcast.19, bf16[320,256]{1,0:T(8,128)(2,1)} %bitcast.20, bf16[320,256]{1,0:T(8,128)(2,1)} %bitcast.21, bf16[320,256]{1,0:T(8,128)(2,1)} %bitcast.22), custom_call_target="tpu_custom_call" | custom-call | tf_op jit(solution)/shard_map/pallas_call | solution.py:313
  9.2 0.0 all-gather.3.cloned.1.call-update
  9.3 8.8 %collective-permute-start = (bf16[320,256]{1,0:T(8,128)(2,1)}, bf16[320,256]{1,0:T(8,128)(2,1)S(1)}, u32[]{:S(2)}, u32[]{:S(2)}) collective-permute-start(bf16[320,256]{1,0:T(8,128)(2,1)} %get-tuple-element.11), channel_id=1, source_target_pairs={{0,16},{16,0},{32,48},{48,32},{64,80},{80,64},{96,112},{112,96},{1... | collective-permute-start | bytes 491528 | tf_op jit(solution)/shard_map/ppermute | solution.py:363
  18.1 1.2 collective-permute-done.got_ref
  19.3 0.0 copy-start
  19.3 0.7 copy-done
  20.0 1.9 %shard_map.69 = bf16[256,640]{1,0:T(8,128)(2,1)} custom-call(s32[1]{0:T(128)} %bitcast.core_ref, bf16[320,256]{1,0:T(8,128)(2,1)} %get-tuple-element.10.keep_ref, bf16[320,256]{1,0:T(8,128)(2,1)} %copy-done), custom_call_target="tpu_custom_call" | custom-call | tf_op jit(solution)/shard_map/pallas_call | solution.py:342
  21.8 12.5 %all_to_all.20 = bf16[16,16,640]{2,1,0:T(8,128)(2,1)S(1)} all-to-all(bf16[16,16,640]{2,1,0:T(8,128)(2,1)} %bitcast.15), channel_id=1, replica_groups=mesh['replica'=32,'shard'=16] {'shard'}, dimensions={0} | all-to-all | bytes 655360 | tf_op jit(solution)/shard_map/all_to_all | solution.py:366
  34.3 33.2 %all_to_all.21 = bf16[16,16,640]{2,1,0:T(8,128)(2,1)S(1)} all-to-all(bf16[16,16,640]{2,1,0:T(8,128)(2,1)S(1)} %all_to_all.20), channel_id=1, replica_groups={{0,32,64,96,128,160,192,224,256,288,320,352,384,416,448,480},{16,48,80,..., dimensions={0} | all-to-all | bytes 655360 | tf_op jit(solution)/shard_map/all_to_all | solution.py:367
  67.5 2.5 %collective-permute-start.1 = (bf16[16,16,640]{2,1,0:T(8,128)(2,1)S(1)}, bf16[16,16,640]{2,1,0:T(8,128)(2,1)S(1)}, u32[]{:S(2)}, u32[]{:S(2)}) collective-permute-start(bf16[16,16,640]{2,1,0:T(8,128)(2,1)S(1)} %all_to_all.21), channel_id=1, source_target_pairs={{0,4},{1,5},{2,6},{3,7},{4,8},{5,9},{6,10},{7,11},{8,12},{9,13},{1... | collective-permute-start | bytes 983048 | tf_op jit(solution)/shard_map/ppermute | solution.py:32
  69.9 1.9 %collective-permute-start.3 = (bf16[16,16,640]{2,1,0:T(8,128)(2,1)S(1)}, bf16[16,16,640]{2,1,0:T(8,128)(2,1)S(1)}, u32[]{:S(2)}, u32[]{:S(2)}) collective-permute-start(bf16[16,16,640]{2,1,0:T(8,128)(2,1)S(1)} %all_to_all.21), channel_id=1, source_target_pairs={{0,8},{1,9},{2,10},{3,11},{4,12},{5,13},{6,14},{7,15},{8,0},{9,1},... | collective-permute-start | bytes 983048 | tf_op jit(solution)/shard_map/ppermute | solution.py:32
  71.9 4.3 %collective-permute-start.2 = (bf16[16,16,640]{2,1,0:T(8,128)(2,1)S(1)}, bf16[16,16,640]{2,1,0:T(8,128)(2,1)S(1)}, u32[]{:S(2)}, u32[]{:S(2)}) collective-permute-start(bf16[16,16,640]{2,1,0:T(8,128)(2,1)S(1)} %all_to_all.21), channel_id=1, source_target_pairs={{0,12},{1,13},{2,14},{3,15},{4,0},{5,1},{6,2},{7,3},{8,4},{9,5},{1... | collective-permute-start | bytes 983048 | tf_op jit(solution)/shard_map/ppermute | solution.py:32
  76.2 4.2 %collective-permute-done.1 = bf16[16,16,640]{2,1,0:T(8,128)(2,1)S(1)} collective-permute-done((bf16[16,16,640]{2,1,0:T(8,128)(2,1)S(1)}, bf16[16,16,640]{2,1,0:T(8,128)(2,1)S(1)}, u32[]{:S(2)}, u32[]{:S(2)}) %collective-permute-start.1) | collective-permute-done | bytes 327712 | tf_op jit(solution)/shard_map/ppermute | solution.py:32
  80.4 0.1 pad_maximum_fusion.refs_0_
  80.4 2.0 %collective-permute-start.4 = (bf16[2,16,16,640]{3,2,1,0:T(8,128)(2,1)S(1)}, bf16[2,16,16,640]{3,2,1,0:T(8,128)(2,1)S(1)}, u32[]{:S(2)}, u32[]{:S(2)}) collective-permute-start(bf16[2,16,16,640]{3,2,1,0:T(8,128)(2,1)S(1)} %pad_maximum_fusion.refs_0_), channel_id=1, source_target_pairs={{0,1},{1,2},{2,3},{3,0},{4,5},{5,6},{6,7},{7,4},{8,9},{9,10},{10,1... | collective-permute-start | bytes 1966088 | tf_op jit(solution)/shard_map/ppermute | solution.py:32
  82.4 0.0 collective-permute-done.3
  82.4 0.5 collective-permute-done.2
  82.9 0.1 pad_maximum_fusion.1.refs_1_
  83.0 4.1 %collective-permute-start.7 = (bf16[2,16,16,640]{3,2,1,0:T(8,128)(2,1)S(1)}, bf16[2,16,16,640]{3,2,1,0:T(8,128)(2,1)S(1)}, u32[]{:S(2)}, u32[]{:S(2)}) collective-permute-start(bf16[2,16,16,640]{3,2,1,0:T(8,128)(2,1)S(1)} %pad_maximum_fusion.1.refs_1_), channel_id=1, source_target_pairs={{0,3},{1,0},{2,1},{3,2},{4,7},{5,4},{6,5},{7,6},{8,11},{9,8},{10,9... | collective-permute-start | bytes 1966088 | tf_op jit(solution)/shard_map/ppermute | solution.py:32
  87.0 2.7 %collective-permute-start.6 = (bf16[2,16,16,640]{3,2,1,0:T(8,128)(2,1)S(1)}, bf16[2,16,16,640]{3,2,1,0:T(8,128)(2,1)S(1)}, u32[]{:S(2)}, u32[]{:S(2)}) collective-permute-start(bf16[2,16,16,640]{3,2,1,0:T(8,128)(2,1)S(1)} %pad_maximum_fusion.refs_0_), channel_id=1, source_target_pairs={{0,3},{1,0},{2,1},{3,2},{4,7},{5,4},{6,5},{7,6},{8,11},{9,8},{10,9... | collective-permute-start | bytes 1966088 | tf_op jit(solution)/shard_map/ppermute | solution.py:32
  89.7 2.6 %collective-permute-start.5 = (bf16[2,16,16,640]{3,2,1,0:T(8,128)(2,1)S(1)}, bf16[2,16,16,640]{3,2,1,0:T(8,128)(2,1)}, u32[]{:S(2)}, u32[]{:S(2)}) collective-permute-start(bf16[2,16,16,640]{3,2,1,0:T(8,128)(2,1)S(1)} %pad_maximum_fusion.1.refs_1_), channel_id=1, source_target_pairs={{0,1},{1,2},{2,3},{3,0},{4,5},{5,6},{6,7},{7,4},{8,9},{9,10},{10,1... | collective-permute-start | bytes 1966088 | tf_op jit(solution)/shard_map/ppermute | solution.py:32
  92.3 1.2 collective-permute-done.4.refs_2_
  93.5 1.9 %collective-permute-start.8 = (bf16[2,16,16,640]{3,2,1,0:T(8,128)(2,1)S(1)}, bf16[2,16,16,640]{3,2,1,0:T(8,128)(2,1)}, u32[]{:S(2)}, u32[]{:S(2)}) collective-permute-start(bf16[2,16,16,640]{3,2,1,0:T(8,128)(2,1)S(1)} %collective-permute-done.4.refs_2_), channel_id=1, source_target_pairs={{0,1},{1,2},{2,3},{3,0},{4,5},{5,6},{6,7},{7,4},{8,9},{9,10},{10,1... | collective-permute-start | bytes 1966088 | tf_op jit(solution)/shard_map/ppermute | solution.py:32
  95.4 0.9 collective-permute-done.7.refs_5_
  96.3 4.3 %collective-permute-start.9 = (bf16[2,16,16,640]{3,2,1,0:T(8,128)(2,1)S(1)}, bf16[2,16,16,640]{3,2,1,0:T(8,128)(2,1)}, u32[]{:S(2)}, u32[]{:S(2)}) collective-permute-start(bf16[2,16,16,640]{3,2,1,0:T(8,128)(2,1)S(1)} %collective-permute-done.7.refs_5_), channel_id=1, source_target_pairs={{0,3},{1,0},{2,1},{3,2},{4,7},{5,4},{6,5},{7,6},{8,11},{9,8},{10,9... | collective-permute-start | bytes 1966088 | tf_op jit(solution)/shard_map/ppermute | solution.py:32
  100.6 0.7 fusion.1
  101.3 0.1 select_multiply_fusion
  101.3 0.1 mul.15.off_ref
  101.4 1.9 %collective-permute-done.6.refs_4_ = bf16[2,16,16,640]{3,2,1,0:T(8,128)(2,1)S(1)} collective-permute-done((bf16[2,16,16,640]{3,2,1,0:T(8,128)(2,1)S(1)}, bf16[2,16,16,640]{3,2,1,0:T(8,128)(2,1)S(1)}, u32[]{:S(2)}, u32[]{:S(2)}) %collective-permute-start.6) | collective-permute-done | bytes 655392 | tf_op jit(solution)/shard_map/ppermute | solution.py:32
  103.3 0.0 collective-permute-done.5.refs_3_
  103.3 6.4 %collective-permute-done.8.refs_6_ = bf16[2,16,16,640]{3,2,1,0:T(8,128)(2,1)} collective-permute-done((bf16[2,16,16,640]{3,2,1,0:T(8,128)(2,1)S(1)}, bf16[2,16,16,640]{3,2,1,0:T(8,128)(2,1)}, u32[]{:S(2)}, u32[]{:S(2)}) %collective-permute-start.8) | collective-permute-done | bytes 655392 | tf_op jit(solution)/shard_map/ppermute | solution.py:32
  109.7 0.6 collective-permute-done.9.refs_7_
  110.3 1.3 all-gather.3.cloned.1.call-done
  111.6 13.2 %shard_map.70 = (bf16[2,32,400,128]{3,2,1,0:T(8,128)(2,1)}, f32[16,128]{1,0:T(8,128)S(1)}) custom-call(s32[16]{0:T(128)S(1)} %mul.15.off_ref, bf16[16,2,2,320,256]{4,3,2,1,0:T(8,128)(2,1)} %bitcast.13, bf16[2,16,16,640]{3,2,1,0:T(8,128)(2,1)S(1)} %pad_maximum_fusion.refs_0_, bf16[2,16,16,640]{3,2,1,0:T(8,128)(2,1)S(1)} %pad_maximum_fusion.1.refs_1_, ...), custom_call_target="tpu_custom_call" | custom-call | tf_op jit(solution)/shard_map/pallas_call | solution.py:173
  124.8 8.1 %collective-permute-start.10 = (f32[16,128]{1,0:T(8,128)S(1)}, f32[16,128]{1,0:T(8,128)S(1)}, u32[]{:S(2)}, u32[]{:S(2)}) collective-permute-start(f32[16,128]{1,0:T(8,128)S(1)} %get-tuple-element.12), channel_id=1, source_target_pairs={{0,16},{16,0},{32,48},{48,32},{64,80},{80,64},{96,112},{112,96},{1... | collective-permute-start | bytes 24584 | tf_op jit(solution)/shard_map/ppermute | solution.py:372
  132.9 0.8 collective-permute-done.10
  133.7 10.5 %all_to_all.22 = f32[16,16,128]{2,1,0:T(8,128)S(1)} all-to-all(f32[16,16,128]{2,1,0:T(8,128)S(1)} %broadcast_in_dim.4), channel_id=1, replica_groups=mesh['replica'=32,'shard'=16] {'shard'}, dimensions={0} | all-to-all | bytes 262144 | tf_op jit(solution)/shard_map/all_to_all | solution.py:374
  144.2 16.6 %all_to_all.23.gram_ref = f32[16,16,128]{2,1,0:T(8,128)S(1)} all-to-all(f32[16,16,128]{2,1,0:T(8,128)S(1)} %broadcast_in_dim.5), channel_id=1, replica_groups={{0,32,64,96,128,160,192,224,256,288,320,352,384,416,448,480},{16,48,80,..., dimensions={0} | all-to-all | bytes 262144 | tf_op jit(solution)/shard_map/all_to_all | solution.py:376
  160.8 4.0 %shard_map.71 = (f32[160,320]{1,0:T(8,128)}, f32[160,320]{1,0:T(8,128)}) custom-call(f32[16,16,128]{2,1,0:T(8,128)S(1)} %all_to_all.23.gram_ref, bf16[2,32,400,128]{3,2,1,0:T(8,128)(2,1)} %get-tuple-element.13.grad_hbm), custom_call_target="tpu_custom_call" | custom-call | tf_op jit(solution)/shard_map/pallas_call | solution.py:272
  (4 shorter events, 0.0 us)
Async XLA Ops:
  7.2 104.4 %all-gather.3.cloned.1.call-start = ((), (), s32[]{:S(2)}) async-start(), calls=%async_computation.4 | async-start | bytes 10813440 | tf_op jit(solution)/shard_map/all_gather | solution.py:362
  9.3 10.0 %collective-permute-start = (bf16[320,256]{1,0:T(8,128)(2,1)}, bf16[320,256]{1,0:T(8,128)(2,1)S(1)}, u32[]{:S(2)}, u32[]{:S(2)}) collective-permute-start(bf16[320,256]{1,0:T(8,128)(2,1)} %get-tuple-element.11), channel_id=1, source_target_pairs={{0,16},{16,0},{32,48},{48,32},{64,80},{80,64},{96,112},{112,96},{1... | collective-permute-start | bytes 491528 | tf_op jit(solution)/shard_map/ppermute | solution.py:363
  19.3 0.7 copy-start
  67.5 12.9 %collective-permute-start.1 = (bf16[16,16,640]{2,1,0:T(8,128)(2,1)S(1)}, bf16[16,16,640]{2,1,0:T(8,128)(2,1)S(1)}, u32[]{:S(2)}, u32[]{:S(2)}) collective-permute-start(bf16[16,16,640]{2,1,0:T(8,128)(2,1)S(1)} %all_to_all.21), channel_id=1, source_target_pairs={{0,4},{1,5},{2,6},{3,7},{4,8},{5,9},{6,10},{7,11},{8,12},{9,13},{1... | collective-permute-start | bytes 983048 | tf_op jit(solution)/shard_map/ppermute | solution.py:32
  69.9 12.5 %collective-permute-start.3 = (bf16[16,16,640]{2,1,0:T(8,128)(2,1)S(1)}, bf16[16,16,640]{2,1,0:T(8,128)(2,1)S(1)}, u32[]{:S(2)}, u32[]{:S(2)}) collective-permute-start(bf16[16,16,640]{2,1,0:T(8,128)(2,1)S(1)} %all_to_all.21), channel_id=1, source_target_pairs={{0,8},{1,9},{2,10},{3,11},{4,12},{5,13},{6,14},{7,15},{8,0},{9,1},... | collective-permute-start | bytes 983048 | tf_op jit(solution)/shard_map/ppermute | solution.py:32
  71.9 11.0 %collective-permute-start.2 = (bf16[16,16,640]{2,1,0:T(8,128)(2,1)S(1)}, bf16[16,16,640]{2,1,0:T(8,128)(2,1)S(1)}, u32[]{:S(2)}, u32[]{:S(2)}) collective-permute-start(bf16[16,16,640]{2,1,0:T(8,128)(2,1)S(1)} %all_to_all.21), channel_id=1, source_target_pairs={{0,12},{1,13},{2,14},{3,15},{4,0},{5,1},{6,2},{7,3},{8,4},{9,5},{1... | collective-permute-start | bytes 983048 | tf_op jit(solution)/shard_map/ppermute | solution.py:32
  80.4 13.1 %collective-permute-start.4 = (bf16[2,16,16,640]{3,2,1,0:T(8,128)(2,1)S(1)}, bf16[2,16,16,640]{3,2,1,0:T(8,128)(2,1)S(1)}, u32[]{:S(2)}, u32[]{:S(2)}) collective-permute-start(bf16[2,16,16,640]{3,2,1,0:T(8,128)(2,1)S(1)} %pad_maximum_fusion.refs_0_), channel_id=1, source_target_pairs={{0,1},{1,2},{2,3},{3,0},{4,5},{5,6},{6,7},{7,4},{8,9},{9,10},{10,1... | collective-permute-start | bytes 1966088 | tf_op jit(solution)/shard_map/ppermute | solution.py:32
  83.0 13.3 %collective-permute-start.7 = (bf16[2,16,16,640]{3,2,1,0:T(8,128)(2,1)S(1)}, bf16[2,16,16,640]{3,2,1,0:T(8,128)(2,1)S(1)}, u32[]{:S(2)}, u32[]{:S(2)}) collective-permute-start(bf16[2,16,16,640]{3,2,1,0:T(8,128)(2,1)S(1)} %pad_maximum_fusion.1.refs_1_), channel_id=1, source_target_pairs={{0,3},{1,0},{2,1},{3,2},{4,7},{5,4},{6,5},{7,6},{8,11},{9,8},{10,9... | collective-permute-start | bytes 1966088 | tf_op jit(solution)/shard_map/ppermute | solution.py:32
  87.0 16.3 %collective-permute-start.6 = (bf16[2,16,16,640]{3,2,1,0:T(8,128)(2,1)S(1)}, bf16[2,16,16,640]{3,2,1,0:T(8,128)(2,1)S(1)}, u32[]{:S(2)}, u32[]{:S(2)}) collective-permute-start(bf16[2,16,16,640]{3,2,1,0:T(8,128)(2,1)S(1)} %pad_maximum_fusion.refs_0_), channel_id=1, source_target_pairs={{0,3},{1,0},{2,1},{3,2},{4,7},{5,4},{6,5},{7,6},{8,11},{9,8},{10,9... | collective-permute-start | bytes 1966088 | tf_op jit(solution)/shard_map/ppermute | solution.py:32
  89.7 13.6 %collective-permute-start.5 = (bf16[2,16,16,640]{3,2,1,0:T(8,128)(2,1)S(1)}, bf16[2,16,16,640]{3,2,1,0:T(8,128)(2,1)}, u32[]{:S(2)}, u32[]{:S(2)}) collective-permute-start(bf16[2,16,16,640]{3,2,1,0:T(8,128)(2,1)S(1)} %pad_maximum_fusion.1.refs_1_), channel_id=1, source_target_pairs={{0,1},{1,2},{2,3},{3,0},{4,5},{5,6},{6,7},{7,4},{8,9},{9,10},{10,1... | collective-permute-start | bytes 1966088 | tf_op jit(solution)/shard_map/ppermute | solution.py:32
  93.5 16.2 %collective-permute-start.8 = (bf16[2,16,16,640]{3,2,1,0:T(8,128)(2,1)S(1)}, bf16[2,16,16,640]{3,2,1,0:T(8,128)(2,1)}, u32[]{:S(2)}, u32[]{:S(2)}) collective-permute-start(bf16[2,16,16,640]{3,2,1,0:T(8,128)(2,1)S(1)} %collective-permute-done.4.refs_2_), channel_id=1, source_target_pairs={{0,1},{1,2},{2,3},{3,0},{4,5},{5,6},{6,7},{7,4},{8,9},{9,10},{10,1... | collective-permute-start | bytes 1966088 | tf_op jit(solution)/shard_map/ppermute | solution.py:32
  96.3 14.0 %collective-permute-start.9 = (bf16[2,16,16,640]{3,2,1,0:T(8,128)(2,1)S(1)}, bf16[2,16,16,640]{3,2,1,0:T(8,128)(2,1)}, u32[]{:S(2)}, u32[]{:S(2)}) collective-permute-start(bf16[2,16,16,640]{3,2,1,0:T(8,128)(2,1)S(1)} %collective-permute-done.7.refs_5_), channel_id=1, source_target_pairs={{0,3},{1,0},{2,1},{3,2},{4,7},{5,4},{6,5},{7,6},{8,11},{9,8},{10,9... | collective-permute-start | bytes 1966088 | tf_op jit(solution)/shard_map/ppermute | solution.py:32
  124.8 8.9 %collective-permute-start.10 = (f32[16,128]{1,0:T(8,128)S(1)}, f32[16,128]{1,0:T(8,128)S(1)}, u32[]{:S(2)}, u32[]{:S(2)}) collective-permute-start(f32[16,128]{1,0:T(8,128)S(1)} %get-tuple-element.12), channel_id=1, source_target_pairs={{0,16},{16,0},{32,48},{48,32},{64,80},{80,64},{96,112},{112,96},{1... | collective-permute-start | bytes 24584 | tf_op jit(solution)/shard_map/ppermute | solution.py:372
Sparse Core Ops, SparseCore 0:
  10.1 101.4 all-gather.2

commit v3 on v2

--- a/solution.py
+++ b/solution.py
@@ -168,7 +168,7 @@
     rem = (pieces[0].shape[-1] - 4 * MAIN) // 4
     _, chips, tok, width = pieces[0].shape
     held = rows + rows * rem // MAIN
-    groups = 4
+    groups = 1
     ctx = ctx.reshape(chips, 2, 2, rows, tokens)
     return pl.pallas_call(
         gradient_kernel,
@@ -286,66 +286,63 @@
     )(gram_parts, grads)
 
 
-def split_kernel(core_ref, a_ref, b_ref, one_ref, two_ref, ctx_ref, keep_ref, give_ref):
-    rows = a_ref.shape[0]
-    cols = rows // 2
-    rem = cols - MAIN
-    ctx_ref[:rows] = a_ref[...]
-    ctx_ref[rows:] = b_ref[...]
-
-    def fill(out_ref, core):
-        for layer, ref in enumerate((one_ref, two_ref)):
-            at = core * cols
-            out_ref[layer * MAIN : (layer + 1) * MAIN] = ref[at : at + MAIN]
-            to = 2 * MAIN + layer * rem
-            out_ref[to : to + rem] = ref[at + MAIN : at + cols]
-
+def stack_kernel(one_ref, two_ref, out_ref):
+    rows = one_ref.shape[0]
+    out_ref[:rows] = one_ref[...]
+    out_ref[rows:] = two_ref[...]
+
+
+def stack_contexts(one, two):
+    rows, tokens = one.shape
+    return pl.pallas_call(
+        stack_kernel,
+        in_specs=[pl.BlockSpec(memory_space=pltpu.VMEM)] * 2,
+        out_specs=pl.BlockSpec(memory_space=pltpu.VMEM),
+        out_shape=jax.ShapeDtypeStruct((2 * rows, tokens), one.dtype),
+    )(one, two)
+
+
+def split_kernel(one_ref, two_ref, out_ref):
+    cols = one_ref.shape[0] // 2
+    shards = out_ref.shape[0] // 2
+    both = (one_ref, two_ref)
     for core in range(2):
-
-        @pl.when(core_ref[0] == core)
-        def _():
-            fill(give_ref, 1 - core)
-            fill(keep_ref, core)
-
-
-def split_columns(core, contexts, cotangents):
-    shape, dtype = contexts[0].shape, contexts[0].dtype
+        at = core * cols
+        parts = [ref[at : at + MAIN] for ref in both] + [ref[at + MAIN : at + cols] for ref in both]
+        value = jnp.concatenate(parts, axis=0).T
+        out_ref[core * shards : (core + 1) * shards] = value.reshape((shards,) + out_ref.shape[1:])
+
+
+def split_cotangents(one, two, shards):
+    cols, tokens = one.shape
     return pl.pallas_call(
         split_kernel,
-        in_specs=[pl.BlockSpec(memory_space=pltpu.SMEM)]
-        + [pl.BlockSpec(memory_space=pltpu.VMEM)] * 4,
-        out_specs=[pl.BlockSpec(memory_space=pltpu.VMEM)] * 3,
-        out_shape=[
-            jax.ShapeDtypeStruct((2 * shape[0], shape[1]), dtype),
-            jax.ShapeDtypeStruct(shape, dtype),
-            jax.ShapeDtypeStruct(shape, dtype),
-        ],
-    )(core, *contexts, *cotangents)
-
-
-def join_kernel(core_ref, keep_ref, got_ref, out_ref):
+        in_specs=[pl.BlockSpec(memory_space=pltpu.VMEM)] * 2,
+        out_specs=pl.BlockSpec(memory_space=pltpu.VMEM),
+        out_shape=jax.ShapeDtypeStruct((2 * shards, tokens // shards, cols), one.dtype),
+    )(one, two)
+
+
+def join_kernel(got_ref, out_ref):
+    shards, tok, width = out_ref.shape
     main = 2 * MAIN
-
-    def fill(first, second):
-        parts = [first[:main], second[:main], first[main:], second[main:]]
-        out_ref[...] = jnp.concatenate(parts, axis=0).T
-
-    for core, (first, second) in enumerate(((keep_ref, got_ref), (got_ref, keep_ref))):
-
-        @pl.when(core_ref[0] == core)
-        def _():
-            fill(first, second)
-
-
-def join_columns(core, keep, got):
-    cols, tokens = keep.shape
+    sides = [
+        got_ref[c * shards : (c + 1) * shards].reshape(shards * tok, width // 2) for c in range(2)
+    ]
+    for c in range(2):
+        out_ref[:, :, c * main : (c + 1) * main] = sides[c][:, :main].reshape(shards, tok, main)
+    edges = jnp.concatenate([side[:, main:] for side in sides], axis=1)
+    out_ref[:, :, 2 * main :] = edges.reshape(shards, tok, width - 2 * main)
+
+
+def join_cores(got):
+    both, tok, cols = got.shape
     return pl.pallas_call(
         join_kernel,
-        in_specs=[pl.BlockSpec(memory_space=pltpu.SMEM)]
-        + [pl.BlockSpec(memory_space=pltpu.VMEM)] * 2,
+        in_specs=[pl.BlockSpec(memory_space=pltpu.VMEM)],
         out_specs=pl.BlockSpec(memory_space=pltpu.VMEM),
-        out_shape=jax.ShapeDtypeStruct((tokens, 2 * cols), keep.dtype),
-    )(core, keep, got)
+        out_shape=jax.ShapeDtypeStruct((both // 2, tok, 2 * cols), got.dtype),
+    )(got)
 
 
 def shards(context_one, cotangent_one, context_two, cotangent_two):
@@ -353,25 +350,22 @@
     reps = lax.axis_size("replica")
     n_shards = lax.axis_size("shard")
     cols = feats // 2
-    core = (lax.axis_index("replica") % 2).reshape(1).astype(jnp.int32)
     same_core = [list(range(c, reps, 2)) for c in range(2)]
-
-    ctx, keep, give = split_columns(
-        core, (context_one.T, context_two.T), (cotangent_one.T, cotangent_two.T)
-    )
+    axes = ("replica", "shard")
+    size = 2 * n_shards
+    planes = [list(range(z * size, (z + 1) * size)) for z in range(reps // 2)]
+
+    ctx = stack_contexts(context_one.T, context_two.T)
     ctx = lax.all_gather(ctx, "replica")
-    got = lax.ppermute(give, "replica", [(i, i ^ 1) for i in range(reps)])
-    cot = join_columns(core, keep, got)
-    cot = cot.reshape(n_shards, tokens // n_shards, cot.shape[1])
-    cot = lax.all_to_all(cot, "shard", 0, 0)
+    cot = split_cotangents(cotangent_one.T, cotangent_two.T, n_shards)
+    cot = join_cores(lax.all_to_all(cot, axes, 0, 0, axis_index_groups=planes))
     cot = lax.all_to_all(cot, "replica", 0, 0, axis_index_groups=same_core)
     pieces = gather_pieces(cot, reps)
 
     offsets = piece_offsets(tokens // n_shards)
     grads, gram = gradients(ctx, pieces, offsets, tokens)
-    gram = gram + lax.ppermute(gram, "replica", [(i, i ^ 1) for i in range(reps)])
-    gram = jnp.broadcast_to(gram[None], (n_shards,) + gram.shape)
-    gram = jnp.sum(lax.all_to_all(gram, "shard", 0, 0), axis=0)
+    gram = jnp.broadcast_to(gram[None], (size,) + gram.shape)
+    gram = jnp.sum(lax.all_to_all(gram, axes, 0, 0, axis_index_groups=planes), axis=0)
     gram = jnp.broadcast_to(gram[None], (reps // 2,) + gram.shape)
     gram = lax.all_to_all(gram, "replica", 0, 0, axis_index_groups=same_core)
     one, two = combine(gram, grads, feats, cols, 1.0 / tokens)

time: 174 us -> 175 us (level)
  blocking collectives: 72.7 us -> 88.8 us
  starting transfers between devices: 43.1 us -> 33.8 us
  waiting for transfers between devices: 18.9 us -> 10.6 us
  Pallas kernels: 21.1 us -> 24.8 us
    ppermute x2 -> x0, starting transfers between devices: 16.9 us -> none  [the longest x1 8.79 us: shards(): got = lax.ppermute(give, 'replica', [(i, i ^ 1) for i in range(reps)])]
    all_to_all x2, blocking collectives: 22.9 us -> 39 us  [the longest x1 20.8 us: shards(): cot = join_cores(lax.all_to_all(cot, axes, 0, 0, axis_index_groups=planes))]
    ppermute x9, starting transfers between devices: 26.2 us -> 33.7 us  [move(): lax.ppermute(value, ('replica', 'shard'), plane_moves(reps, stage, d))]
    ppermute x9, waiting for transfers between devices: 15.6 us -> 10.3 us  [move(): lax.ppermute(value, ('replica', 'shard'), plane_moves(reps, stage, d))]
    pallas_call x1, Pallas kernels: 13.2 us -> 15.3 us  [gradients(): pl.pallas_call(gradient_kernel, in_specs=[pl.BlockSpec(memory_space=pltpu...]
    ppermute x2 -> x0, waiting for transfers between devices: 2.02 us -> none  [the longest x1 1.22 us: shards(): got = lax.ppermute(give, 'replica', [(i, i ^ 1) for i in range(reps)])]
    pallas_call x2 -> x3, Pallas kernels: 3.89 us -> 5.46 us  [the longest x1 1.91 us: split_cotangents(): pl.pallas_call(split_kernel, in_specs=[pl.BlockSpec(memory_space=pltpu.VM...]
  transfers between devices with their start and end apart: 12 -> 10, of which waited for: 10 -> 6; matrix products, arithmetic and copies ran while one was open for 1% -> 1% of each run, Pallas kernels for 1% -> 2%
where the time goes in v3:
time: 175 us; the launch traced here: 173 us
  blocking collectives  88.8 us (51%)
  starting transfers between devices  33.8 us (19%)
  Pallas kernels  24.8 us (14%)
  between operations  14.2 us (8%)
  waiting for transfers between devices  10.6 us (6%)
    ppermute x9, starting transfers between devices, move(): lax.ppermute(value, ('replica', 'shard'), plane_moves(reps, stage, d))  33.7 us
    all_to_all x1, blocking collectives, shards(): cot = lax.all_to_all(cot, 'replica', 0, 0, axis_index_groups=same_core)  32.9 us
    all_to_all x1, blocking collectives, shards(): cot = join_cores(lax.all_to_all(cot, axes, 0, 0, axis_index_groups=planes))  20.8 us
    all_to_all x1, blocking collectives, shards(): lax.all_to_all(gram, axes, 0, 0, axis_index_groups=planes)  18.2 us
    all_to_all x1, blocking collectives, shards(): gram = lax.all_to_all(gram, 'replica', 0, 0, axis_index_groups=same_core)  16.8 us
    pallas_call x1, Pallas kernels, gradients(): pl.pallas_call(gradient_kernel, in_specs=[pl.BlockSpec(memory_space=pltpu...  15.3 us
    ppermute x9, waiting for transfers between devices, move(): lax.ppermute(value, ('replica', 'shard'), plane_moves(reps, stage, d))  10.3 us
    pallas_call x1, Pallas kernels, combine(): pl.pallas_call(functools.partial(combine_kernel, scale), in_specs=[pl.Blo...  3.97 us
  transfers between devices with their start and end apart: 10, of which 6 were waited for; matrix products, arithmetic and copies ran while one was open for 1% of the time, Pallas kernels for 2%

profile of v3, /device:TPU:1, one launch (start us, length us, event | category | flops | bytes accessed | tf_op | source)
XLA Modules:
  0.0 173.2 jit_solution(6224696166614040364)
XLA Ops:
  7.2 0.0 all-gather.3.cloned.1.call-start
  7.2 1.7 %shard_map.68 = bf16[640,256]{1,0:T(8,128)(2,1)} custom-call(bf16[320,256]{1,0:T(8,128)(2,1)} %bitcast.16, bf16[320,256]{1,0:T(8,128)(2,1)} %bitcast.17), custom_call_target="tpu_custom_call" | custom-call | tf_op jit(solution)/shard_map/pallas_call | solution.py:297
  9.0 0.0 all-gather.3.cloned.1.call-update
  9.0 1.9 %shard_map.69 = bf16[32,16,320]{2,1,0:T(8,128)(2,1)} custom-call(bf16[320,256]{1,0:T(8,128)(2,1)} %bitcast.18, bf16[320,256]{1,0:T(8,128)(2,1)} %bitcast.19), custom_call_target="tpu_custom_call" | custom-call | tf_op jit(solution)/shard_map/pallas_call | solution.py:318
  10.9 20.8 %all_to_all.20.got_ref = bf16[32,16,320]{2,1,0:T(8,128)(2,1)} all-to-all(bf16[32,16,320]{2,1,0:T(8,128)(2,1)} %shard_map.69), channel_id=1, replica_groups={{0,1,2,3,4,5,6,7,8,9,10,11,12,13,14,15,16,17,18,19,20,21,22,23,24,25,26..., dimensions={0} | all-to-all | bytes 655360 | tf_op jit(solution)/shard_map/all_to_all | solution.py:361
  31.7 1.8 %shard_map.70 = bf16[16,16,640]{2,1,0:T(8,128)(2,1)} custom-call(bf16[32,16,320]{2,1,0:T(8,128)(2,1)} %all_to_all.20.got_ref), custom_call_target="tpu_custom_call" | custom-call | tf_op jit(solution)/shard_map/pallas_call | solution.py:340
  33.5 32.9 %all_to_all.21 = bf16[16,16,640]{2,1,0:T(8,128)(2,1)S(1)} all-to-all(bf16[16,16,640]{2,1,0:T(8,128)(2,1)} %shard_map.70), channel_id=1, replica_groups={{0,32,64,96,128,160,192,224,256,288,320,352,384,416,448,480},{16,48,80,..., dimensions={0} | all-to-all | bytes 655360 | tf_op jit(solution)/shard_map/all_to_all | solution.py:362
  66.5 2.8 %collective-permute-start = (bf16[16,16,640]{2,1,0:T(8,128)(2,1)S(1)}, bf16[16,16,640]{2,1,0:T(8,128)(2,1)S(1)}, u32[]{:S(2)}, u32[]{:S(2)}) collective-permute-start(bf16[16,16,640]{2,1,0:T(8,128)(2,1)S(1)} %all_to_all.21), channel_id=1, source_target_pairs={{0,4},{1,5},{2,6},{3,7},{4,8},{5,9},{6,10},{7,11},{8,12},{9,13},{1... | collective-permute-start | bytes 983048 | tf_op jit(solution)/shard_map/ppermute | solution.py:32
  69.2 5.7 %collective-permute-start.2 = (bf16[16,16,640]{2,1,0:T(8,128)(2,1)S(1)}, bf16[16,16,640]{2,1,0:T(8,128)(2,1)S(1)}, u32[]{:S(2)}, u32[]{:S(2)}) collective-permute-start(bf16[16,16,640]{2,1,0:T(8,128)(2,1)S(1)} %all_to_all.21), channel_id=1, source_target_pairs={{0,8},{1,9},{2,10},{3,11},{4,12},{5,13},{6,14},{7,15},{8,0},{9,1},... | collective-permute-start | bytes 983048 | tf_op jit(solution)/shard_map/ppermute | solution.py:32
  74.9 4.0 %collective-permute-start.1 = (bf16[16,16,640]{2,1,0:T(8,128)(2,1)S(1)}, bf16[16,16,640]{2,1,0:T(8,128)(2,1)S(1)}, u32[]{:S(2)}, u32[]{:S(2)}) collective-permute-start(bf16[16,16,640]{2,1,0:T(8,128)(2,1)S(1)} %all_to_all.21), channel_id=1, source_target_pairs={{0,12},{1,13},{2,14},{3,15},{4,0},{5,1},{6,2},{7,3},{8,4},{9,5},{1... | collective-permute-start | bytes 983048 | tf_op jit(solution)/shard_map/ppermute | solution.py:32
  78.9 0.0 collective-permute-done
  78.9 0.1 pad_maximum_fusion.refs_0_
  79.0 3.4 %collective-permute-start.3 = (bf16[2,16,16,640]{3,2,1,0:T(8,128)(2,1)S(1)}, bf16[2,16,16,640]{3,2,1,0:T(8,128)(2,1)S(1)}, u32[]{:S(2)}, u32[]{:S(2)}) collective-permute-start(bf16[2,16,16,640]{3,2,1,0:T(8,128)(2,1)S(1)} %pad_maximum_fusion.refs_0_), channel_id=1, source_target_pairs={{0,1},{1,2},{2,3},{3,0},{4,5},{5,6},{6,7},{7,4},{8,9},{9,10},{10,1... | collective-permute-start | bytes 1966088 | tf_op jit(solution)/shard_map/ppermute | solution.py:32
  82.4 0.0 collective-permute-done.2
  82.5 0.7 collective-permute-done.1
  83.2 0.1 pad_maximum_fusion.1.refs_1_
  83.2 5.5 %collective-permute-start.6 = (bf16[2,16,16,640]{3,2,1,0:T(8,128)(2,1)S(1)}, bf16[2,16,16,640]{3,2,1,0:T(8,128)(2,1)S(1)}, u32[]{:S(2)}, u32[]{:S(2)}) collective-permute-start(bf16[2,16,16,640]{3,2,1,0:T(8,128)(2,1)S(1)} %pad_maximum_fusion.1.refs_1_), channel_id=1, source_target_pairs={{0,3},{1,0},{2,1},{3,2},{4,7},{5,4},{6,5},{7,6},{8,11},{9,8},{10,9... | collective-permute-start | bytes 1966088 | tf_op jit(solution)/shard_map/ppermute | solution.py:32
  88.7 2.9 %collective-permute-start.5 = (bf16[2,16,16,640]{3,2,1,0:T(8,128)(2,1)S(1)}, bf16[2,16,16,640]{3,2,1,0:T(8,128)(2,1)S(1)}, u32[]{:S(2)}, u32[]{:S(2)}) collective-permute-start(bf16[2,16,16,640]{3,2,1,0:T(8,128)(2,1)S(1)} %pad_maximum_fusion.refs_0_), channel_id=1, source_target_pairs={{0,3},{1,0},{2,1},{3,2},{4,7},{5,4},{6,5},{7,6},{8,11},{9,8},{10,9... | collective-permute-start | bytes 1966088 | tf_op jit(solution)/shard_map/ppermute | solution.py:32
  91.6 2.4 %collective-permute-start.4 = (bf16[2,16,16,640]{3,2,1,0:T(8,128)(2,1)S(1)}, bf16[2,16,16,640]{3,2,1,0:T(8,128)(2,1)}, u32[]{:S(2)}, u32[]{:S(2)}) collective-permute-start(bf16[2,16,16,640]{3,2,1,0:T(8,128)(2,1)S(1)} %pad_maximum_fusion.1.refs_1_), channel_id=1, source_target_pairs={{0,1},{1,2},{2,3},{3,0},{4,5},{5,6},{6,7},{7,4},{8,9},{9,10},{10,1... | collective-permute-start | bytes 1966088 | tf_op jit(solution)/shard_map/ppermute | solution.py:32
  94.0 0.5 collective-permute-done.3.refs_2_
  94.6 1.9 %collective-permute-start.7 = (bf16[2,16,16,640]{3,2,1,0:T(8,128)(2,1)S(1)}, bf16[2,16,16,640]{3,2,1,0:T(8,128)(2,1)}, u32[]{:S(2)}, u32[]{:S(2)}) collective-permute-start(bf16[2,16,16,640]{3,2,1,0:T(8,128)(2,1)S(1)} %collective-permute-done.3.refs_2_), channel_id=1, source_target_pairs={{0,1},{1,2},{2,3},{3,0},{4,5},{5,6},{6,7},{7,4},{8,9},{9,10},{10,1... | collective-permute-start | bytes 1966088 | tf_op jit(solution)/shard_map/ppermute | solution.py:32
  96.5 0.0 collective-permute-done.6.refs_5_
  96.5 5.2 %collective-permute-start.8 = (bf16[2,16,16,640]{3,2,1,0:T(8,128)(2,1)S(1)}, bf16[2,16,16,640]{3,2,1,0:T(8,128)(2,1)}, u32[]{:S(2)}, u32[]{:S(2)}) collective-permute-start(bf16[2,16,16,640]{3,2,1,0:T(8,128)(2,1)S(1)} %collective-permute-done.6.refs_5_), channel_id=1, source_target_pairs={{0,3},{1,0},{2,1},{3,2},{4,7},{5,4},{6,5},{7,6},{8,11},{9,8},{10,9... | collective-permute-start | bytes 1966088 | tf_op jit(solution)/shard_map/ppermute | solution.py:32
  101.7 0.7 fusion.1
  102.4 0.1 select_multiply_fusion
  102.5 0.1 mul.15.off_ref
  102.5 0.7 collective-permute-done.5.refs_4_
  103.3 1.3 collective-permute-done.4.refs_3_
  104.5 7.0 %collective-permute-done.7.refs_6_ = bf16[2,16,16,640]{3,2,1,0:T(8,128)(2,1)} collective-permute-done((bf16[2,16,16,640]{3,2,1,0:T(8,128)(2,1)S(1)}, bf16[2,16,16,640]{3,2,1,0:T(8,128)(2,1)}, u32[]{:S(2)}, u32[]{:S(2)}) %collective-permute-start.7) | collective-permute-done | bytes 655392 | tf_op jit(solution)/shard_map/ppermute | solution.py:32
  111.6 0.0 collective-permute-done.8.refs_7_
  111.6 0.3 all-gather.3.cloned.1.call-done
  111.9 15.3 %shard_map.71 = (bf16[2,32,400,128]{3,2,1,0:T(8,128)(2,1)}, f32[16,128]{1,0:T(8,128)S(1)}) custom-call(s32[16]{0:T(128)S(1)} %mul.15.off_ref, bf16[16,2,2,320,256]{4,3,2,1,0:T(8,128)(2,1)} %bitcast.11, bf16[2,16,16,640]{3,2,1,0:T(8,128)(2,1)S(1)} %pad_maximum_fusion.refs_0_, bf16[2,16,16,640]{3,2,1,0:T(8,128)(2,1)S(1)} %pad_maximum_fusion.1.refs_1_, ...), custom_call_target="tpu_custom_call" | custom-call | tf_op jit(solution)/shard_map/pallas_call | solution.py:173
  127.3 18.2 %all_to_all.22 = f32[32,16,128]{2,1,0:T(8,128)S(1)} all-to-all(f32[32,16,128]{2,1,0:T(8,128)S(1)} %broadcast_in_dim.4), channel_id=1, replica_groups={{0,1,2,3,4,5,6,7,8,9,10,11,12,13,14,15,16,17,18,19,20,21,22,23,24,25,26..., dimensions={0} | all-to-all | bytes 524288 | tf_op jit(solution)/shard_map/all_to_all | solution.py:368
  145.5 16.8 %all_to_all.23.gram_ref = f32[16,16,128]{2,1,0:T(8,128)S(1)} all-to-all(f32[16,16,128]{2,1,0:T(8,128)S(1)} %broadcast_in_dim.5), channel_id=1, replica_groups={{0,32,64,96,128,160,192,224,256,288,320,352,384,416,448,480},{16,48,80,..., dimensions={0} | all-to-all | bytes 262144 | tf_op jit(solution)/shard_map/all_to_all | solution.py:370
  162.3 4.0 %shard_map.72 = (f32[160,320]{1,0:T(8,128)}, f32[160,320]{1,0:T(8,128)}) custom-call(f32[16,16,128]{2,1,0:T(8,128)S(1)} %all_to_all.23.gram_ref, bf16[2,32,400,128]{3,2,1,0:T(8,128)(2,1)} %get-tuple-element.7.grad_hbm), custom_call_target="tpu_custom_call" | custom-call | tf_op jit(solution)/shard_map/pallas_call | solution.py:272
  (3 shorter events, 0.1 us)
Async XLA Ops:
  7.2 104.7 %all-gather.3.cloned.1.call-start = ((), (), s32[]{:S(2)}) async-start(), calls=%async_computation.4 | async-start | bytes 10813440 | tf_op jit(solution)/shard_map/all_gather | solution.py:359
  66.5 12.5 %collective-permute-start = (bf16[16,16,640]{2,1,0:T(8,128)(2,1)S(1)}, bf16[16,16,640]{2,1,0:T(8,128)(2,1)S(1)}, u32[]{:S(2)}, u32[]{:S(2)}) collective-permute-start(bf16[16,16,640]{2,1,0:T(8,128)(2,1)S(1)} %all_to_all.21), channel_id=1, source_target_pairs={{0,4},{1,5},{2,6},{3,7},{4,8},{5,9},{6,10},{7,11},{8,12},{9,13},{1... | collective-permute-start | bytes 983048 | tf_op jit(solution)/shard_map/ppermute | solution.py:32
  69.2 13.2 %collective-permute-start.2 = (bf16[16,16,640]{2,1,0:T(8,128)(2,1)S(1)}, bf16[16,16,640]{2,1,0:T(8,128)(2,1)S(1)}, u32[]{:S(2)}, u32[]{:S(2)}) collective-permute-start(bf16[16,16,640]{2,1,0:T(8,128)(2,1)S(1)} %all_to_all.21), channel_id=1, source_target_pairs={{0,8},{1,9},{2,10},{3,11},{4,12},{5,13},{6,14},{7,15},{8,0},{9,1},... | collective-permute-start | bytes 983048 | tf_op jit(solution)/shard_map/ppermute | solution.py:32
  74.9 8.2 %collective-permute-start.1 = (bf16[16,16,640]{2,1,0:T(8,128)(2,1)S(1)}, bf16[16,16,640]{2,1,0:T(8,128)(2,1)S(1)}, u32[]{:S(2)}, u32[]{:S(2)}) collective-permute-start(bf16[16,16,640]{2,1,0:T(8,128)(2,1)S(1)} %all_to_all.21), channel_id=1, source_target_pairs={{0,12},{1,13},{2,14},{3,15},{4,0},{5,1},{6,2},{7,3},{8,4},{9,5},{1... | collective-permute-start | bytes 983048 | tf_op jit(solution)/shard_map/ppermute | solution.py:32
  79.0 15.6 %collective-permute-start.3 = (bf16[2,16,16,640]{3,2,1,0:T(8,128)(2,1)S(1)}, bf16[2,16,16,640]{3,2,1,0:T(8,128)(2,1)S(1)}, u32[]{:S(2)}, u32[]{:S(2)}) collective-permute-start(bf16[2,16,16,640]{3,2,1,0:T(8,128)(2,1)S(1)} %pad_maximum_fusion.refs_0_), channel_id=1, source_target_pairs={{0,1},{1,2},{2,3},{3,0},{4,5},{5,6},{6,7},{7,4},{8,9},{9,10},{10,1... | collective-permute-start | bytes 1966088 | tf_op jit(solution)/shard_map/ppermute | solution.py:32
  83.2 13.3 %collective-permute-start.6 = (bf16[2,16,16,640]{3,2,1,0:T(8,128)(2,1)S(1)}, bf16[2,16,16,640]{3,2,1,0:T(8,128)(2,1)S(1)}, u32[]{:S(2)}, u32[]{:S(2)}) collective-permute-start(bf16[2,16,16,640]{3,2,1,0:T(8,128)(2,1)S(1)} %pad_maximum_fusion.1.refs_1_), channel_id=1, source_target_pairs={{0,3},{1,0},{2,1},{3,2},{4,7},{5,4},{6,5},{7,6},{8,11},{9,8},{10,9... | collective-permute-start | bytes 1966088 | tf_op jit(solution)/shard_map/ppermute | solution.py:32
  88.7 14.5 %collective-permute-start.5 = (bf16[2,16,16,640]{3,2,1,0:T(8,128)(2,1)S(1)}, bf16[2,16,16,640]{3,2,1,0:T(8,128)(2,1)S(1)}, u32[]{:S(2)}, u32[]{:S(2)}) collective-permute-start(bf16[2,16,16,640]{3,2,1,0:T(8,128)(2,1)S(1)} %pad_maximum_fusion.refs_0_), channel_id=1, source_target_pairs={{0,3},{1,0},{2,1},{3,2},{4,7},{5,4},{6,5},{7,6},{8,11},{9,8},{10,9... | collective-permute-start | bytes 1966088 | tf_op jit(solution)/shard_map/ppermute | solution.py:32
  91.6 12.9 %collective-permute-start.4 = (bf16[2,16,16,640]{3,2,1,0:T(8,128)(2,1)S(1)}, bf16[2,16,16,640]{3,2,1,0:T(8,128)(2,1)}, u32[]{:S(2)}, u32[]{:S(2)}) collective-permute-start(bf16[2,16,16,640]{3,2,1,0:T(8,128)(2,1)S(1)} %pad_maximum_fusion.1.refs_1_), channel_id=1, source_target_pairs={{0,1},{1,2},{2,3},{3,0},{4,5},{5,6},{6,7},{7,4},{8,9},{9,10},{10,1... | collective-permute-start | bytes 1966088 | tf_op jit(solution)/shard_map/ppermute | solution.py:32
  94.6 17.0 %collective-permute-start.7 = (bf16[2,16,16,640]{3,2,1,0:T(8,128)(2,1)S(1)}, bf16[2,16,16,640]{3,2,1,0:T(8,128)(2,1)}, u32[]{:S(2)}, u32[]{:S(2)}) collective-permute-start(bf16[2,16,16,640]{3,2,1,0:T(8,128)(2,1)S(1)} %collective-permute-done.3.refs_2_), channel_id=1, source_target_pairs={{0,1},{1,2},{2,3},{3,0},{4,5},{5,6},{6,7},{7,4},{8,9},{9,10},{10,1... | collective-permute-start | bytes 1966088 | tf_op jit(solution)/shard_map/ppermute | solution.py:32
  96.5 15.1 %collective-permute-start.8 = (bf16[2,16,16,640]{3,2,1,0:T(8,128)(2,1)S(1)}, bf16[2,16,16,640]{3,2,1,0:T(8,128)(2,1)}, u32[]{:S(2)}, u32[]{:S(2)}) collective-permute-start(bf16[2,16,16,640]{3,2,1,0:T(8,128)(2,1)S(1)} %collective-permute-done.6.refs_5_), channel_id=1, source_target_pairs={{0,3},{1,0},{2,1},{3,2},{4,7},{5,4},{6,5},{7,6},{8,11},{9,8},{10,9... | collective-permute-start | bytes 1966088 | tf_op jit(solution)/shard_map/ppermute | solution.py:32
Sparse Core Ops, SparseCore 0:
  10.1 101.7 all-gather.2

commit v4 on v3

--- a/solution.py
+++ b/solution.py
@@ -168,7 +168,7 @@
     rem = (pieces[0].shape[-1] - 4 * MAIN) // 4
     _, chips, tok, width = pieces[0].shape
     held = rows + rows * rem // MAIN
-    groups = 1
+    groups = 4
     ctx = ctx.reshape(chips, 2, 2, rows, tokens)
     return pl.pallas_call(
         gradient_kernel,
@@ -286,25 +286,12 @@
     )(gram_parts, grads)
 
 
-def stack_kernel(one_ref, two_ref, out_ref):
-    rows = one_ref.shape[0]
-    out_ref[:rows] = one_ref[...]
-    out_ref[rows:] = two_ref[...]
-
-
-def stack_contexts(one, two):
-    rows, tokens = one.shape
-    return pl.pallas_call(
-        stack_kernel,
-        in_specs=[pl.BlockSpec(memory_space=pltpu.VMEM)] * 2,
-        out_specs=pl.BlockSpec(memory_space=pltpu.VMEM),
-        out_shape=jax.ShapeDtypeStruct((2 * rows, tokens), one.dtype),
-    )(one, two)
-
-
-def split_kernel(one_ref, two_ref, out_ref):
-    cols = one_ref.shape[0] // 2
+def split_kernel(a_ref, b_ref, one_ref, two_ref, ctx_ref, out_ref):
+    rows = a_ref.shape[0]
+    cols = rows // 2
     shards = out_ref.shape[0] // 2
+    ctx_ref[:rows] = a_ref[...]
+    ctx_ref[rows:] = b_ref[...]
     both = (one_ref, two_ref)
     for core in range(2):
         at = core * cols
@@ -313,14 +300,18 @@
         out_ref[core * shards : (core + 1) * shards] = value.reshape((shards,) + out_ref.shape[1:])
 
 
-def split_cotangents(one, two, shards):
-    cols, tokens = one.shape
+def split_arguments(contexts, cotangents, shards):
+    cols, tokens = contexts[0].shape
+    dtype = contexts[0].dtype
     return pl.pallas_call(
         split_kernel,
-        in_specs=[pl.BlockSpec(memory_space=pltpu.VMEM)] * 2,
-        out_specs=pl.BlockSpec(memory_space=pltpu.VMEM),
-        out_shape=jax.ShapeDtypeStruct((2 * shards, tokens // shards, cols), one.dtype),
-    )(one, two)
+        in_specs=[pl.BlockSpec(memory_space=pltpu.VMEM)] * 4,
+        out_specs=[pl.BlockSpec(memory_space=pltpu.VMEM)] * 2,
+        out_shape=[
+            jax.ShapeDtypeStruct((2 * cols, tokens), dtype),
+            jax.ShapeDtypeStruct((2 * shards, tokens // shards, cols), dtype),
+        ],
+    )(*contexts, *cotangents)
 
 
 def join_kernel(got_ref, out_ref):
@@ -355,9 +346,10 @@
     size = 2 * n_shards
     planes = [list(range(z * size, (z + 1) * size)) for z in range(reps // 2)]
 
-    ctx = stack_contexts(context_one.T, context_two.T)
+    ctx, cot = split_arguments(
+        (context_one.T, context_two.T), (cotangent_one.T, cotangent_two.T), n_shards
+    )
     ctx = lax.all_gather(ctx, "replica")
-    cot = split_cotangents(cotangent_one.T, cotangent_two.T, n_shards)
     cot = join_cores(lax.all_to_all(cot, axes, 0, 0, axis_index_groups=planes))
     cot = lax.all_to_all(cot, "replica", 0, 0, axis_index_groups=same_core)
     pieces = gather_pieces(cot, reps)

time: 175 us -> 172 us (0.983)
  waiting for transfers between devices: 10.6 us -> 17.2 us
  starting transfers between devices: 33.8 us -> 27.9 us
  Pallas kernels: 24.8 us -> 21.2 us
    ppermute x9, starting transfers between devices: 33.7 us -> 27.9 us  [move(): lax.ppermute(value, ('replica', 'shard'), plane_moves(reps, stage, d))]
    ppermute x9, waiting for transfers between devices: 10.3 us -> 13.8 us  [move(): lax.ppermute(value, ('replica', 'shard'), plane_moves(reps, stage, d))]
    all_gather x1, waiting for transfers between devices: 0.32 us -> 3.34 us  [shards(): ctx = lax.all_gather(ctx, 'replica')]
    pallas_call x1, Pallas kernels: 15.3 us -> 13.2 us  [gradients(): pl.pallas_call(gradient_kernel, in_specs=[pl.BlockSpec(memory_space=pltpu...]
    pallas_call x2 -> x1, Pallas kernels: 3.65 us -> 2.17 us  [split_arguments(): pl.pallas_call(split_kernel, in_specs=[pl.BlockSpec(memory_space=pltpu.VM...]
  transfers between devices with their start and end apart: 10 -> 10, of which waited for: 6 -> 8; matrix products, arithmetic and copies ran while one was open for 1% -> 1% of each run, Pallas kernels for 2% -> 1%
where the time goes in v4:
time: 172 us; the launch traced here: 170 us
  blocking collectives  88 us (51%)
  starting transfers between devices  27.9 us (16%)
  Pallas kernels  21.2 us (12%)
  waiting for transfers between devices  17.2 us (10%)
  between operations  14.2 us (8%)
    all_to_all x1, blocking collectives, shards(): cot = lax.all_to_all(cot, 'replica', 0, 0, axis_index_groups=same_core)  33.3 us
    ppermute x9, starting transfers between devices, move(): lax.ppermute(value, ('replica', 'shard'), plane_moves(reps, stage, d))  27.9 us
    all_to_all x1, blocking collectives, shards(): cot = join_cores(lax.all_to_all(cot, axes, 0, 0, axis_index_groups=planes))  20.8 us
    all_to_all x1, blocking collectives, shards(): gram = lax.all_to_all(gram, 'replica', 0, 0, axis_index_groups=same_core)  17.1 us
    all_to_all x1, blocking collectives, shards(): lax.all_to_all(gram, axes, 0, 0, axis_index_groups=planes)  16.8 us
    ppermute x9, waiting for transfers between devices, move(): lax.ppermute(value, ('replica', 'shard'), plane_moves(reps, stage, d))  13.8 us
    pallas_call x1, Pallas kernels, gradients(): pl.pallas_call(gradient_kernel, in_specs=[pl.BlockSpec(memory_space=pltpu...  13.2 us
    pallas_call x1, Pallas kernels, combine(): pl.pallas_call(functools.partial(combine_kernel, scale), in_specs=[pl.Blo...  3.97 us
  transfers between devices with their start and end apart: 10, of which 8 were waited for; matrix products, arithmetic and copies ran while one was open for 1% of the time, Pallas kernels for 1%

profile of v4, /device:TPU:1, one launch (start us, length us, event | category | flops | bytes accessed | tf_op | source)
XLA Modules:
  0.0 169.5 jit_solution(14505644885121899253)
XLA Ops:
  7.2 0.0 all-gather.3.cloned.1.call-start
  7.2 2.2 %shard_map.68 = (bf16[640,256]{1,0:T(8,128)(2,1)}, bf16[32,16,320]{2,1,0:T(8,128)(2,1)}) custom-call(bf16[320,256]{1,0:T(8,128)(2,1)} %bitcast.16, bf16[320,256]{1,0:T(8,128)(2,1)} %bitcast.17, bf16[320,256]{1,0:T(8,128)(2,1)} %bitcast.18, bf16[320,256]{1,0:T(8,128)(2,1)} %bitcast.19), custom_call_target="tpu_custom_call" | custom-call | tf_op jit(solution)/shard_map/pallas_call | solution.py:306
  9.4 0.0 all-gather.3.cloned.1.call-update
  9.4 20.8 %all_to_all.20.got_ref = bf16[32,16,320]{2,1,0:T(8,128)(2,1)} all-to-all(bf16[32,16,320]{2,1,0:T(8,128)(2,1)} %get-tuple-element.9), channel_id=1, replica_groups={{0,1,2,3,4,5,6,7,8,9,10,11,12,13,14,15,16,17,18,19,20,21,22,23,24,25,26..., dimensions={0} | all-to-all | bytes 655360 | tf_op jit(solution)/shard_map/all_to_all | solution.py:353
  30.2 1.8 %shard_map.69 = bf16[16,16,640]{2,1,0:T(8,128)(2,1)} custom-call(bf16[32,16,320]{2,1,0:T(8,128)(2,1)} %all_to_all.20.got_ref), custom_call_target="tpu_custom_call" | custom-call | tf_op jit(solution)/shard_map/pallas_call | solution.py:331
  32.1 33.3 %all_to_all.21 = bf16[16,16,640]{2,1,0:T(8,128)(2,1)S(1)} all-to-all(bf16[16,16,640]{2,1,0:T(8,128)(2,1)} %shard_map.69), channel_id=1, replica_groups={{0,32,64,96,128,160,192,224,256,288,320,352,384,416,448,480},{16,48,80,..., dimensions={0} | all-to-all | bytes 655360 | tf_op jit(solution)/shard_map/all_to_all | solution.py:354
  65.4 2.4 %collective-permute-start = (bf16[16,16,640]{2,1,0:T(8,128)(2,1)S(1)}, bf16[16,16,640]{2,1,0:T(8,128)(2,1)S(1)}, u32[]{:S(2)}, u32[]{:S(2)}) collective-permute-start(bf16[16,16,640]{2,1,0:T(8,128)(2,1)S(1)} %all_to_all.21), channel_id=1, source_target_pairs={{0,4},{1,5},{2,6},{3,7},{4,8},{5,9},{6,10},{7,11},{8,12},{9,13},{1... | collective-permute-start | bytes 983048 | tf_op jit(solution)/shard_map/ppermute | solution.py:32
  67.8 4.3 %collective-permute-start.2 = (bf16[16,16,640]{2,1,0:T(8,128)(2,1)S(1)}, bf16[16,16,640]{2,1,0:T(8,128)(2,1)S(1)}, u32[]{:S(2)}, u32[]{:S(2)}) collective-permute-start(bf16[16,16,640]{2,1,0:T(8,128)(2,1)S(1)} %all_to_all.21), channel_id=1, source_target_pairs={{0,8},{1,9},{2,10},{3,11},{4,12},{5,13},{6,14},{7,15},{8,0},{9,1},... | collective-permute-start | bytes 983048 | tf_op jit(solution)/shard_map/ppermute | solution.py:32
  72.1 3.3 %collective-permute-start.1 = (bf16[16,16,640]{2,1,0:T(8,128)(2,1)S(1)}, bf16[16,16,640]{2,1,0:T(8,128)(2,1)S(1)}, u32[]{:S(2)}, u32[]{:S(2)}) collective-permute-start(bf16[16,16,640]{2,1,0:T(8,128)(2,1)S(1)} %all_to_all.21), channel_id=1, source_target_pairs={{0,12},{1,13},{2,14},{3,15},{4,0},{5,1},{6,2},{7,3},{8,4},{9,5},{1... | collective-permute-start | bytes 983048 | tf_op jit(solution)/shard_map/ppermute | solution.py:32
  75.5 0.0 collective-permute-done
  75.5 0.1 pad_maximum_fusion.refs_0_
  75.6 1.9 %collective-permute-start.3 = (bf16[2,16,16,640]{3,2,1,0:T(8,128)(2,1)S(1)}, bf16[2,16,16,640]{3,2,1,0:T(8,128)(2,1)S(1)}, u32[]{:S(2)}, u32[]{:S(2)}) collective-permute-start(bf16[2,16,16,640]{3,2,1,0:T(8,128)(2,1)S(1)} %pad_maximum_fusion.refs_0_), channel_id=1, source_target_pairs={{0,1},{1,2},{2,3},{3,0},{4,5},{5,6},{6,7},{7,4},{8,9},{9,10},{10,1... | collective-permute-start | bytes 1966088 | tf_op jit(solution)/shard_map/ppermute | solution.py:32
  77.5 0.7 collective-permute-done.2
  78.2 2.6 %collective-permute-done.1 = bf16[16,16,640]{2,1,0:T(8,128)(2,1)S(1)} collective-permute-done((bf16[16,16,640]{2,1,0:T(8,128)(2,1)S(1)}, bf16[16,16,640]{2,1,0:T(8,128)(2,1)S(1)}, u32[]{:S(2)}, u32[]{:S(2)}) %collective-permute-start.1) | collective-permute-done | bytes 327712 | tf_op jit(solution)/shard_map/ppermute | solution.py:32
  80.8 0.1 pad_maximum_fusion.1.refs_1_
  80.9 4.4 %collective-permute-start.6 = (bf16[2,16,16,640]{3,2,1,0:T(8,128)(2,1)S(1)}, bf16[2,16,16,640]{3,2,1,0:T(8,128)(2,1)S(1)}, u32[]{:S(2)}, u32[]{:S(2)}) collective-permute-start(bf16[2,16,16,640]{3,2,1,0:T(8,128)(2,1)S(1)} %pad_maximum_fusion.1.refs_1_), channel_id=1, source_target_pairs={{0,3},{1,0},{2,1},{3,2},{4,7},{5,4},{6,5},{7,6},{8,11},{9,8},{10,9... | collective-permute-start | bytes 1966088 | tf_op jit(solution)/shard_map/ppermute | solution.py:32
  85.3 2.9 %collective-permute-start.5 = (bf16[2,16,16,640]{3,2,1,0:T(8,128)(2,1)S(1)}, bf16[2,16,16,640]{3,2,1,0:T(8,128)(2,1)S(1)}, u32[]{:S(2)}, u32[]{:S(2)}) collective-permute-start(bf16[2,16,16,640]{3,2,1,0:T(8,128)(2,1)S(1)} %pad_maximum_fusion.refs_0_), channel_id=1, source_target_pairs={{0,3},{1,0},{2,1},{3,2},{4,7},{5,4},{6,5},{7,6},{8,11},{9,8},{10,9... | collective-permute-start | bytes 1966088 | tf_op jit(solution)/shard_map/ppermute | solution.py:32
  88.2 2.4 %collective-permute-start.4 = (bf16[2,16,16,640]{3,2,1,0:T(8,128)(2,1)S(1)}, bf16[2,16,16,640]{3,2,1,0:T(8,128)(2,1)}, u32[]{:S(2)}, u32[]{:S(2)}) collective-permute-start(bf16[2,16,16,640]{3,2,1,0:T(8,128)(2,1)S(1)} %pad_maximum_fusion.1.refs_1_), channel_id=1, source_target_pairs={{0,1},{1,2},{2,3},{3,0},{4,5},{5,6},{6,7},{7,4},{8,9},{9,10},{10,1... | collective-permute-start | bytes 1966088 | tf_op jit(solution)/shard_map/ppermute | solution.py:32
  90.6 0.6 collective-permute-done.3.refs_2_
  91.2 1.9 %collective-permute-start.7 = (bf16[2,16,16,640]{3,2,1,0:T(8,128)(2,1)S(1)}, bf16[2,16,16,640]{3,2,1,0:T(8,128)(2,1)}, u32[]{:S(2)}, u32[]{:S(2)}) collective-permute-start(bf16[2,16,16,640]{3,2,1,0:T(8,128)(2,1)S(1)} %collective-permute-done.3.refs_2_), channel_id=1, source_target_pairs={{0,1},{1,2},{2,3},{3,0},{4,5},{5,6},{6,7},{7,4},{8,9},{9,10},{10,1... | collective-permute-start | bytes 1966088 | tf_op jit(solution)/shard_map/ppermute | solution.py:32
  93.1 0.9 collective-permute-done.6.refs_5_
  93.9 4.3 %collective-permute-start.8 = (bf16[2,16,16,640]{3,2,1,0:T(8,128)(2,1)S(1)}, bf16[2,16,16,640]{3,2,1,0:T(8,128)(2,1)}, u32[]{:S(2)}, u32[]{:S(2)}) collective-permute-start(bf16[2,16,16,640]{3,2,1,0:T(8,128)(2,1)S(1)} %collective-permute-done.6.refs_5_), channel_id=1, source_target_pairs={{0,3},{1,0},{2,1},{3,2},{4,7},{5,4},{6,5},{7,6},{8,11},{9,8},{10,9... | collective-permute-start | bytes 1966088 | tf_op jit(solution)/shard_map/ppermute | solution.py:32
  98.3 0.7 fusion.1
  98.9 0.1 select_multiply_fusion
  99.0 0.1 mul.15.off_ref
  99.1 1.9 %collective-permute-done.5.refs_4_ = bf16[2,16,16,640]{3,2,1,0:T(8,128)(2,1)S(1)} collective-permute-done((bf16[2,16,16,640]{3,2,1,0:T(8,128)(2,1)S(1)}, bf16[2,16,16,640]{3,2,1,0:T(8,128)(2,1)S(1)}, u32[]{:S(2)}, u32[]{:S(2)}) %collective-permute-start.5) | collective-permute-done | bytes 655392 | tf_op jit(solution)/shard_map/ppermute | solution.py:32
  100.9 0.2 collective-permute-done.4.refs_3_
  101.1 7.0 %collective-permute-done.7.refs_6_ = bf16[2,16,16,640]{3,2,1,0:T(8,128)(2,1)} collective-permute-done((bf16[2,16,16,640]{3,2,1,0:T(8,128)(2,1)S(1)}, bf16[2,16,16,640]{3,2,1,0:T(8,128)(2,1)}, u32[]{:S(2)}, u32[]{:S(2)}) %collective-permute-start.7) | collective-permute-done | bytes 655392 | tf_op jit(solution)/shard_map/ppermute | solution.py:32
  108.2 0.0 collective-permute-done.8.refs_7_
  108.2 3.3 %all-gather.3.cloned.1.call-done = bf16[20480,256]{1,0:T(8,128)(2,1)} async-done(((bf16[640,256]{1,0:T(8,128)(2,1)}), bf16[20480,256]{1,0:T(8,128)(2,1)}) %all-gather.3.cloned.1.call-update) | async-done | bytes 10485776 | tf_op jit(solution)/shard_map/all_gather | solution.py:352
  111.5 13.2 %shard_map.70 = (bf16[2,32,400,128]{3,2,1,0:T(8,128)(2,1)}, f32[16,128]{1,0:T(8,128)S(1)}) custom-call(s32[16]{0:T(128)S(1)} %mul.15.off_ref, bf16[16,2,2,320,256]{4,3,2,1,0:T(8,128)(2,1)} %bitcast.11, bf16[2,16,16,640]{3,2,1,0:T(8,128)(2,1)S(1)} %pad_maximum_fusion.refs_0_, bf16[2,16,16,640]{3,2,1,0:T(8,128)(2,1)S(1)} %pad_maximum_fusion.1.refs_1_, ...), custom_call_target="tpu_custom_call" | custom-call | tf_op jit(solution)/shard_map/pallas_call | solution.py:173
  124.7 16.8 %all_to_all.22 = f32[32,16,128]{2,1,0:T(8,128)S(1)} all-to-all(f32[32,16,128]{2,1,0:T(8,128)S(1)} %broadcast_in_dim.4), channel_id=1, replica_groups={{0,1,2,3,4,5,6,7,8,9,10,11,12,13,14,15,16,17,18,19,20,21,22,23,24,25,26..., dimensions={0} | all-to-all | bytes 524288 | tf_op jit(solution)/shard_map/all_to_all | solution.py:360
  141.6 17.1 %all_to_all.23.gram_ref = f32[16,16,128]{2,1,0:T(8,128)S(1)} all-to-all(f32[16,16,128]{2,1,0:T(8,128)S(1)} %broadcast_in_dim.5), channel_id=1, replica_groups={{0,32,64,96,128,160,192,224,256,288,320,352,384,416,448,480},{16,48,80,..., dimensions={0} | all-to-all | bytes 262144 | tf_op jit(solution)/shard_map/all_to_all | solution.py:362
  158.7 4.0 %shard_map.71 = (f32[160,320]{1,0:T(8,128)}, f32[160,320]{1,0:T(8,128)}) custom-call(f32[16,16,128]{2,1,0:T(8,128)S(1)} %all_to_all.23.gram_ref, bf16[2,32,400,128]{3,2,1,0:T(8,128)(2,1)} %get-tuple-element.11.grad_hbm), custom_call_target="tpu_custom_call" | custom-call | tf_op jit(solution)/shard_map/pallas_call | solution.py:272
  (3 shorter events, 0.1 us)
Async XLA Ops:
  7.2 104.3 %all-gather.3.cloned.1.call-start = ((), (), s32[]{:S(2)}) async-start(), calls=%async_computation.4 | async-start | bytes 10813440 | tf_op jit(solution)/shard_map/all_gather | solution.py:352
  65.4 10.1 %collective-permute-start = (bf16[16,16,640]{2,1,0:T(8,128)(2,1)S(1)}, bf16[16,16,640]{2,1,0:T(8,128)(2,1)S(1)}, u32[]{:S(2)}, u32[]{:S(2)}) collective-permute-start(bf16[16,16,640]{2,1,0:T(8,128)(2,1)S(1)} %all_to_all.21), channel_id=1, source_target_pairs={{0,4},{1,5},{2,6},{3,7},{4,8},{5,9},{6,10},{7,11},{8,12},{9,13},{1... | collective-permute-start | bytes 983048 | tf_op jit(solution)/shard_map/ppermute | solution.py:32
  67.8 10.3 %collective-permute-start.2 = (bf16[16,16,640]{2,1,0:T(8,128)(2,1)S(1)}, bf16[16,16,640]{2,1,0:T(8,128)(2,1)S(1)}, u32[]{:S(2)}, u32[]{:S(2)}) collective-permute-start(bf16[16,16,640]{2,1,0:T(8,128)(2,1)S(1)} %all_to_all.21), channel_id=1, source_target_pairs={{0,8},{1,9},{2,10},{3,11},{4,12},{5,13},{6,14},{7,15},{8,0},{9,1},... | collective-permute-start | bytes 983048 | tf_op jit(solution)/shard_map/ppermute | solution.py:32
  72.1 8.7 %collective-permute-start.1 = (bf16[16,16,640]{2,1,0:T(8,128)(2,1)S(1)}, bf16[16,16,640]{2,1,0:T(8,128)(2,1)S(1)}, u32[]{:S(2)}, u32[]{:S(2)}) collective-permute-start(bf16[16,16,640]{2,1,0:T(8,128)(2,1)S(1)} %all_to_all.21), channel_id=1, source_target_pairs={{0,12},{1,13},{2,14},{3,15},{4,0},{5,1},{6,2},{7,3},{8,4},{9,5},{1... | collective-permute-start | bytes 983048 | tf_op jit(solution)/shard_map/ppermute | solution.py:32
  75.6 15.6 %collective-permute-start.3 = (bf16[2,16,16,640]{3,2,1,0:T(8,128)(2,1)S(1)}, bf16[2,16,16,640]{3,2,1,0:T(8,128)(2,1)S(1)}, u32[]{:S(2)}, u32[]{:S(2)}) collective-permute-start(bf16[2,16,16,640]{3,2,1,0:T(8,128)(2,1)S(1)} %pad_maximum_fusion.refs_0_), channel_id=1, source_target_pairs={{0,1},{1,2},{2,3},{3,0},{4,5},{5,6},{6,7},{7,4},{8,9},{9,10},{10,1... | collective-permute-start | bytes 1966088 | tf_op jit(solution)/shard_map/ppermute | solution.py:32
  80.9 13.1 %collective-permute-start.6 = (bf16[2,16,16,640]{3,2,1,0:T(8,128)(2,1)S(1)}, bf16[2,16,16,640]{3,2,1,0:T(8,128)(2,1)S(1)}, u32[]{:S(2)}, u32[]{:S(2)}) collective-permute-start(bf16[2,16,16,640]{3,2,1,0:T(8,128)(2,1)S(1)} %pad_maximum_fusion.1.refs_1_), channel_id=1, source_target_pairs={{0,3},{1,0},{2,1},{3,2},{4,7},{5,4},{6,5},{7,6},{8,11},{9,8},{10,9... | collective-permute-start | bytes 1966088 | tf_op jit(solution)/shard_map/ppermute | solution.py:32
  85.3 15.7 %collective-permute-start.5 = (bf16[2,16,16,640]{3,2,1,0:T(8,128)(2,1)S(1)}, bf16[2,16,16,640]{3,2,1,0:T(8,128)(2,1)S(1)}, u32[]{:S(2)}, u32[]{:S(2)}) collective-permute-start(bf16[2,16,16,640]{3,2,1,0:T(8,128)(2,1)S(1)} %pad_maximum_fusion.refs_0_), channel_id=1, source_target_pairs={{0,3},{1,0},{2,1},{3,2},{4,7},{5,4},{6,5},{7,6},{8,11},{9,8},{10,9... | collective-permute-start | bytes 1966088 | tf_op jit(solution)/shard_map/ppermute | solution.py:32
  88.2 12.9 %collective-permute-start.4 = (bf16[2,16,16,640]{3,2,1,0:T(8,128)(2,1)S(1)}, bf16[2,16,16,640]{3,2,1,0:T(8,128)(2,1)}, u32[]{:S(2)}, u32[]{:S(2)}) collective-permute-start(bf16[2,16,16,640]{3,2,1,0:T(8,128)(2,1)S(1)} %pad_maximum_fusion.1.refs_1_), channel_id=1, source_target_pairs={{0,1},{1,2},{2,3},{3,0},{4,5},{5,6},{6,7},{7,4},{8,9},{9,10},{10,1... | collective-permute-start | bytes 1966088 | tf_op jit(solution)/shard_map/ppermute | solution.py:32
  91.2 17.0 %collective-permute-start.7 = (bf16[2,16,16,640]{3,2,1,0:T(8,128)(2,1)S(1)}, bf16[2,16,16,640]{3,2,1,0:T(8,128)(2,1)}, u32[]{:S(2)}, u32[]{:S(2)}) collective-permute-start(bf16[2,16,16,640]{3,2,1,0:T(8,128)(2,1)S(1)} %collective-permute-done.3.refs_2_), channel_id=1, source_target_pairs={{0,1},{1,2},{2,3},{3,0},{4,5},{5,6},{6,7},{7,4},{8,9},{9,10},{10,1... | collective-permute-start | bytes 1966088 | tf_op jit(solution)/shard_map/ppermute | solution.py:32
  93.9 14.2 %collective-permute-start.8 = (bf16[2,16,16,640]{3,2,1,0:T(8,128)(2,1)S(1)}, bf16[2,16,16,640]{3,2,1,0:T(8,128)(2,1)}, u32[]{:S(2)}, u32[]{:S(2)}) collective-permute-start(bf16[2,16,16,640]{3,2,1,0:T(8,128)(2,1)S(1)} %collective-permute-done.6.refs_5_), channel_id=1, source_target_pairs={{0,3},{1,0},{2,1},{3,2},{4,7},{5,4},{6,5},{7,6},{8,11},{9,8},{10,9... | collective-permute-start | bytes 1966088 | tf_op jit(solution)/shard_map/ppermute | solution.py:32
Sparse Core Ops, SparseCore 0:
  10.1 101.3 all-gather.2

commit v5 on v4

--- a/solution.py
+++ b/solution.py
@@ -119,7 +119,7 @@
         lax.fori_loop(group * span, (group + 1) * span, one_chip, 0)
 
     size = reps * 8
-    deep = 5
+    deep = 25
     acc_ref[...] = jnp.zeros_like(acc_ref)
 
     def body(i, carry):
@@ -314,28 +314,6 @@
     )(*contexts, *cotangents)
 
 
-def join_kernel(got_ref, out_ref):
-    shards, tok, width = out_ref.shape
-    main = 2 * MAIN
-    sides = [
-        got_ref[c * shards : (c + 1) * shards].reshape(shards * tok, width // 2) for c in range(2)
-    ]
-    for c in range(2):
-        out_ref[:, :, c * main : (c + 1) * main] = sides[c][:, :main].reshape(shards, tok, main)
-    edges = jnp.concatenate([side[:, main:] for side in sides], axis=1)
-    out_ref[:, :, 2 * main :] = edges.reshape(shards, tok, width - 2 * main)
-
-
-def join_cores(got):
-    both, tok, cols = got.shape
-    return pl.pallas_call(
-        join_kernel,
-        in_specs=[pl.BlockSpec(memory_space=pltpu.VMEM)],
-        out_specs=pl.BlockSpec(memory_space=pltpu.VMEM),
-        out_shape=jax.ShapeDtypeStruct((both // 2, tok, 2 * cols), got.dtype),
-    )(got)
-
-
 def shards(context_one, cotangent_one, context_two, cotangent_two):
     tokens, feats = context_one.shape
     reps = lax.axis_size("replica")
@@ -350,7 +328,12 @@
         (context_one.T, context_two.T), (cotangent_one.T, cotangent_two.T), n_shards
     )
     ctx = lax.all_gather(ctx, "replica")
-    cot = join_cores(lax.all_to_all(cot, axes, 0, 0, axis_index_groups=planes))
+    got = lax.all_to_all(cot, axes, 0, 0, axis_index_groups=planes)
+    sides = (got[:n_shards], got[n_shards:])
+    main = 2 * MAIN
+    cot = jnp.concatenate(
+        [side[:, :, :main] for side in sides] + [side[:, :, main:] for side in sides], axis=2
+    )
     cot = lax.all_to_all(cot, "replica", 0, 0, axis_index_groups=same_core)
     pieces = gather_pieces(cot, reps)
 

time: 172 us -> 170 us (0.988)
  Pallas kernels: 21.2 us -> 18.4 us
  waiting for transfers between devices: 17.2 us -> 19.3 us
    all_gather x1, waiting for transfers between devices: 3.34 us -> 5.79 us  [shards(): ctx = lax.all_gather(ctx, 'replica')]
    pallas_call x1 -> x0, Pallas kernels: 1.83 us -> none  [join_cores(): pl.pallas_call(join_kernel, in_specs=[pl.BlockSpec(memory_space=pltpu.VME...]
  transfers between devices with their start and end apart: 10 -> 10, of which waited for: 8 -> 8; matrix products, arithmetic and copies ran while one was open for 1% -> 1% of each run, Pallas kernels for 1% -> 0%
where the time goes in v5:
time: 170 us; the launch traced here: 168 us
  blocking collectives  87.9 us (52%)
  starting transfers between devices  27.4 us (16%)
  waiting for transfers between devices  19.3 us (11%)
  Pallas kernels  18.4 us (11%)
  between operations  14.2 us (8%)
    all_to_all x1, blocking collectives, shards(): cot = lax.all_to_all(cot, 'replica', 0, 0, axis_index_groups=same_core)  34.3 us
    ppermute x9, starting transfers between devices, move(): lax.ppermute(value, ('replica', 'shard'), plane_moves(reps, stage, d))  27.3 us
    all_to_all x1, blocking collectives, shards(): got = lax.all_to_all(cot, axes, 0, 0, axis_index_groups=planes)  20.1 us
    all_to_all x1, blocking collectives, shards(): gram = lax.all_to_all(gram, 'replica', 0, 0, axis_index_groups=same_core)  18 us
    all_to_all x1, blocking collectives, shards(): lax.all_to_all(gram, axes, 0, 0, axis_index_groups=planes)  15.5 us
    ppermute x9, waiting for transfers between devices, move(): lax.ppermute(value, ('replica', 'shard'), plane_moves(reps, stage, d))  13.5 us
    pallas_call x1, Pallas kernels, gradients(): pl.pallas_call(gradient_kernel, in_specs=[pl.BlockSpec(memory_space=pltpu...  12.3 us
    all_gather x1, waiting for transfers between devices, shards(): ctx = lax.all_gather(ctx, 'replica')  5.79 us
  transfers between devices with their start and end apart: 10, of which 8 were waited for; matrix products, arithmetic and copies ran while one was open for 1% of the time, Pallas kernels for 0%

profile of v5, /device:TPU:1, one launch (start us, length us, event | category | flops | bytes accessed | tf_op | source)
XLA Modules:
  0.0 168.4 jit_solution(10201079728474196199)
XLA Ops:
  7.2 0.0 all-gather.3.cloned.1.call-start
  7.2 2.1 %shard_map.68 = (bf16[640,256]{1,0:T(8,128)(2,1)}, bf16[32,16,320]{2,1,0:T(8,128)(2,1)}) custom-call(bf16[320,256]{1,0:T(8,128)(2,1)} %bitcast.16, bf16[320,256]{1,0:T(8,128)(2,1)} %bitcast.17, bf16[320,256]{1,0:T(8,128)(2,1)} %bitcast.18, bf16[320,256]{1,0:T(8,128)(2,1)} %bitcast.19), custom_call_target="tpu_custom_call" | custom-call | tf_op jit(solution)/shard_map/pallas_call | solution.py:306
  9.3 0.0 all-gather.3.cloned.1.call-update
  9.4 20.1 %all_to_all.20 = bf16[32,16,320]{2,1,0:T(8,128)(2,1)S(1)} all-to-all(bf16[32,16,320]{2,1,0:T(8,128)(2,1)} %get-tuple-element.9), channel_id=1, replica_groups={{0,1,2,3,4,5,6,7,8,9,10,11,12,13,14,15,16,17,18,19,20,21,22,23,24,25,26..., dimensions={0} | all-to-all | bytes 655360 | tf_op jit(solution)/shard_map/all_to_all | solution.py:331
  29.6 0.1 pad_maximum_fusion.2
  29.7 34.3 %all_to_all.21 = bf16[16,16,640]{2,1,0:T(8,128)(2,1)S(1)} all-to-all(bf16[16,16,640]{2,1,0:T(8,128)(2,1)S(1)} %pad_maximum_fusion.2), channel_id=1, replica_groups={{0,32,64,96,128,160,192,224,256,288,320,352,384,416,448,480},{16,48,80,..., dimensions={0} | all-to-all | bytes 655360 | tf_op jit(solution)/shard_map/all_to_all | solution.py:337
  63.9 1.9 %collective-permute-start = (bf16[16,16,640]{2,1,0:T(8,128)(2,1)S(1)}, bf16[16,16,640]{2,1,0:T(8,128)(2,1)S(1)}, u32[]{:S(2)}, u32[]{:S(2)}) collective-permute-start(bf16[16,16,640]{2,1,0:T(8,128)(2,1)S(1)} %all_to_all.21), channel_id=1, source_target_pairs={{0,4},{1,5},{2,6},{3,7},{4,8},{5,9},{6,10},{7,11},{8,12},{9,13},{1... | collective-permute-start | bytes 983048 | tf_op jit(solution)/shard_map/ppermute | solution.py:32
  65.8 3.8 %collective-permute-start.2 = (bf16[16,16,640]{2,1,0:T(8,128)(2,1)S(1)}, bf16[16,16,640]{2,1,0:T(8,128)(2,1)S(1)}, u32[]{:S(2)}, u32[]{:S(2)}) collective-permute-start(bf16[16,16,640]{2,1,0:T(8,128)(2,1)S(1)} %all_to_all.21), channel_id=1, source_target_pairs={{0,8},{1,9},{2,10},{3,11},{4,12},{5,13},{6,14},{7,15},{8,0},{9,1},... | collective-permute-start | bytes 983048 | tf_op jit(solution)/shard_map/ppermute | solution.py:32
  69.6 3.6 %collective-permute-start.1 = (bf16[16,16,640]{2,1,0:T(8,128)(2,1)S(1)}, bf16[16,16,640]{2,1,0:T(8,128)(2,1)S(1)}, u32[]{:S(2)}, u32[]{:S(2)}) collective-permute-start(bf16[16,16,640]{2,1,0:T(8,128)(2,1)S(1)} %all_to_all.21), channel_id=1, source_target_pairs={{0,12},{1,13},{2,14},{3,15},{4,0},{5,1},{6,2},{7,3},{8,4},{9,5},{1... | collective-permute-start | bytes 983048 | tf_op jit(solution)/shard_map/ppermute | solution.py:32
  73.2 3.5 %collective-permute-done = bf16[16,16,640]{2,1,0:T(8,128)(2,1)S(1)} collective-permute-done((bf16[16,16,640]{2,1,0:T(8,128)(2,1)S(1)}, bf16[16,16,640]{2,1,0:T(8,128)(2,1)S(1)}, u32[]{:S(2)}, u32[]{:S(2)}) %collective-permute-start) | collective-permute-done | bytes 327712 | tf_op jit(solution)/shard_map/ppermute | solution.py:32
  76.7 0.1 pad_maximum_fusion.refs_0_
  76.8 2.4 %collective-permute-start.3 = (bf16[2,16,16,640]{3,2,1,0:T(8,128)(2,1)S(1)}, bf16[2,16,16,640]{3,2,1,0:T(8,128)(2,1)S(1)}, u32[]{:S(2)}, u32[]{:S(2)}) collective-permute-start(bf16[2,16,16,640]{3,2,1,0:T(8,128)(2,1)S(1)} %pad_maximum_fusion.refs_0_), channel_id=1, source_target_pairs={{0,1},{1,2},{2,3},{3,0},{4,5},{5,6},{6,7},{7,4},{8,9},{9,10},{10,1... | collective-permute-start | bytes 1966088 | tf_op jit(solution)/shard_map/ppermute | solution.py:32
  79.2 0.0 collective-permute-done.2
  79.2 0.1 collective-permute-done.1
  79.3 0.1 pad_maximum_fusion.1.refs_1_
  79.4 4.0 %collective-permute-start.6 = (bf16[2,16,16,640]{3,2,1,0:T(8,128)(2,1)S(1)}, bf16[2,16,16,640]{3,2,1,0:T(8,128)(2,1)S(1)}, u32[]{:S(2)}, u32[]{:S(2)}) collective-permute-start(bf16[2,16,16,640]{3,2,1,0:T(8,128)(2,1)S(1)} %pad_maximum_fusion.1.refs_1_), channel_id=1, source_target_pairs={{0,3},{1,0},{2,1},{3,2},{4,7},{5,4},{6,5},{7,6},{8,11},{9,8},{10,9... | collective-permute-start | bytes 1966088 | tf_op jit(solution)/shard_map/ppermute | solution.py:32
  83.4 1.9 %collective-permute-start.5 = (bf16[2,16,16,640]{3,2,1,0:T(8,128)(2,1)S(1)}, bf16[2,16,16,640]{3,2,1,0:T(8,128)(2,1)S(1)}, u32[]{:S(2)}, u32[]{:S(2)}) collective-permute-start(bf16[2,16,16,640]{3,2,1,0:T(8,128)(2,1)S(1)} %pad_maximum_fusion.refs_0_), channel_id=1, source_target_pairs={{0,3},{1,0},{2,1},{3,2},{4,7},{5,4},{6,5},{7,6},{8,11},{9,8},{10,9... | collective-permute-start | bytes 1966088 | tf_op jit(solution)/shard_map/ppermute | solution.py:32
  85.3 3.4 %collective-permute-start.4 = (bf16[2,16,16,640]{3,2,1,0:T(8,128)(2,1)S(1)}, bf16[2,16,16,640]{3,2,1,0:T(8,128)(2,1)}, u32[]{:S(2)}, u32[]{:S(2)}) collective-permute-start(bf16[2,16,16,640]{3,2,1,0:T(8,128)(2,1)S(1)} %pad_maximum_fusion.1.refs_1_), channel_id=1, source_target_pairs={{0,1},{1,2},{2,3},{3,0},{4,5},{5,6},{6,7},{7,4},{8,9},{9,10},{10,1... | collective-permute-start | bytes 1966088 | tf_op jit(solution)/shard_map/ppermute | solution.py:32
  88.7 1.0 collective-permute-done.3.refs_2_
  89.7 1.9 %collective-permute-start.7 = (bf16[2,16,16,640]{3,2,1,0:T(8,128)(2,1)S(1)}, bf16[2,16,16,640]{3,2,1,0:T(8,128)(2,1)}, u32[]{:S(2)}, u32[]{:S(2)}) collective-permute-start(bf16[2,16,16,640]{3,2,1,0:T(8,128)(2,1)S(1)} %collective-permute-done.3.refs_2_), channel_id=1, source_target_pairs={{0,1},{1,2},{2,3},{3,0},{4,5},{5,6},{6,7},{7,4},{8,9},{9,10},{10,1... | collective-permute-start | bytes 1966088 | tf_op jit(solution)/shard_map/ppermute | solution.py:32
  91.7 0.2 collective-permute-done.6.refs_5_
  91.8 4.4 %collective-permute-start.8 = (bf16[2,16,16,640]{3,2,1,0:T(8,128)(2,1)S(1)}, bf16[2,16,16,640]{3,2,1,0:T(8,128)(2,1)}, u32[]{:S(2)}, u32[]{:S(2)}) collective-permute-start(bf16[2,16,16,640]{3,2,1,0:T(8,128)(2,1)S(1)} %collective-permute-done.6.refs_5_), channel_id=1, source_target_pairs={{0,3},{1,0},{2,1},{3,2},{4,7},{5,4},{6,5},{7,6},{8,11},{9,8},{10,9... | collective-permute-start | bytes 1966088 | tf_op jit(solution)/shard_map/ppermute | solution.py:32
  96.3 0.7 fusion.1
  97.0 0.1 select_multiply_fusion
  97.0 0.1 mul.15.off_ref
  97.1 1.7 %collective-permute-done.5.refs_4_ = bf16[2,16,16,640]{3,2,1,0:T(8,128)(2,1)S(1)} collective-permute-done((bf16[2,16,16,640]{3,2,1,0:T(8,128)(2,1)S(1)}, bf16[2,16,16,640]{3,2,1,0:T(8,128)(2,1)S(1)}, u32[]{:S(2)}, u32[]{:S(2)}) %collective-permute-start.5) | collective-permute-done | bytes 655392 | tf_op jit(solution)/shard_map/ppermute | solution.py:32
  98.8 0.0 collective-permute-done.4.refs_3_
  98.8 6.5 %collective-permute-done.7.refs_6_ = bf16[2,16,16,640]{3,2,1,0:T(8,128)(2,1)} collective-permute-done((bf16[2,16,16,640]{3,2,1,0:T(8,128)(2,1)S(1)}, bf16[2,16,16,640]{3,2,1,0:T(8,128)(2,1)}, u32[]{:S(2)}, u32[]{:S(2)}) %collective-permute-start.7) | collective-permute-done | bytes 655392 | tf_op jit(solution)/shard_map/ppermute | solution.py:32
  105.3 0.6 collective-permute-done.8.refs_7_
  105.9 5.8 %all-gather.3.cloned.1.call-done = bf16[20480,256]{1,0:T(8,128)(2,1)} async-done(((bf16[640,256]{1,0:T(8,128)(2,1)}), bf16[20480,256]{1,0:T(8,128)(2,1)}) %all-gather.3.cloned.1.call-update) | async-done | bytes 10485776 | tf_op jit(solution)/shard_map/all_gather | solution.py:330
  111.7 12.3 %shard_map.69 = (bf16[2,32,400,128]{3,2,1,0:T(8,128)(2,1)}, f32[16,128]{1,0:T(8,128)S(1)}) custom-call(s32[16]{0:T(128)S(1)} %mul.15.off_ref, bf16[16,2,2,320,256]{4,3,2,1,0:T(8,128)(2,1)} %bitcast.11, bf16[2,16,16,640]{3,2,1,0:T(8,128)(2,1)S(1)} %pad_maximum_fusion.refs_0_, bf16[2,16,16,640]{3,2,1,0:T(8,128)(2,1)S(1)} %pad_maximum_fusion.1.refs_1_, ...), custom_call_target="tpu_custom_call" | custom-call | tf_op jit(solution)/shard_map/pallas_call | solution.py:173
  124.0 15.5 %all_to_all.22 = f32[32,16,128]{2,1,0:T(8,128)S(1)} all-to-all(f32[32,16,128]{2,1,0:T(8,128)S(1)} %broadcast_in_dim.4), channel_id=1, replica_groups={{0,1,2,3,4,5,6,7,8,9,10,11,12,13,14,15,16,17,18,19,20,21,22,23,24,25,26..., dimensions={0} | all-to-all | bytes 524288 | tf_op jit(solution)/shard_map/all_to_all | solution.py:343
  139.5 18.0 %all_to_all.23.gram_ref = f32[16,16,128]{2,1,0:T(8,128)S(1)} all-to-all(f32[16,16,128]{2,1,0:T(8,128)S(1)} %broadcast_in_dim.5), channel_id=1, replica_groups={{0,32,64,96,128,160,192,224,256,288,320,352,384,416,448,480},{16,48,80,..., dimensions={0} | all-to-all | bytes 262144 | tf_op jit(solution)/shard_map/all_to_all | solution.py:345
  157.5 4.0 %shard_map.70 = (f32[160,320]{1,0:T(8,128)}, f32[160,320]{1,0:T(8,128)}) custom-call(f32[16,16,128]{2,1,0:T(8,128)S(1)} %all_to_all.23.gram_ref, bf16[2,32,400,128]{3,2,1,0:T(8,128)(2,1)} %get-tuple-element.11.grad_hbm), custom_call_target="tpu_custom_call" | custom-call | tf_op jit(solution)/shard_map/pallas_call | solution.py:272
  (5 shorter events, 0.1 us)
Async XLA Ops:
  7.2 104.5 %all-gather.3.cloned.1.call-start = ((), (), s32[]{:S(2)}) async-start(), calls=%async_computation.4 | async-start | bytes 10813440 | tf_op jit(solution)/shard_map/all_gather | solution.py:330
  63.9 12.8 %collective-permute-start = (bf16[16,16,640]{2,1,0:T(8,128)(2,1)S(1)}, bf16[16,16,640]{2,1,0:T(8,128)(2,1)S(1)}, u32[]{:S(2)}, u32[]{:S(2)}) collective-permute-start(bf16[16,16,640]{2,1,0:T(8,128)(2,1)S(1)} %all_to_all.21), channel_id=1, source_target_pairs={{0,4},{1,5},{2,6},{3,7},{4,8},{5,9},{6,10},{7,11},{8,12},{9,13},{1... | collective-permute-start | bytes 983048 | tf_op jit(solution)/shard_map/ppermute | solution.py:32
  65.8 13.4 %collective-permute-start.2 = (bf16[16,16,640]{2,1,0:T(8,128)(2,1)S(1)}, bf16[16,16,640]{2,1,0:T(8,128)(2,1)S(1)}, u32[]{:S(2)}, u32[]{:S(2)}) collective-permute-start(bf16[16,16,640]{2,1,0:T(8,128)(2,1)S(1)} %all_to_all.21), channel_id=1, source_target_pairs={{0,8},{1,9},{2,10},{3,11},{4,12},{5,13},{6,14},{7,15},{8,0},{9,1},... | collective-permute-start | bytes 983048 | tf_op jit(solution)/shard_map/ppermute | solution.py:32
  69.6 9.7 %collective-permute-start.1 = (bf16[16,16,640]{2,1,0:T(8,128)(2,1)S(1)}, bf16[16,16,640]{2,1,0:T(8,128)(2,1)S(1)}, u32[]{:S(2)}, u32[]{:S(2)}) collective-permute-start(bf16[16,16,640]{2,1,0:T(8,128)(2,1)S(1)} %all_to_all.21), channel_id=1, source_target_pairs={{0,12},{1,13},{2,14},{3,15},{4,0},{5,1},{6,2},{7,3},{8,4},{9,5},{1... | collective-permute-start | bytes 983048 | tf_op jit(solution)/shard_map/ppermute | solution.py:32
  76.8 12.9 %collective-permute-start.3 = (bf16[2,16,16,640]{3,2,1,0:T(8,128)(2,1)S(1)}, bf16[2,16,16,640]{3,2,1,0:T(8,128)(2,1)S(1)}, u32[]{:S(2)}, u32[]{:S(2)}) collective-permute-start(bf16[2,16,16,640]{3,2,1,0:T(8,128)(2,1)S(1)} %pad_maximum_fusion.refs_0_), channel_id=1, source_target_pairs={{0,1},{1,2},{2,3},{3,0},{4,5},{5,6},{6,7},{7,4},{8,9},{9,10},{10,1... | collective-permute-start | bytes 1966088 | tf_op jit(solution)/shard_map/ppermute | solution.py:32
  79.4 12.4 %collective-permute-start.6 = (bf16[2,16,16,640]{3,2,1,0:T(8,128)(2,1)S(1)}, bf16[2,16,16,640]{3,2,1,0:T(8,128)(2,1)S(1)}, u32[]{:S(2)}, u32[]{:S(2)}) collective-permute-start(bf16[2,16,16,640]{3,2,1,0:T(8,128)(2,1)S(1)} %pad_maximum_fusion.1.refs_1_), channel_id=1, source_target_pairs={{0,3},{1,0},{2,1},{3,2},{4,7},{5,4},{6,5},{7,6},{8,11},{9,8},{10,9... | collective-permute-start | bytes 1966088 | tf_op jit(solution)/shard_map/ppermute | solution.py:32
  83.4 15.4 %collective-permute-start.5 = (bf16[2,16,16,640]{3,2,1,0:T(8,128)(2,1)S(1)}, bf16[2,16,16,640]{3,2,1,0:T(8,128)(2,1)S(1)}, u32[]{:S(2)}, u32[]{:S(2)}) collective-permute-start(bf16[2,16,16,640]{3,2,1,0:T(8,128)(2,1)S(1)} %pad_maximum_fusion.refs_0_), channel_id=1, source_target_pairs={{0,3},{1,0},{2,1},{3,2},{4,7},{5,4},{6,5},{7,6},{8,11},{9,8},{10,9... | collective-permute-start | bytes 1966088 | tf_op jit(solution)/shard_map/ppermute | solution.py:32
  85.3 13.5 %collective-permute-start.4 = (bf16[2,16,16,640]{3,2,1,0:T(8,128)(2,1)S(1)}, bf16[2,16,16,640]{3,2,1,0:T(8,128)(2,1)}, u32[]{:S(2)}, u32[]{:S(2)}) collective-permute-start(bf16[2,16,16,640]{3,2,1,0:T(8,128)(2,1)S(1)} %pad_maximum_fusion.1.refs_1_), channel_id=1, source_target_pairs={{0,1},{1,2},{2,3},{3,0},{4,5},{5,6},{6,7},{7,4},{8,9},{9,10},{10,1... | collective-permute-start | bytes 1966088 | tf_op jit(solution)/shard_map/ppermute | solution.py:32
  89.7 15.6 %collective-permute-start.7 = (bf16[2,16,16,640]{3,2,1,0:T(8,128)(2,1)S(1)}, bf16[2,16,16,640]{3,2,1,0:T(8,128)(2,1)}, u32[]{:S(2)}, u32[]{:S(2)}) collective-permute-start(bf16[2,16,16,640]{3,2,1,0:T(8,128)(2,1)S(1)} %collective-permute-done.3.refs_2_), channel_id=1, source_target_pairs={{0,1},{1,2},{2,3},{3,0},{4,5},{5,6},{6,7},{7,4},{8,9},{9,10},{10,1... | collective-permute-start | bytes 1966088 | tf_op jit(solution)/shard_map/ppermute | solution.py:32
  91.8 14.0 %collective-permute-start.8 = (bf16[2,16,16,640]{3,2,1,0:T(8,128)(2,1)S(1)}, bf16[2,16,16,640]{3,2,1,0:T(8,128)(2,1)}, u32[]{:S(2)}, u32[]{:S(2)}) collective-permute-start(bf16[2,16,16,640]{3,2,1,0:T(8,128)(2,1)S(1)} %collective-permute-done.6.refs_5_), channel_id=1, source_target_pairs={{0,3},{1,0},{2,1},{3,2},{4,7},{5,4},{6,5},{7,6},{8,11},{9,8},{10,9... | collective-permute-start | bytes 1966088 | tf_op jit(solution)/shard_map/ppermute | solution.py:32
Sparse Core Ops, SparseCore 0:
  10.1 101.4 all-gather.2

commit v6 on v5

--- a/solution.py
+++ b/solution.py
@@ -192,10 +192,10 @@
 
 
 def tree_weights(gram):
-    n = gram.shape[0]
-    ri = lax.broadcasted_iota(jnp.int32, (n, n), 0)
-    ci = lax.broadcasted_iota(jnp.int32, (n, n), 1)
-    weight = jnp.ones((n, 1), jnp.float32)
+    n = gram.shape[1]
+    ri = lax.broadcasted_iota(jnp.int32, gram.shape, 1)
+    ci = lax.broadcasted_iota(jnp.int32, gram.shape, 2)
+    weight = jnp.ones((gram.shape[0], n, 1), jnp.float32)
     for k in range(n.bit_length() - 1):
         same = (ri >> k) == (ci >> k)
         other = (ri >> k) == ((ci >> k) ^ 1)
@@ -203,15 +203,15 @@
         own = jnp.where(same, gram, 0.0)
         cross = jnp.where(other, gram, 0.0)
         coeffs = []
-        for axis in (1, 0):
-            norm = jnp.sum(own, axis=1 - axis, keepdims=True)
+        for axis in (2, 1):
+            norm = jnp.sum(own, axis=3 - axis, keepdims=True)
             norm = jnp.sum(jnp.where(same, norm, 0.0), axis=axis, keepdims=True)
-            inner = jnp.sum(cross, axis=1 - axis, keepdims=True)
+            inner = jnp.sum(cross, axis=3 - axis, keepdims=True)
             inner = jnp.sum(jnp.where(same, inner, 0.0), axis=axis, keepdims=True)
             coeffs.append((jnp.maximum(norm, 0.0), inner))
         (norm_r, inner_r), (norm_c, inner_c) = coeffs
-        twin_r = jnp.sum(jnp.where(twin, norm_c, 0.0), axis=1, keepdims=True)
-        twin_c = jnp.sum(jnp.where(twin, norm_r, 0.0), axis=0, keepdims=True)
+        twin_r = jnp.sum(jnp.where(twin, norm_c, 0.0), axis=2, keepdims=True)
+        twin_c = jnp.sum(jnp.where(twin, norm_r, 0.0), axis=1, keepdims=True)
         cap_r = jnp.sqrt(norm_r) * jnp.sqrt(twin_r)
         cap_c = jnp.sqrt(norm_c) * jnp.sqrt(twin_c)
         inner_r = jnp.clip(inner_r, -cap_r, cap_r)
@@ -241,10 +241,10 @@
         for k in range(len(starts)):
             grad_copy(layer, k).start()
     total = jnp.sum(gram_ref[...], axis=0) * (scale * scale)
+    parts = [total[:, k * 32 : (k + 1) * 32] for k in range(4)]
+    weights = tree_weights(jnp.concatenate(parts, axis=0).reshape(2, reps, reps))
     for layer in range(2):
-        parts = [total[:, (2 * layer + h) * 32 : (2 * layer + h + 1) * 32] for h in range(2)]
-        weights = tree_weights(jnp.concatenate(parts, axis=0))
-        weight_ref[layer] = jnp.broadcast_to(weights * scale, (reps, MAIN))
+        weight_ref[layer] = jnp.broadcast_to(weights[layer] * scale, (reps, MAIN))
     outs = []
     for layer, (out_ref, out_hbm) in enumerate(((one_ref, one_hbm), (two_ref, two_hbm))):
         sums = []

time: 170 us -> 171 us (level)
  no operation moved by 1% of the time
where the time goes in v6:
time: 171 us; the launch traced here: 168 us
  blocking collectives  87.9 us (51%)
  starting transfers between devices  27.4 us (16%)
  waiting for transfers between devices  19.3 us (11%)
  Pallas kernels  18.4 us (11%)
  between operations  14.2 us (8%)
    all_to_all x1, blocking collectives, shards(): cot = lax.all_to_all(cot, 'replica', 0, 0, axis_index_groups=same_core)  34.3 us
    ppermute x9, starting transfers between devices, move(): lax.ppermute(value, ('replica', 'shard'), plane_moves(reps, stage, d))  27.3 us
    all_to_all x1, blocking collectives, shards(): got = lax.all_to_all(cot, axes, 0, 0, axis_index_groups=planes)  20.1 us
    all_to_all x1, blocking collectives, shards(): gram = lax.all_to_all(gram, 'replica', 0, 0, axis_index_groups=same_core)  18 us
    all_to_all x1, blocking collectives, shards(): lax.all_to_all(gram, axes, 0, 0, axis_index_groups=planes)  15.5 us
    ppermute x9, waiting for transfers between devices, move(): lax.ppermute(value, ('replica', 'shard'), plane_moves(reps, stage, d))  13.5 us
    pallas_call x1, Pallas kernels, gradients(): pl.pallas_call(gradient_kernel, in_specs=[pl.BlockSpec(memory_space=pltpu...  12.3 us
    all_gather x1, waiting for transfers between devices, shards(): ctx = lax.all_gather(ctx, 'replica')  5.79 us
  transfers between devices with their start and end apart: 10, of which 8 were waited for; matrix products, arithmetic and copies ran while one was open for 1% of the time, Pallas kernels for 0%

profile of v6, /device:TPU:1, one launch (start us, length us, event | category | flops | bytes accessed | tf_op | source)
XLA Modules:
  0.0 168.4 jit_solution(10442784828045819957)
XLA Ops:
  7.2 0.0 all-gather.3.cloned.1.call-start
  7.2 2.1 %shard_map.68 = (bf16[640,256]{1,0:T(8,128)(2,1)}, bf16[32,16,320]{2,1,0:T(8,128)(2,1)}) custom-call(bf16[320,256]{1,0:T(8,128)(2,1)} %bitcast.16, bf16[320,256]{1,0:T(8,128)(2,1)} %bitcast.17, bf16[320,256]{1,0:T(8,128)(2,1)} %bitcast.18, bf16[320,256]{1,0:T(8,128)(2,1)} %bitcast.19), custom_call_target="tpu_custom_call" | custom-call | tf_op jit(solution)/shard_map/pallas_call | solution.py:306
  9.3 0.0 all-gather.3.cloned.1.call-update
  9.4 20.1 %all_to_all.20 = bf16[32,16,320]{2,1,0:T(8,128)(2,1)S(1)} all-to-all(bf16[32,16,320]{2,1,0:T(8,128)(2,1)} %get-tuple-element.9), channel_id=1, replica_groups={{0,1,2,3,4,5,6,7,8,9,10,11,12,13,14,15,16,17,18,19,20,21,22,23,24,25,26..., dimensions={0} | all-to-all | bytes 655360 | tf_op jit(solution)/shard_map/all_to_all | solution.py:331
  29.6 0.1 pad_maximum_fusion.2
  29.7 34.3 %all_to_all.21 = bf16[16,16,640]{2,1,0:T(8,128)(2,1)S(1)} all-to-all(bf16[16,16,640]{2,1,0:T(8,128)(2,1)S(1)} %pad_maximum_fusion.2), channel_id=1, replica_groups={{0,32,64,96,128,160,192,224,256,288,320,352,384,416,448,480},{16,48,80,..., dimensions={0} | all-to-all | bytes 655360 | tf_op jit(solution)/shard_map/all_to_all | solution.py:337
  63.9 1.9 %collective-permute-start = (bf16[16,16,640]{2,1,0:T(8,128)(2,1)S(1)}, bf16[16,16,640]{2,1,0:T(8,128)(2,1)S(1)}, u32[]{:S(2)}, u32[]{:S(2)}) collective-permute-start(bf16[16,16,640]{2,1,0:T(8,128)(2,1)S(1)} %all_to_all.21), channel_id=1, source_target_pairs={{0,4},{1,5},{2,6},{3,7},{4,8},{5,9},{6,10},{7,11},{8,12},{9,13},{1... | collective-permute-start | bytes 983048 | tf_op jit(solution)/shard_map/ppermute | solution.py:32
  65.8 3.8 %collective-permute-start.2 = (bf16[16,16,640]{2,1,0:T(8,128)(2,1)S(1)}, bf16[16,16,640]{2,1,0:T(8,128)(2,1)S(1)}, u32[]{:S(2)}, u32[]{:S(2)}) collective-permute-start(bf16[16,16,640]{2,1,0:T(8,128)(2,1)S(1)} %all_to_all.21), channel_id=1, source_target_pairs={{0,8},{1,9},{2,10},{3,11},{4,12},{5,13},{6,14},{7,15},{8,0},{9,1},... | collective-permute-start | bytes 983048 | tf_op jit(solution)/shard_map/ppermute | solution.py:32
  69.6 3.6 %collective-permute-start.1 = (bf16[16,16,640]{2,1,0:T(8,128)(2,1)S(1)}, bf16[16,16,640]{2,1,0:T(8,128)(2,1)S(1)}, u32[]{:S(2)}, u32[]{:S(2)}) collective-permute-start(bf16[16,16,640]{2,1,0:T(8,128)(2,1)S(1)} %all_to_all.21), channel_id=1, source_target_pairs={{0,12},{1,13},{2,14},{3,15},{4,0},{5,1},{6,2},{7,3},{8,4},{9,5},{1... | collective-permute-start | bytes 983048 | tf_op jit(solution)/shard_map/ppermute | solution.py:32
  73.2 3.5 %collective-permute-done = bf16[16,16,640]{2,1,0:T(8,128)(2,1)S(1)} collective-permute-done((bf16[16,16,640]{2,1,0:T(8,128)(2,1)S(1)}, bf16[16,16,640]{2,1,0:T(8,128)(2,1)S(1)}, u32[]{:S(2)}, u32[]{:S(2)}) %collective-permute-start) | collective-permute-done | bytes 327712 | tf_op jit(solution)/shard_map/ppermute | solution.py:32
  76.7 0.1 pad_maximum_fusion.refs_0_
  76.8 2.4 %collective-permute-start.3 = (bf16[2,16,16,640]{3,2,1,0:T(8,128)(2,1)S(1)}, bf16[2,16,16,640]{3,2,1,0:T(8,128)(2,1)S(1)}, u32[]{:S(2)}, u32[]{:S(2)}) collective-permute-start(bf16[2,16,16,640]{3,2,1,0:T(8,128)(2,1)S(1)} %pad_maximum_fusion.refs_0_), channel_id=1, source_target_pairs={{0,1},{1,2},{2,3},{3,0},{4,5},{5,6},{6,7},{7,4},{8,9},{9,10},{10,1... | collective-permute-start | bytes 1966088 | tf_op jit(solution)/shard_map/ppermute | solution.py:32
  79.2 0.0 collective-permute-done.2
  79.2 0.1 collective-permute-done.1
  79.3 0.1 pad_maximum_fusion.1.refs_1_
  79.4 4.0 %collective-permute-start.6 = (bf16[2,16,16,640]{3,2,1,0:T(8,128)(2,1)S(1)}, bf16[2,16,16,640]{3,2,1,0:T(8,128)(2,1)S(1)}, u32[]{:S(2)}, u32[]{:S(2)}) collective-permute-start(bf16[2,16,16,640]{3,2,1,0:T(8,128)(2,1)S(1)} %pad_maximum_fusion.1.refs_1_), channel_id=1, source_target_pairs={{0,3},{1,0},{2,1},{3,2},{4,7},{5,4},{6,5},{7,6},{8,11},{9,8},{10,9... | collective-permute-start | bytes 1966088 | tf_op jit(solution)/shard_map/ppermute | solution.py:32
  83.4 1.9 %collective-permute-start.5 = (bf16[2,16,16,640]{3,2,1,0:T(8,128)(2,1)S(1)}, bf16[2,16,16,640]{3,2,1,0:T(8,128)(2,1)S(1)}, u32[]{:S(2)}, u32[]{:S(2)}) collective-permute-start(bf16[2,16,16,640]{3,2,1,0:T(8,128)(2,1)S(1)} %pad_maximum_fusion.refs_0_), channel_id=1, source_target_pairs={{0,3},{1,0},{2,1},{3,2},{4,7},{5,4},{6,5},{7,6},{8,11},{9,8},{10,9... | collective-permute-start | bytes 1966088 | tf_op jit(solution)/shard_map/ppermute | solution.py:32
  85.3 3.4 %collective-permute-start.4 = (bf16[2,16,16,640]{3,2,1,0:T(8,128)(2,1)S(1)}, bf16[2,16,16,640]{3,2,1,0:T(8,128)(2,1)}, u32[]{:S(2)}, u32[]{:S(2)}) collective-permute-start(bf16[2,16,16,640]{3,2,1,0:T(8,128)(2,1)S(1)} %pad_maximum_fusion.1.refs_1_), channel_id=1, source_target_pairs={{0,1},{1,2},{2,3},{3,0},{4,5},{5,6},{6,7},{7,4},{8,9},{9,10},{10,1... | collective-permute-start | bytes 1966088 | tf_op jit(solution)/shard_map/ppermute | solution.py:32
  88.7 1.0 collective-permute-done.3.refs_2_
  89.7 1.9 %collective-permute-start.7 = (bf16[2,16,16,640]{3,2,1,0:T(8,128)(2,1)S(1)}, bf16[2,16,16,640]{3,2,1,0:T(8,128)(2,1)}, u32[]{:S(2)}, u32[]{:S(2)}) collective-permute-start(bf16[2,16,16,640]{3,2,1,0:T(8,128)(2,1)S(1)} %collective-permute-done.3.refs_2_), channel_id=1, source_target_pairs={{0,1},{1,2},{2,3},{3,0},{4,5},{5,6},{6,7},{7,4},{8,9},{9,10},{10,1... | collective-permute-start | bytes 1966088 | tf_op jit(solution)/shard_map/ppermute | solution.py:32
  91.7 0.2 collective-permute-done.6.refs_5_
  91.8 4.4 %collective-permute-start.8 = (bf16[2,16,16,640]{3,2,1,0:T(8,128)(2,1)S(1)}, bf16[2,16,16,640]{3,2,1,0:T(8,128)(2,1)}, u32[]{:S(2)}, u32[]{:S(2)}) collective-permute-start(bf16[2,16,16,640]{3,2,1,0:T(8,128)(2,1)S(1)} %collective-permute-done.6.refs_5_), channel_id=1, source_target_pairs={{0,3},{1,0},{2,1},{3,2},{4,7},{5,4},{6,5},{7,6},{8,11},{9,8},{10,9... | collective-permute-start | bytes 1966088 | tf_op jit(solution)/shard_map/ppermute | solution.py:32
  96.3 0.7 fusion.1
  97.0 0.1 select_multiply_fusion
  97.0 0.1 mul.15.off_ref
  97.1 1.7 %collective-permute-done.5.refs_4_ = bf16[2,16,16,640]{3,2,1,0:T(8,128)(2,1)S(1)} collective-permute-done((bf16[2,16,16,640]{3,2,1,0:T(8,128)(2,1)S(1)}, bf16[2,16,16,640]{3,2,1,0:T(8,128)(2,1)S(1)}, u32[]{:S(2)}, u32[]{:S(2)}) %collective-permute-start.5) | collective-permute-done | bytes 655392 | tf_op jit(solution)/shard_map/ppermute | solution.py:32
  98.8 0.0 collective-permute-done.4.refs_3_
  98.8 6.5 %collective-permute-done.7.refs_6_ = bf16[2,16,16,640]{3,2,1,0:T(8,128)(2,1)} collective-permute-done((bf16[2,16,16,640]{3,2,1,0:T(8,128)(2,1)S(1)}, bf16[2,16,16,640]{3,2,1,0:T(8,128)(2,1)}, u32[]{:S(2)}, u32[]{:S(2)}) %collective-permute-start.7) | collective-permute-done | bytes 655392 | tf_op jit(solution)/shard_map/ppermute | solution.py:32
  105.3 0.6 collective-permute-done.8.refs_7_
  105.9 5.8 %all-gather.3.cloned.1.call-done = bf16[20480,256]{1,0:T(8,128)(2,1)} async-done(((bf16[640,256]{1,0:T(8,128)(2,1)}), bf16[20480,256]{1,0:T(8,128)(2,1)}) %all-gather.3.cloned.1.call-update) | async-done | bytes 10485776 | tf_op jit(solution)/shard_map/all_gather | solution.py:330
  111.7 12.3 %shard_map.69 = (bf16[2,32,400,128]{3,2,1,0:T(8,128)(2,1)}, f32[16,128]{1,0:T(8,128)S(1)}) custom-call(s32[16]{0:T(128)S(1)} %mul.15.off_ref, bf16[16,2,2,320,256]{4,3,2,1,0:T(8,128)(2,1)} %bitcast.11, bf16[2,16,16,640]{3,2,1,0:T(8,128)(2,1)S(1)} %pad_maximum_fusion.refs_0_, bf16[2,16,16,640]{3,2,1,0:T(8,128)(2,1)S(1)} %pad_maximum_fusion.1.refs_1_, ...), custom_call_target="tpu_custom_call" | custom-call | tf_op jit(solution)/shard_map/pallas_call | solution.py:173
  124.0 15.5 %all_to_all.22 = f32[32,16,128]{2,1,0:T(8,128)S(1)} all-to-all(f32[32,16,128]{2,1,0:T(8,128)S(1)} %broadcast_in_dim.4), channel_id=1, replica_groups={{0,1,2,3,4,5,6,7,8,9,10,11,12,13,14,15,16,17,18,19,20,21,22,23,24,25,26..., dimensions={0} | all-to-all | bytes 524288 | tf_op jit(solution)/shard_map/all_to_all | solution.py:343
  139.5 18.0 %all_to_all.23.gram_ref = f32[16,16,128]{2,1,0:T(8,128)S(1)} all-to-all(f32[16,16,128]{2,1,0:T(8,128)S(1)} %broadcast_in_dim.5), channel_id=1, replica_groups={{0,32,64,96,128,160,192,224,256,288,320,352,384,416,448,480},{16,48,80,..., dimensions={0} | all-to-all | bytes 262144 | tf_op jit(solution)/shard_map/all_to_all | solution.py:345
  157.5 4.0 %shard_map.70 = (f32[160,320]{1,0:T(8,128)}, f32[160,320]{1,0:T(8,128)}) custom-call(f32[16,16,128]{2,1,0:T(8,128)S(1)} %all_to_all.23.gram_ref, bf16[2,32,400,128]{3,2,1,0:T(8,128)(2,1)} %get-tuple-element.11.grad_hbm), custom_call_target="tpu_custom_call" | custom-call | tf_op jit(solution)/shard_map/pallas_call | solution.py:272
  (5 shorter events, 0.1 us)
Async XLA Ops:
  7.2 104.5 %all-gather.3.cloned.1.call-start = ((), (), s32[]{:S(2)}) async-start(), calls=%async_computation.4 | async-start | bytes 10813440 | tf_op jit(solution)/shard_map/all_gather | solution.py:330
  63.9 12.8 %collective-permute-start = (bf16[16,16,640]{2,1,0:T(8,128)(2,1)S(1)}, bf16[16,16,640]{2,1,0:T(8,128)(2,1)S(1)}, u32[]{:S(2)}, u32[]{:S(2)}) collective-permute-start(bf16[16,16,640]{2,1,0:T(8,128)(2,1)S(1)} %all_to_all.21), channel_id=1, source_target_pairs={{0,4},{1,5},{2,6},{3,7},{4,8},{5,9},{6,10},{7,11},{8,12},{9,13},{1... | collective-permute-start | bytes 983048 | tf_op jit(solution)/shard_map/ppermute | solution.py:32
  65.8 13.4 %collective-permute-start.2 = (bf16[16,16,640]{2,1,0:T(8,128)(2,1)S(1)}, bf16[16,16,640]{2,1,0:T(8,128)(2,1)S(1)}, u32[]{:S(2)}, u32[]{:S(2)}) collective-permute-start(bf16[16,16,640]{2,1,0:T(8,128)(2,1)S(1)} %all_to_all.21), channel_id=1, source_target_pairs={{0,8},{1,9},{2,10},{3,11},{4,12},{5,13},{6,14},{7,15},{8,0},{9,1},... | collective-permute-start | bytes 983048 | tf_op jit(solution)/shard_map/ppermute | solution.py:32
  69.6 9.7 %collective-permute-start.1 = (bf16[16,16,640]{2,1,0:T(8,128)(2,1)S(1)}, bf16[16,16,640]{2,1,0:T(8,128)(2,1)S(1)}, u32[]{:S(2)}, u32[]{:S(2)}) collective-permute-start(bf16[16,16,640]{2,1,0:T(8,128)(2,1)S(1)} %all_to_all.21), channel_id=1, source_target_pairs={{0,12},{1,13},{2,14},{3,15},{4,0},{5,1},{6,2},{7,3},{8,4},{9,5},{1... | collective-permute-start | bytes 983048 | tf_op jit(solution)/shard_map/ppermute | solution.py:32
  76.8 12.9 %collective-permute-start.3 = (bf16[2,16,16,640]{3,2,1,0:T(8,128)(2,1)S(1)}, bf16[2,16,16,640]{3,2,1,0:T(8,128)(2,1)S(1)}, u32[]{:S(2)}, u32[]{:S(2)}) collective-permute-start(bf16[2,16,16,640]{3,2,1,0:T(8,128)(2,1)S(1)} %pad_maximum_fusion.refs_0_), channel_id=1, source_target_pairs={{0,1},{1,2},{2,3},{3,0},{4,5},{5,6},{6,7},{7,4},{8,9},{9,10},{10,1... | collective-permute-start | bytes 1966088 | tf_op jit(solution)/shard_map/ppermute | solution.py:32
  79.4 12.4 %collective-permute-start.6 = (bf16[2,16,16,640]{3,2,1,0:T(8,128)(2,1)S(1)}, bf16[2,16,16,640]{3,2,1,0:T(8,128)(2,1)S(1)}, u32[]{:S(2)}, u32[]{:S(2)}) collective-permute-start(bf16[2,16,16,640]{3,2,1,0:T(8,128)(2,1)S(1)} %pad_maximum_fusion.1.refs_1_), channel_id=1, source_target_pairs={{0,3},{1,0},{2,1},{3,2},{4,7},{5,4},{6,5},{7,6},{8,11},{9,8},{10,9... | collective-permute-start | bytes 1966088 | tf_op jit(solution)/shard_map/ppermute | solution.py:32
  83.4 15.4 %collective-permute-start.5 = (bf16[2,16,16,640]{3,2,1,0:T(8,128)(2,1)S(1)}, bf16[2,16,16,640]{3,2,1,0:T(8,128)(2,1)S(1)}, u32[]{:S(2)}, u32[]{:S(2)}) collective-permute-start(bf16[2,16,16,640]{3,2,1,0:T(8,128)(2,1)S(1)} %pad_maximum_fusion.refs_0_), channel_id=1, source_target_pairs={{0,3},{1,0},{2,1},{3,2},{4,7},{5,4},{6,5},{7,6},{8,11},{9,8},{10,9... | collective-permute-start | bytes 1966088 | tf_op jit(solution)/shard_map/ppermute | solution.py:32
  85.3 13.5 %collective-permute-start.4 = (bf16[2,16,16,640]{3,2,1,0:T(8,128)(2,1)S(1)}, bf16[2,16,16,640]{3,2,1,0:T(8,128)(2,1)}, u32[]{:S(2)}, u32[]{:S(2)}) collective-permute-start(bf16[2,16,16,640]{3,2,1,0:T(8,128)(2,1)S(1)} %pad_maximum_fusion.1.refs_1_), channel_id=1, source_target_pairs={{0,1},{1,2},{2,3},{3,0},{4,5},{5,6},{6,7},{7,4},{8,9},{9,10},{10,1... | collective-permute-start | bytes 1966088 | tf_op jit(solution)/shard_map/ppermute | solution.py:32
  89.7 15.6 %collective-permute-start.7 = (bf16[2,16,16,640]{3,2,1,0:T(8,128)(2,1)S(1)}, bf16[2,16,16,640]{3,2,1,0:T(8,128)(2,1)}, u32[]{:S(2)}, u32[]{:S(2)}) collective-permute-start(bf16[2,16,16,640]{3,2,1,0:T(8,128)(2,1)S(1)} %collective-permute-done.3.refs_2_), channel_id=1, source_target_pairs={{0,1},{1,2},{2,3},{3,0},{4,5},{5,6},{6,7},{7,4},{8,9},{9,10},{10,1... | collective-permute-start | bytes 1966088 | tf_op jit(solution)/shard_map/ppermute | solution.py:32
  91.8 14.0 %collective-permute-start.8 = (bf16[2,16,16,640]{3,2,1,0:T(8,128)(2,1)S(1)}, bf16[2,16,16,640]{3,2,1,0:T(8,128)(2,1)}, u32[]{:S(2)}, u32[]{:S(2)}) collective-permute-start(bf16[2,16,16,640]{3,2,1,0:T(8,128)(2,1)S(1)} %collective-permute-done.6.refs_5_), channel_id=1, source_target_pairs={{0,3},{1,0},{2,1},{3,2},{4,7},{5,4},{6,5},{7,6},{8,11},{9,8},{10,9... | collective-permute-start | bytes 1966088 | tf_op jit(solution)/shard_map/ppermute | solution.py:32
Sparse Core Ops, SparseCore 0:
  10.1 101.4 all-gather.2
